TPU v7x, 256 devices: a whole 4x4x8 slice. The times are simulated.
256 devices in a mesh: row: 32 (over x_hi, z, core), col: 8 (over x_lo, y).
Axes of the slice: x: 4 (x_hi: 2, x_lo: 2; x = x_hi * 2 + x_lo), y: 4, z: 8, core: 2. Of those that a mesh axis runs over, the one named last changes fastest.
Arguments:
- regions: bfloat16 [16384, 256], P(('row', 'col')), may hold values from -1.25 to 1.25
- phrases: bfloat16 [16384, 256], P(('row', 'col')), may hold values from -1.25 to 1.25
Outputs:
- grad_regions: float32 [16384, 256], P(('row', 'col'))
- grad_phrases: float32 [16384, 256], P(('row', 'col'))
- divergence: float32 [], replicated
All inputs are finite; a program needn't handle non-finite values.
Results may differ from a plain program's by a relative error of at most 0.0035.
Values may be sent and summed in bfloat16 or wider, within the bound.
No kernel may reach another device: no remote copies, remote signals or barrier semaphores. Data moves between devices by JAX's collectives and lax.ppermute only.
A program may use at most 64 MiB of HBM per device.

v0:
```python
import math

import jax
import jax.numpy as jnp
from jax import lax
from jax.sharding import PartitionSpec as P

ITERS = 2


epsilon = 0.1


def half_square(points):
    values = points.astype(jnp.float32)
    return 0.5 * jnp.sum(values * values, axis=1)


def pair_dot(left_rows, right_rows):
    return lax.dot_general(
        left_rows, right_rows, (((1,), (1,)), ((), ())), preferred_element_type=jnp.float32
    )


def column_blocks(columns):
    step_cols = min(128, columns.shape[0])
    return (step_cols, columns.shape[0] // step_cols)


def row_partial(rows_emb, columns, col_shift):
    step_cols, blocks = column_blocks(columns)
    start_peak = jnp.full((rows_emb.shape[0],), -jnp.inf, jnp.float32)
    start_mass = jnp.zeros((rows_emb.shape[0],), jnp.float32)

    def advance(running, block_index):
        peak_now, mass_now = running
        offset = block_index * step_cols
        column_panel = lax.dynamic_slice_in_dim(columns, offset, step_cols, 0)
        shifts = lax.dynamic_slice_in_dim(col_shift, offset, step_cols, 0)
        scores = shifts[None, :] + pair_dot(rows_emb, column_panel) / epsilon
        peak_new = jnp.maximum(peak_now, jnp.max(scores, axis=1))
        mass_new = mass_now * jnp.exp(peak_now - peak_new) + jnp.sum(
            jnp.exp(scores - peak_new[:, None]), axis=1
        )
        return ((peak_new, mass_new), None)

    result, unused = lax.scan(advance, (start_peak, start_mass), jnp.arange(blocks))
    return result


def column_partial(rows_emb, columns, row_shift):
    step_cols, blocks = column_blocks(columns)

    def advance(running, block_index):
        column_panel = lax.dynamic_slice_in_dim(columns, block_index * step_cols, step_cols, 0)
        scores = row_shift[:, None] + pair_dot(rows_emb, column_panel) / epsilon
        col_peak = jnp.max(scores, axis=0)
        col_mass = jnp.sum(jnp.exp(scores - col_peak[None, :]), axis=0)
        return (running, (col_peak, col_mass))

    unused, outputs = lax.scan(advance, 0, jnp.arange(blocks))
    return (outputs[0].reshape(-1), outputs[1].reshape(-1))


def row_term(rows_emb, columns, row_shift, col_shift, log_count):
    step_cols, blocks = column_blocks(columns)
    start_mass = jnp.zeros((rows_emb.shape[0],), jnp.float32)
    start_mixed = jnp.zeros((rows_emb.shape[0], rows_emb.shape[1]), jnp.float32)

    def advance(running, block_index):
        mass_now, mixed_now = running
        offset = block_index * step_cols
        column_panel = lax.dynamic_slice_in_dim(columns, offset, step_cols, 0)
        shifts = lax.dynamic_slice_in_dim(col_shift, offset, step_cols, 0)
        products = pair_dot(rows_emb, column_panel) / epsilon
        weights = jnp.exp(row_shift[:, None] + shifts[None, :] + products - log_count)
        mass_now = mass_now + jnp.sum(weights, axis=1)
        mixed_now = mixed_now + jnp.dot(
            weights.astype(jnp.bfloat16), column_panel, preferred_element_type=jnp.float32
        )
        return ((mass_now, mixed_now), None)

    result, unused = lax.scan(advance, (start_mass, start_mixed), jnp.arange(blocks))
    return rows_emb.astype(jnp.float32) * result[0][:, None] - result[1]


def both_terms(rows_emb, columns, row_shift, col_shift, log_count):
    step_cols, blocks = column_blocks(columns)
    start_mass = jnp.zeros((rows_emb.shape[0],), jnp.float32)
    start_mixed = jnp.zeros((rows_emb.shape[0], rows_emb.shape[1]), jnp.float32)

    def advance(running, block_index):
        mass_now, mixed_now = running
        offset = block_index * step_cols
        column_panel = lax.dynamic_slice_in_dim(columns, offset, step_cols, 0)
        shifts = lax.dynamic_slice_in_dim(col_shift, offset, step_cols, 0)
        products = pair_dot(rows_emb, column_panel) / epsilon
        weights = jnp.exp(row_shift[:, None] + shifts[None, :] + products - log_count)
        rounded = weights.astype(jnp.bfloat16)
        mass_now = mass_now + jnp.sum(weights, axis=1)
        mixed_now = mixed_now + jnp.dot(rounded, column_panel, preferred_element_type=jnp.float32)
        col_mass = jnp.sum(weights, axis=0)
        col_mixed = lax.dot_general(
            rounded, rows_emb, (((0,), (0,)), ((), ())), preferred_element_type=jnp.float32
        )
        col_part = column_panel.astype(jnp.float32) * col_mass[:, None] - col_mixed
        return ((mass_now, mixed_now), col_part)

    result, col_parts = lax.scan(advance, (start_mass, start_mixed), jnp.arange(blocks))
    row_part = rows_emb.astype(jnp.float32) * result[0][:, None] - result[1]
    return (row_part, col_parts.reshape(blocks * step_cols, rows_emb.shape[1]))


def on_device(regions, phrases):
    own_rows = regions.shape[0]
    row_place = lax.axis_index("row")
    col_place = lax.axis_index("col")
    point_count = own_rows * lax.axis_size("row") * lax.axis_size("col")
    log_count = math.log(point_count)
    row_regions, row_phrases = (
        lax.all_gather(regions, "col", axis=0, tiled=True),
        lax.all_gather(phrases, "col", axis=0, tiled=True),
    )
    col_regions, col_phrases = (
        lax.all_gather(regions, "row", axis=0, tiled=True),
        lax.all_gather(phrases, "row", axis=0, tiled=True),
    )
    row_norm_x = half_square(row_regions)
    row_norm_y = half_square(row_phrases)
    col_norm_x = half_square(col_regions)
    col_norm_y = half_square(col_phrases)

    def own_piece(values, place):
        return lax.dynamic_slice_in_dim(values, place * own_rows, own_rows, values.ndim - 1)

    def soft_update(norms, peak_rows, masses):
        return norms + epsilon * log_count - epsilon * (peak_rows + jnp.log(masses))

    def across_rows(peak_rows, masses):
        highest = lax.pmax(peak_rows, "row")
        joined = (highest, lax.psum(masses * jnp.exp(peak_rows - highest), "row"))
        return joined

    cross_g = jnp.zeros((col_regions.shape[0],), jnp.float32)
    cross_f = jnp.zeros((row_regions.shape[0],), jnp.float32)
    self_prow = jnp.zeros((row_regions.shape[0],), jnp.float32)
    self_qrow = jnp.zeros((row_regions.shape[0],), jnp.float32)
    self_pcol = jnp.zeros((col_regions.shape[0],), jnp.float32)
    self_qcol = jnp.zeros((col_regions.shape[0],), jnp.float32)
    for sweep_index in range(ITERS):
        cross_peak, cross_mass = row_partial(
            row_regions, col_phrases, (cross_g - col_norm_y) / epsilon
        )
        prow_peak, prow_mass = row_partial(
            row_regions, col_regions, (self_pcol - col_norm_x) / epsilon
        )
        qrow_peak, qrow_mass = row_partial(
            row_phrases, col_phrases, (self_qcol - col_norm_y) / epsilon
        )
        across_peak_rows = jnp.stack([cross_peak, prow_peak, qrow_peak])
        across_highest = lax.pmax(across_peak_rows, "col")
        peak_rows = across_highest
        masses = lax.psum(
            jnp.stack([cross_mass, prow_mass, qrow_mass])
            * jnp.exp(across_peak_rows - across_highest),
            "col",
        )
        updated = soft_update(jnp.stack([row_norm_x, row_norm_x, row_norm_y]), peak_rows, masses)
        cross_f = updated[0]
        self_prow = updated[1] if sweep_index == 0 else 0.5 * (self_prow + updated[1])
        self_qrow = updated[2] if sweep_index == 0 else 0.5 * (self_qrow + updated[2])
        g_peak, g_mass = column_partial(row_regions, col_phrases, (cross_f - row_norm_x) / epsilon)
        peak_cols, col_masses = across_rows(g_peak[None, :], g_mass[None, :])
        cross_g = soft_update(col_norm_y, peak_cols[0], col_masses[0])
        pieces = jnp.stack([own_piece(self_prow, col_place), own_piece(self_qrow, col_place)])
        spread = lax.all_gather(pieces, "row", axis=1, tiled=True)
        self_pcol = spread[0]
        self_qcol = spread[1]
    local_sum = jnp.sum(own_piece(cross_f, col_place) - own_piece(self_prow, col_place)) + jnp.sum(
        own_piece(cross_g, row_place) - own_piece(self_qrow, col_place)
    )
    divergence = lax.psum(local_sum, ("row", "col")) / point_count
    shift_urow = (cross_f - row_norm_x) / epsilon
    shift_hcol = (cross_g - col_norm_y) / epsilon
    shift_prow = (self_prow - row_norm_x) / epsilon
    shift_pcol = (self_pcol - col_norm_x) / epsilon
    shift_qrow = (self_qrow - row_norm_y) / epsilon
    shift_qcol = (self_qcol - col_norm_y) / epsilon
    cross_rows, cross_cols = both_terms(row_regions, col_phrases, shift_urow, shift_hcol, log_count)
    grad_x = cross_rows - row_term(row_regions, col_regions, shift_prow, shift_pcol, log_count)
    grad_y = -row_term(row_phrases, col_phrases, shift_qrow, shift_qcol, log_count)
    summed = lax.psum_scatter(
        jnp.stack([grad_x, grad_y], axis=1), "col", scatter_dimension=0, tiled=True
    )
    grad_regions = summed[:, 0]
    grad_phrases = summed[:, 1] + lax.psum_scatter(
        cross_cols, "row", scatter_dimension=0, tiled=True
    )
    return (grad_regions, grad_phrases, divergence)


def solution(mesh):
    placed = (P(("row", "col"), None), P(("row", "col"), None))
    return jax.shard_map(
        on_device,
        mesh=mesh,
        in_specs=placed,
        out_specs=(P(("row", "col"), None), P(("row", "col"), None), P()),
        check_vma=False,
    )
```

profile of v0, /device:TPU:1, one launch (start us, length us, event | category | flops | bytes accessed | tf_op | source)
XLA Modules:
  0.0 1115.2 jit_solution(2560315616028894979)
XLA Ops:
  8.9 24.2 %all_gather.18 = bf16[512,256]{1,0:T(8,128)(2,1)S(1)} all-gather(bf16[64,256]{1,0:T(8,128)(2,1)} %param.24), channel_id=1, replica_groups=mesh['row'=32,'col'=8] {'col'}, dimensions={0}, use_global_device_ids=true | all-gather | bytes 294912 | tf_op jit(solution)/shard_map/all_gather | solution.py:121
  33.1 22.6 %all_gather.19 = bf16[512,256]{1,0:T(8,128)(2,1)S(1)} all-gather(bf16[64,256]{1,0:T(8,128)(2,1)} %param.25), channel_id=1, replica_groups=mesh['row'=32,'col'=8] {'col'}, dimensions={0}, use_global_device_ids=true | all-gather | bytes 294912 | tf_op jit(solution)/shard_map/all_gather | solution.py:122
  56.0 36.5 %all-gather.5.cloned.1.call-done = bf16[2048,256]{1,0:T(8,128)(2,1)} async-done(((bf16[64,256]{1,0:T(8,128)(2,1)}), bf16[2048,256]{1,0:T(8,128)(2,1)}) %all-gather.5.cloned.1.call-update) | async-done | bytes 1048592 | tf_op jit(solution)/shard_map/all_gather | solution.py:126
  94.2 75.5 %all-gather.7.cloned.1.call-done = bf16[2048,256]{1,0:T(8,128)(2,1)} async-done(((bf16[64,256]{1,0:T(8,128)(2,1)}), bf16[2048,256]{1,0:T(8,128)(2,1)}) %all-gather.7.cloned.1.call-update) | async-done | bytes 1048592 | tf_op jit(solution)/shard_map/all_gather | solution.py:125
  171.4 24.7 %while.151 = (s32[]{:T(128)}, f32[512]{0:T(512)S(1)}, f32[512]{0:T(512)S(1)}, s32[16]{0:T(128)S(1)}, f32[2048]{0:T(1024)S(1)}, /*index=5*/bf16[2048,256]{1,0:T(8...) while((s32[]{:T(128)}, f32[512]{0:T(512)S(1)}, ...), condition=%wide.region_6.0_spmd.clone, body=%wide.region_3.6_spmd.clone.sunk | while | flops 33884676 | bytes 880322 | solution.py:47
  196.1 38.1 %while.152 = (s32[]{:T(128)}, f32[512]{0:T(512)S(1)}, f32[512]{0:T(512)S(1)}, s32[16]{0:T(128)S(1)}, f32[2048]{0:T(1024)S(1)}, /*index=5*/bf16[2048,256]{1,0:T(8...) while((s32[]{:T(128)}, f32[512]{0:T(512)S(1)}, ...), condition=%wide.region_11.12_spmd.clone, body=%wide.region_8.11_spmd.clone.sunk | while | flops 33884676 | bytes 880322 | solution.py:47
  234.3 24.7 %while.153 = (s32[]{:T(128)}, f32[512]{0:T(512)S(1)}, f32[512]{0:T(512)S(1)}, s32[16]{0:T(128)S(1)}, f32[2048]{0:T(1024)S(1)}, /*index=5*/bf16[2048,256]{1,0:T(8...) while((s32[]{:T(128)}, f32[512]{0:T(512)S(1)}, ...), condition=%wide.region_15.16_spmd.clone, body=%wide.region_12.15_spmd.clone.sunk | while | flops 33884676 | bytes 880322 | solution.py:47
  259.0 15.2 %pmax.28 = f32[3,512]{1,0:T(4,128)S(1)} all-reduce(f32[3,512]{1,0:T(4,128)S(1)} %pad_maximum_fusion.1), channel_id=1, replica_groups=mesh['row'=32,'col'=8] {'col'}, use_global_device_ids=true, to_apply=%region_16.17 | all-reduce | flops 1536 | bytes 12288 | tf_op jit(solution)/shard_map/pmax | solution.py:161
  287.0 27.2 %while.149 = (s32[]{:T(128)}, f32[16,128]{1,0:T(8,128)S(1)}, f32[16,128]{1,0:T(8,128)S(1)}, f32[512]{0:T(512)S(1)}, s32[16]{0:T(128)S(1)}, /*index=5*/bf16[2048,...) while((s32[]{:T(128)}, f32[16,128]{1,0:T(8,128)S(1)}, ...), condition=%wide.region_21.22_spmd, body=%wide.region_18.21_spmd.sunk | while | flops 33881860 | bytes 857787 | solution.py:61
  314.2 72.8 %pmax.29 = f32[1,2048]{1,0:T(1,128)S(1)} all-reduce(f32[1,2048]{1,0:T(1,128)S(1)} %bitcast.203), channel_id=1, replica_groups=mesh['row'=32,'col'=8] {'row'}, use_global_device_ids=true, to_apply=%region_22.23 | all-reduce | flops 2048 | bytes 16384 | tf_op jit(solution)/shard_map/pmax | solution.py:140
  387.1 66.0 %psum.36 = f32[1,2048]{1,0:T(1,128)S(1)} all-reduce(f32[1,2048]{1,0:T(1,128)S(1)} %exponential_multiply_fusion.1), channel_id=1, replica_groups=mesh['row'=32,'col'=8] {'row'}, use_global_device_ids=true, to_apply=%region_23.24 | all-reduce | flops 2048 | bytes 16384 | tf_op jit(solution)/shard_map/psum | solution.py:141
  453.3 36.9 %all-gather = f32[32,64,2]{1,2,0:T(2,128)S(1)} all-gather(f32[1,64,2]{1,2,0:T(2,128)S(1)} %maximum_bitcast_fusion), channel_id=1, replica_groups=mesh['row'=32,'col'=8] {'row'}, dimensions={0}, use_global_device_ids=true | all-gather | bytes 16896 | tf_op jit(solution)/shard_map/all_gather | solution.py:176
  490.4 26.9 %while.154 = (s32[]{:T(128)}, f32[512]{0:T(512)S(1)}, f32[512]{0:T(512)S(1)}, s32[16]{0:T(128)S(1)}, f32[2048]{0:T(1024)S(1)}, /*index=5*/bf16[2048,256]{1,0:T(8...) while((s32[]{:T(128)}, f32[512]{0:T(512)S(1)}, ...), condition=%wide.region_27.28_spmd.clone, body=%wide.region_24.27_spmd.clone.sunk | while | flops 33884676 | bytes 880322 | solution.py:47
  517.3 26.9 %while.156 = (s32[]{:T(128)}, f32[512]{0:T(512)S(1)}, f32[512]{0:T(512)S(1)}, s32[16]{0:T(128)S(1)}, f32[2048]{0:T(1024)S(1)}, /*index=5*/bf16[2048,256]{1,0:T(8...) while((s32[]{:T(128)}, f32[512]{0:T(512)S(1)}, ...), condition=%wide.region_35.36_spmd.clone, body=%wide.region_32.35_spmd.clone.sunk | while | flops 33884676 | bytes 880322 | solution.py:47
  544.2 40.3 %while.155 = (s32[]{:T(128)}, f32[512]{0:T(512)S(1)}, f32[512]{0:T(512)S(1)}, s32[16]{0:T(128)S(1)}, f32[2048]{0:T(1024)S(1)}, /*index=5*/bf16[2048,256]{1,0:T(8...) while((s32[]{:T(128)}, f32[512]{0:T(512)S(1)}, ...), condition=%wide.region_31.32_spmd.clone, body=%wide.region_28.31_spmd.clone.sunk | while | flops 33884676 | bytes 880322 | solution.py:47
  612.6 29.4 %while.150 = (s32[]{:T(128)}, f32[16,128]{1,0:T(8,128)S(1)}, f32[16,128]{1,0:T(8,128)S(1)}, f32[512]{0:T(512)S(1)}, s32[16]{0:T(128)S(1)}, /*index=5*/bf16[2048,...) while((s32[]{:T(128)}, f32[16,128]{1,0:T(8,128)S(1)}, ...), condition=%wide.region_41.42_spmd, body=%wide.region_38.41_spmd.sunk | while | flops 33881860 | bytes 857787 | solution.py:61
  641.9 72.8 %pmax.31 = f32[1,2048]{1,0:T(1,128)S(1)} all-reduce(f32[1,2048]{1,0:T(1,128)S(1)} %bitcast.201), channel_id=1, replica_groups=mesh['row'=32,'col'=8] {'row'}, use_global_device_ids=true, to_apply=%region_42.43 | all-reduce | flops 2048 | bytes 16384 | tf_op jit(solution)/shard_map/pmax | solution.py:140
  714.8 66.0 %psum.38 = f32[1,2048]{1,0:T(1,128)S(1)} all-reduce(f32[1,2048]{1,0:T(1,128)S(1)} %exponential_multiply_fusion), channel_id=1, replica_groups=mesh['row'=32,'col'=8] {'row'}, use_global_device_ids=true, to_apply=%region_43.44 | all-reduce | flops 2048 | bytes 16384 | tf_op jit(solution)/shard_map/psum | solution.py:141
  781.5 36.9 %all-gather.1 = f32[32,64,2]{1,2,0:T(2,128)S(1)} all-gather(f32[1,64,2]{1,2,0:T(2,128)S(1)} %maximum_bitcast_fusion.1), channel_id=1, replica_groups=mesh['row'=32,'col'=8] {'row'}, dimensions={0}, use_global_device_ids=true | all-gather | bytes 16896 | tf_op jit(solution)/shard_map/all_gather | solution.py:176
  818.6 28.7 %while.159 = (s32[]{:T(128)}, f32[512]{0:T(512)S(1)}, f32[512,256]{1,0:T(8,128)S(1)}, f32[512]{0:T(512)S(1)}, s32[16]{0:T(128)S(1)}, /*index=5*/f32[2048]{0:T(10...) while((s32[]{:T(128)}, f32[512]{0:T(512)S(1)}, ...), condition=%wide.region_53.54_spmd.clone, body=%wide.region_51.53_spmd.clone.sunk | while | flops 67764736 | bytes 1715918 | solution.py:83
  847.3 57.8 %while.158 = (s32[]{:T(128)}, f32[512]{0:T(512)S(1)}, f32[512,256]{1,0:T(8,128)S(1)}, f32[512]{0:T(512)S(1)}, s32[16]{0:T(128)S(1)}, /*index=5*/f32[2048]{0:T(10...) while((s32[]{:T(128)}, f32[512]{0:T(512)S(1)}, ...), condition=%wide.region_50.51_spmd.clone, body=%wide.region_48.0_spmd.clone.sunk | while | flops 67764736 | bytes 1715918 | solution.py:83
  905.1 45.4 %while.157 = (s32[]{:T(128)}, f32[512]{0:T(512)S(1)}, f32[512,256]{1,0:T(8,128)S(1)}, f32[16,128,256]{2,1,0:T(8,128)}, f32[512]{0:T(512)S(1)}, /*index=5*/s32[16...) while((s32[]{:T(128)}, f32[512]{0:T(512)S(1)}, ...), condition=%wide.region_47.48_spmd.clone, body=%wide.region_44.0_spmd.clone.sunk | while | flops 101482880 | bytes 2306782 | solution.py:109
  953.8 75.7 %psum.39 = f32[]{:T(128)} all-reduce(f32[]{:T(128)S(6)} %add.388), channel_id=1, replica_groups=mesh['row'=32,'col'=8] {'row','col'}, use_global_device_ids=true, to_apply=%region_58.59 | all-reduce | flops 1 | bytes 8 | tf_op jit(solution)/shard_map/psum | solution.py:182
  1031.7 74.4 %reduce-scatter.5.cloned.1.call-done = f32[64,256]{1,0:T(8,128)} async-done(((f32[2048,256]{1,0:T(8,128)}), f32[64,256]{1,0:T(8,128)}) %reduce-scatter.5.cloned.1.call-update) | async-done | bytes 65552 | tf_op jit(solution)/shard_map/reduce_scatter | solution.py:196
  (1180 shorter events, 309.7 us)
Async XLA Ops:
  7.2 85.4 %all-gather.5.cloned.1.call-start = ((), (), s32[]{:S(2)}) async-start(), calls=%async_computation.2 | async-start | bytes 1081344 | tf_op jit(solution)/shard_map/all_gather | solution.py:126
  7.9 161.9 %all-gather.7.cloned.1.call-start = ((), (), s32[]{:S(2)}) async-start(), calls=%async_computation.3 | async-start | bytes 1081344 | tf_op jit(solution)/shard_map/all_gather | solution.py:125
  8.6 1021.6 %reduce-scatter.3.cloned.1.call-start = ((), (), s32[]{:S(2)}) async-start(), calls=%async_computation.4 | async-start | bytes 1179648 | tf_op jit(solution)/shard_map/reduce_scatter | solution.py:192
  92.5 78.8 %copy-start = (bf16[2048,256]{1,0:T(8,128)(2,1)S(1)}, bf16[2048,256]{1,0:T(8,128)(2,1)}, u32[]{:S(2)}) copy-start(bf16[2048,256]{1,0:T(8,128)(2,1)} %all-gather.5.cloned.1.call-done) | copy-start | bytes 3145732
  951.9 154.1 %reduce-scatter.5.cloned.1.call-start = ((), (), s32[]{:S(2)}) async-start(), calls=%async_computation.5 | async-start | bytes 2162688 | tf_op jit(solution)/shard_map/reduce_scatter | solution.py:196
Sparse Core Ops, SparseCore 0:
  10.8 81.7 all-gather.4
  95.3 74.4 all-gather.6
  952.1 31.9 reduce-scatter.2
  988.1 117.8 reduce-scatter.4
where the time goes:
time: 1120 us
  blocking collectives  529 us (47%)
  waiting for transfers between devices  188 us (17%)
  matrix products  128 us (11%)
  local copies, waits for them, and re-layouts  116 us (10%)
  loops' own time  112 us (10%)
  other arithmetic  23.4 us (2%)
  between operations  17.5 us (2%)
    pmax x2, blocking collectives, across_rows(): highest = lax.pmax(peak_rows, 'row')  146 us
    psum x2, blocking collectives, across_rows(): joined = (highest, lax.psum(masses * jnp.exp(peak_rows - highest), 'row'))  132 us
    dynamic_slice x176, local copies, waits for them, and re-layouts, row_partial(): lax.scan(advance, (start_peak, start_mass), jnp.arange(blocks))  100 us
    dot_general x176, matrix products, pair_dot(): lax.dot_general(left_rows, right_rows, (((1,), (1,)), ((), ())), preferre...  86.7 us
    psum x1, blocking collectives, on_device(): divergence = lax.psum(local_sum, ('row', 'col')) / point_count  75.7 us
    all_gather x1, waiting for transfers between devices, on_device(): lax.all_gather(regions, 'row', axis=0, tiled=True)  75.5 us
    reduce_scatter x1, waiting for transfers between devices, on_device(): lax.psum_scatter(cross_cols, 'row', scatter_dimension=0, tiled=True)  74.4 us
    all_gather x2, blocking collectives, on_device(): spread = lax.all_gather(pieces, 'row', axis=1, tiled=True)  73.9 us
  transfers between devices with their start and end apart: 4, of which 3 were waited for; matrix products, arithmetic and copies ran while one was open for 0% of the time, Pallas kernels for 0%

commit v1 on v0

v1 whole, which is shorter than its diff:
```python
import math

import jax
import jax.numpy as jnp
from jax import lax
from jax.experimental import pallas as pl
from jax.experimental.pallas import tpu as pltpu
from jax.sharding import Mesh
from jax.sharding import PartitionSpec as P

EPSILON = 0.1
POINTS = 16384
OWN = 64
WIDTH = 256
HALF = 512
BLOCK = 1024
LOG_COUNT = math.log2(POINTS)
BETA = 1.0 / (EPSILON * math.log(2.0))
INV_LN2 = 1.0 / math.log(2.0)

AXES = ("xh", "z", "core", "xl", "y")
ROW_GROUP = ("core", "xl", "y")
COL_GROUP = ("xh", "z")

VMEM_LIMIT = 32 * 1024 * 1024


def log2(values):
    return jnp.log(values) * INV_LN2


def dot_nt(left, right):
    return lax.dot_general(left, right, (((1,), (1,)), ((), ())), preferred_element_type=jnp.float32)


def dense_to_sub(values):
    pieces = [jnp.broadcast_to(values[t : t + 1, :], (128, 128)).T for t in range(8)]
    return jnp.concatenate(pieces, axis=0)


def dense_to_lane(values):
    return jnp.concatenate([values[t : t + 1, :] for t in range(8)], axis=1)


def lane_to_dense(values):
    return jnp.concatenate([values[:, t * 128 : (t + 1) * 128] for t in range(8)], axis=0)


def widen(sub, lanes):
    return jnp.concatenate([sub] * (lanes // 128), axis=1)


def block_rows(own, other, which):
    parts = [ref[:, which * OWN : (which + 1) * OWN, :].reshape(HALF, WIDTH) for ref in (own, other)]
    return jnp.concatenate(parts, axis=0)


def quarter_rows(own, other, which, quarter):
    ref = own if quarter < 2 else other
    start = (quarter % 2) * 4
    return ref[start : start + 4, which * OWN : (which + 1) * OWN, :].reshape(256, WIDTH)


def half_rows(ref, which):
    return ref[:, which * OWN : (which + 1) * OWN, :].reshape(HALF, WIDTH)


def squares_split(rows):
    values = rows.astype(jnp.float32)
    squares = values * values
    high = squares.astype(jnp.bfloat16)
    low = (squares - high.astype(jnp.float32)).astype(jnp.bfloat16)
    return high, low


def norms_sub(rows):
    high, low = squares_split(rows)
    ones = jnp.ones((WIDTH, 128), jnp.bfloat16)
    total = jnp.dot(high, ones, preferred_element_type=jnp.float32) + jnp.dot(
        low, ones, preferred_element_type=jnp.float32
    )
    return total * (0.5 * BETA)


def norms_lane(rows):
    high, low = squares_split(rows)
    ones = jnp.ones((8, WIDTH), jnp.bfloat16)
    total = dot_nt(ones, high) + dot_nt(ones, low)
    return total[0:1, :] * (0.5 * BETA)


def sum_pass(reduced, own, other, which, sub, lane):
    outs = []
    wide = widen(sub, 256)
    for quarter in range(4):
        products = dot_nt(reduced, quarter_rows(own, other, which, quarter))
        part = lane[:, quarter * 256 : (quarter + 1) * 256]
        outs.append(jnp.sum(jnp.exp2(products * BETA + wide + part), axis=0, keepdims=True))
    return lane_to_dense(jnp.concatenate(outs, axis=1))


def peak_pass(reduced, own, other, which, sub):
    outs = []
    wide = widen(sub, 256)
    for quarter in range(4):
        products = dot_nt(reduced, quarter_rows(own, other, which, quarter))
        scores = products * BETA + wide
        peak = jnp.max(scores, axis=0, keepdims=True)
        mass = jnp.sum(jnp.exp2(scores - peak), axis=0, keepdims=True)
        outs.append(peak + log2(mass))
    return lane_to_dense(jnp.concatenate(outs, axis=1))


def swap_halves(values):
    return jnp.concatenate([values[4:8], values[0:4]], axis=0)


def peer_halves(ref, place, offset):
    mine = ref[pl.ds(place * 8, 8), offset : offset + 8, :]
    theirs = ref[pl.ds((1 - place) * 8, 8), offset : offset + 8, :]
    return mine, theirs


def join_sums(ref, place, offset):
    mine, theirs = peer_halves(ref, place, offset)
    return jnp.sum(mine, axis=0) + swap_halves(jnp.sum(theirs, axis=0))


def join_logs(ref, place, offset):
    mine, theirs = peer_halves(ref, place, offset)
    peak = jnp.maximum(jnp.max(mine, axis=0), swap_halves(jnp.max(theirs, axis=0)))
    other_peak = swap_halves(peak)
    mass = jnp.sum(jnp.exp2(mine - peak[None]), axis=0) + swap_halves(
        jnp.sum(jnp.exp2(theirs - other_peak[None]), axis=0)
    )
    return peak + log2(mass)


def lane_index():
    return lax.broadcasted_iota(jnp.int32, (1, 128), 1)


def own_piece(dense, place):
    row = jnp.zeros((1, 128), jnp.float32)
    for k in range(4):
        row = jnp.where(place // 2 == k, dense[k : k + 1, :], row)
    return jnp.where(place % 2 == 0, row, pltpu.roll(row, 64, 1))


def pair_row(first, second):
    return jnp.where(lane_index() < 64, first, pltpu.roll(second, 64, 1))


def piggy_rows(ref, place, row):
    order = []
    for base in (place * 8, (1 - place) * 8):
        for k in range(8):
            order.append(ref[base + k, row : row + 1, :])
    even = jnp.concatenate(order[0::2], axis=0)
    odd = jnp.concatenate(order[1::2], axis=0)
    return even, odd


def unpair(even, odd):
    lane = lax.broadcasted_iota(jnp.int32, (8, 128), 1)
    first = jnp.where(lane < 64, even, pltpu.roll(odd, 64, 1))
    second = jnp.where(lane < 64, pltpu.roll(even, 64, 1), odd)
    return first, second


def canonical_sum(values):
    return jnp.sum(values[0:4], keepdims=True) + jnp.sum(values[4:8], keepdims=True)


def send_all(message_ref, rows):
    message_ref[...] = jnp.broadcast_to(rows[None], message_ref.shape)


def first_rows(r_own, r_other, c_own, c_other, message, norms):
    x_col = block_rows(c_own, c_other, 0)
    y_col = block_rows(c_own, c_other, 1)
    x_norm_sub = norms_sub(x_col)
    y_norm_sub = norms_sub(y_col)
    x_norm = norms_lane(block_rows(r_own, r_other, 0))
    y_norm = norms_lane(block_rows(r_own, r_other, 1))
    cross = peak_pass(y_col, r_own, r_other, 0, -y_norm_sub)
    self_p = sum_pass(x_col, r_own, r_other, 0, -x_norm_sub, -x_norm)
    self_q = sum_pass(y_col, r_own, r_other, 1, -y_norm_sub, -y_norm)
    send_all(message, jnp.concatenate([cross, self_p, self_q], axis=0))
    x_norm_col = norms_lane(x_col)
    y_norm_col = norms_lane(y_col)
    norms[...] = jnp.concatenate(
        [lane_to_dense(v) for v in (x_norm, y_norm, x_norm_col, y_norm_col)], axis=0
    )


def first_cols(place, r_own, r_other, c_own, c_other, got, message, state):
    core, spot = place[0], place[1]
    u = LOG_COUNT - join_logs(got, core, 0)
    p = LOG_COUNT - log2(join_sums(got, core, 8))
    q = LOG_COUNT - log2(join_sums(got, core, 16))
    x_row = block_rows(r_own, r_other, 0)
    cross = peak_pass(x_row, c_own, c_other, 1, dense_to_sub(u))
    carry = pair_row(own_piece(p, spot), own_piece(q, spot))
    send_all(message, jnp.concatenate([cross, jnp.broadcast_to(carry, (8, 128))], axis=0))
    state[...] = jnp.concatenate([u, p, q], axis=0)


def second_rows(place, r_own, r_other, c_own, c_other, norms, state, got, message, h_out):
    far = place[2]
    h = LOG_COUNT - join_logs(got, far, 0)
    p_col, q_col = unpair(*piggy_rows(got, far, 8))
    x_col = block_rows(c_own, c_other, 0)
    y_col = block_rows(c_own, c_other, 1)
    cross = sum_pass(y_col, r_own, r_other, 0, dense_to_sub(h), dense_to_lane(state[0:8, :]))
    self_p = sum_pass(
        x_col, r_own, r_other, 0, dense_to_sub(p_col - norms[16:24, :]), -dense_to_lane(norms[0:8, :])
    )
    self_q = sum_pass(
        y_col, r_own, r_other, 1, dense_to_sub(q_col - norms[24:32, :]), -dense_to_lane(norms[8:16, :])
    )
    send_all(message, jnp.concatenate([cross, self_p, self_q], axis=0))
    h_out[...] = h


def second_cols(place, r_own, r_other, c_own, c_other, norms, state, h_in, got, message, shifts):
    core, spot = place[0], place[1]
    u = state[0:8, :] + (LOG_COUNT - log2(join_sums(got, core, 0)))
    p = 0.5 * (state[8:16, :] + (LOG_COUNT - log2(join_sums(got, core, 8))))
    q = 0.5 * (state[16:24, :] + (LOG_COUNT - log2(join_sums(got, core, 16))))
    pt = p - norms[0:8, :]
    qt = q - norms[8:16, :]
    x_row = block_rows(r_own, r_other, 0)
    cross = sum_pass(x_row, c_own, c_other, 1, dense_to_sub(u), dense_to_lane(h_in[...]))
    first = pair_row(own_piece(u, spot), own_piece(pt, spot))
    second = pair_row(own_piece(qt, spot), jnp.zeros((1, 128), jnp.float32))
    total = jnp.broadcast_to(canonical_sum(u - pt - qt), (6, 128))
    send_all(message, jnp.concatenate([cross, first, second, total], axis=0))
    shifts[...] = jnp.concatenate([u, pt, qt], axis=0)


def last_cols(place, h_in, got, message, cols, total):
    far, spot = place[2], place[3]
    h = h_in[...] + (LOG_COUNT - log2(join_sums(got, far, 0)))
    u_col, p_col = unpair(*piggy_rows(got, far, 8))
    q_col, unused = unpair(*piggy_rows(got, far, 9))
    piece = own_piece(h, spot)
    part = jnp.broadcast_to(canonical_sum(h), (7, 128))
    send_all(message, jnp.concatenate([piece, part], axis=0))
    cols[...] = jnp.concatenate([h, u_col, p_col, q_col], axis=0)
    total[...] = jnp.sum(got[:, 8:16, :], axis=0)


def gradients(place, r_own, r_other, c_own, c_other, shifts, cols, total, got, kept, sent, divergence):
    core = place[0]
    h_row, unused = unpair(*piggy_rows(got, core, 0))
    summed = total[...] + jnp.sum(got[...], axis=0)
    divergence[...] = summed * (1.0 / (POINTS * BETA))
    u_sub = dense_to_sub(shifts[0:8, :])
    p_sub = dense_to_sub(shifts[8:16, :])
    q_sub = dense_to_sub(shifts[16:24, :])
    h_sub = dense_to_sub(h_row)
    h_lane, u_lane, p_lane, q_lane = [
        dense_to_lane(cols[8 * k : 8 * k + 8, :]) - LOG_COUNT for k in range(4)
    ]
    x_col = block_rows(c_own, c_other, 0)
    y_col = block_rows(c_own, c_other, 1)

    def weights(rows, columns, sub, lane):
        products = dot_nt(rows, columns)
        values = jnp.exp2(products * BETA + widen(sub, BLOCK) + lane)
        mass = jnp.sum(values, axis=1, keepdims=True)
        mixed = jnp.dot(values.astype(jnp.bfloat16), columns, preferred_element_type=jnp.float32)
        return mass, mixed

    for ref, out, start in ((r_other, sent, HALF), (r_own, kept, 0)):
        part = slice(start, start + HALF)
        for which, cross_col, self_col, cross_sub, self_sub, cross_lane, self_lane in (
            (0, y_col, x_col, u_sub, p_sub, h_lane, p_lane),
            (1, x_col, y_col, h_sub, q_sub, u_lane, q_lane),
        ):
            rows = half_rows(ref, which)
            cross_mass, cross_mixed = weights(rows, cross_col, cross_sub[part], cross_lane)
            self_mass, self_mixed = weights(rows, self_col, self_sub[part], self_lane)
            grad = rows.astype(jnp.float32) * (cross_mass - self_mass) - cross_mixed + self_mixed
            out[:, which * OWN : (which + 1) * OWN, :] = grad.reshape(8, OWN, WIDTH).astype(out.dtype)


def call(body, outs, smem, *args):
    shapes = [jax.ShapeDtypeStruct(shape, dtype) for shape, dtype in outs]
    specs = [pl.BlockSpec(memory_space=pltpu.VMEM)] * len(args)
    if smem:
        specs[0] = pl.BlockSpec(memory_space=pltpu.SMEM)
    return pl.pallas_call(
        body,
        out_shape=shapes,
        in_specs=specs,
        out_specs=[pl.BlockSpec(memory_space=pltpu.VMEM)] * len(outs),
        compiler_params=pltpu.CompilerParams(vmem_limit_bytes=VMEM_LIMIT),
    )(*args)


def share(message, axes):
    return lax.all_to_all(message, axes, 0, 0, tiled=True)


def on_device(regions, phrases):
    f32 = jnp.float32
    core = lax.axis_index("core")
    spot_row = lax.axis_index("xl") * 4 + lax.axis_index("y")
    far = lax.axis_index("xh")
    spot_col = lax.axis_index("z")
    place = jnp.stack([core, spot_row, far, spot_col]).astype(jnp.int32)

    own = jnp.concatenate([regions, phrases], axis=0)
    copies = jnp.broadcast_to(own[None], (8, 2 * OWN, WIDTH))
    c_own = share(copies, ("z",))
    c_other = lax.ppermute(c_own, "xh", [(0, 1), (1, 0)])
    r_own = share(copies, ("xl", "y"))
    r_other = lax.ppermute(r_own, "core", [(0, 1), (1, 0)])
    points = (r_own, r_other, c_own, c_other)

    def message(rows):
        return ((16, rows, 128), f32)

    sent, norms = call(first_rows, [message(24), ((32, 128), f32)], False, *points)
    got = share(sent, ROW_GROUP)
    sent, state = call(first_cols, [message(16), ((24, 128), f32)], True, place, *points, got)
    got = share(sent, COL_GROUP)
    sent, h_first = call(
        second_rows, [message(24), ((8, 128), f32)], True, place, *points, norms, state, got
    )
    got = share(sent, ROW_GROUP)
    sent, shifts = call(
        second_cols, [message(16), ((24, 128), f32)], True, place, *points, norms, state, h_first, got
    )
    got = share(sent, COL_GROUP)
    sent, cols, total = call(
        last_cols, [message(8), ((32, 128), f32), ((8, 128), f32)], True, place, h_first, got
    )
    got = share(sent, ROW_GROUP)
    kept, away, divergence = call(
        gradients,
        [((8, 2 * OWN, WIDTH), f32), ((8, 2 * OWN, WIDTH), f32), ((8, 128), f32)],
        True,
        place,
        *points,
        shifts,
        cols,
        total,
        got,
    )
    joined = kept + lax.ppermute(away, "core", [(0, 1), (1, 0)])
    summed = jnp.sum(share(joined, ("xl", "y")), axis=0)
    return (summed[0:OWN], summed[OWN : 2 * OWN], divergence[2, 0])


def solution(mesh):
    fine = Mesh(mesh.devices.reshape(2, 8, 2, 2, 4), AXES)
    return jax.shard_map(
        on_device,
        mesh=fine,
        in_specs=(P(AXES, None), P(AXES, None)),
        out_specs=(P(AXES, None), P(AXES, None), P()),
        check_vma=False,
    )
```

time: 1120 us -> 155 us (0.14)
  blocking collectives: 529 us -> 61.5 us
  waiting for transfers between devices: 188 us -> 44.4 us
  matrix products: 128 us -> 0 us
  local copies, waits for them, and re-layouts: 116 us -> 2 us
  loops' own time: 112 us -> 0 us
  starting transfers between devices: 0.16 us -> 26.2 us
  other arithmetic: 23.4 us -> 2.03 us
  Pallas kernels: 0 us -> 17.2 us
  between operations: 17.5 us -> 0.68 us
    psum x5 -> x0, blocking collectives: 233 us -> none  [the longest x2 132 us: across_rows(): joined = (highest, lax.psum(masses * jnp.exp(peak_rows - highest), 'row'))]
    pmax x4 -> x0, blocking collectives: 175 us -> none  [the longest x2 146 us: across_rows(): highest = lax.pmax(peak_rows, 'row')]
    dot_general x240 -> x0, matrix products: 128 us -> none  [the longest x176 86.7 us: pair_dot(): lax.dot_general(left_rows, right_rows, (((1,), (1,)), ((), ())), preferre...]
    all_gather x4 -> x0, blocking collectives: 121 us -> none  [the longest x2 73.9 us: on_device(): spread = lax.all_gather(pieces, 'row', axis=1, tiled=True)]
    another operation x11 -> x0, loops' own time: 112 us -> none  [the longest x6 61.5 us: row_partial(): lax.scan(advance, (start_peak, start_mass), jnp.arange(blocks))]
    all_gather x2 -> x0, waiting for transfers between devices: 112 us -> none  [the longest x1 75.5 us: on_device(): lax.all_gather(regions, 'row', axis=0, tiled=True)]
    dynamic_slice x321 -> x0, local copies, waits for them, and re-layouts: 112 us -> none  [the longest x176 100 us: row_partial(): lax.scan(advance, (start_peak, start_mass), jnp.arange(blocks))]
    reduce_scatter x2 -> x0, waiting for transfers between devices: 74.4 us -> none  [the longest x1 74.4 us: on_device(): lax.psum_scatter(cross_cols, 'row', scatter_dimension=0, tiled=True)]
  transfers between devices with their start and end apart: 4 -> 6, of which waited for: 3 -> 5; matrix products, arithmetic and copies ran while one was open for 0% -> 0% of each run, Pallas kernels for 0% -> 0%
where the time goes in v1:
time: 155 us; the launch traced here: 154 us
  blocking collectives  61.5 us (40%)
  waiting for transfers between devices  44.4 us (29%)
  starting transfers between devices  26.2 us (17%)
  Pallas kernels  17.2 us (11%)
  other arithmetic  2.03 us (1%)
  local copies, waits for them, and re-layouts  2 us (1%)
    all_to_all x5, blocking collectives, share(): return lax.all_to_all(message, axes, 0, 0, tiled=True)  61.5 us
    all_to_all x3, waiting for transfers between devices, share(): return lax.all_to_all(message, axes, 0, 0, tiled=True)  33.4 us
    all_to_all x3, starting transfers between devices, share(): return lax.all_to_all(message, axes, 0, 0, tiled=True)  20.6 us
    pallas_call x6, Pallas kernels, call(): pl.pallas_call(body, out_shape=shapes, in_specs=specs, out_specs=[pl.Bloc...  17.2 us
    ppermute x1, waiting for transfers between devices, on_device(): c_other = lax.ppermute(c_own, 'xh', [(0, 1), (1, 0)])  8.73 us
  transfers between devices with their start and end apart: 6, of which 5 were waited for; matrix products, arithmetic and copies ran while one was open for 0% of the time, Pallas kernels for 0%

profile of v1, /device:TPU:1, one launch (start us, length us, event | category | flops | bytes accessed | tf_op | source)
XLA Modules:
  0.0 154.1 jit_solution(9263585572169487892)
XLA Ops:
  0.6 0.8 pad_maximum_fusion
  1.4 0.8 broadcast_in_dim.2
  2.2 14.6 %all_to_all.40.r_own = bf16[8,128,256]{2,1,0:T(8,128)(2,1)S(1)} all-to-all(bf16[8,128,256]{2,1,0:T(8,128)(2,1)} %broadcast_in_dim.2), channel_id=1, replica_groups=mesh['xh'=2,'z'=8,'core'=2,'xl'=2,'y'=4] {'xl','y'}, dimensions={0} | all-to-all | bytes 1048576 | tf_op jit(solution)/shard_map/all_to_all | solution.py:304
  16.8 8.2 %all-to-all-start.1 = ((bf16[8,128,256]{2,1,0:T(8,128)(2,1)}), bf16[8,128,256]{2,1,0:T(8,128)(2,1)S(1)}, u32[]{:S(2)}, u32[]{:S(2)}) async-start(bf16[8,128,256]{2,1,0:T(8,128)(2,1)} %broadcast_in_dim.2), calls=%async_computation.1 | async-start | bytes 1048576 | tf_op jit(solution)/shard_map/all_to_all | solution.py:304
  25.0 2.7 %collective-permute-start = (bf16[8,128,256]{2,1,0:T(8,128)(2,1)S(1)}, bf16[8,128,256]{2,1,0:T(8,128)(2,1)S(1)}, u32[]{:S(2)}, u32[]{:S(2)}) collective-permute-start(bf16[8,128,256]{2,1,0:T(8,128)(2,1)S(1)} %all_to_all.40.r_own), channel_id=1, source_target_pairs={{0,8},{8,0},{1,9},{9,1},{2,10},{10,2},{3,11},{11,3},{4,12},{12,4},... | collective-permute-start | bytes 1572872 | tf_op jit(solution)/shard_map/ppermute | solution.py:320
  27.7 12.0 %all-to-all-done.1.c_own = bf16[8,128,256]{2,1,0:T(8,128)(2,1)S(1)} async-done(((bf16[8,128,256]{2,1,0:T(8,128)(2,1)}), bf16[8,128,256]{2,1,0:T(8,128)(2,1)S(1)}, u32[]{:S(2)}, u32[]{:S(2)}) %all-to-all-start.1) | async-done | bytes 524320 | tf_op jit(solution)/shard_map/all_to_all | solution.py:304
  39.7 2.5 %collective-permute-start.1 = (bf16[8,128,256]{2,1,0:T(8,128)(2,1)S(1)}, bf16[8,128,256]{2,1,0:T(8,128)(2,1)S(1)}, u32[]{:S(2)}, u32[]{:S(2)}) collective-permute-start(bf16[8,128,256]{2,1,0:T(8,128)(2,1)S(1)} %all-to-all-done.1.c_own), channel_id=1, source_target_pairs={{0,128},{128,0},{1,129},{129,1},{2,130},{130,2},{3,131},{131,3},{4... | collective-permute-start | bytes 1572872 | tf_op jit(solution)/shard_map/ppermute | solution.py:318
  42.2 8.7 %collective-permute-done.1.c_other = bf16[8,128,256]{2,1,0:T(8,128)(2,1)S(1)} collective-permute-done((bf16[8,128,256]{2,1,0:T(8,128)(2,1)S(1)}, bf16[8,128,256]{2,1,0:T(8,128)(2,1)S(1)}, u32[]{:S(2)}, u32[]{:S(2)}) %collective-permute-start.1) | collective-permute-done | bytes 524320 | tf_op jit(solution)/shard_map/ppermute | solution.py:318
  50.9 4.7 %shard_map.49 = (f32[16,24,128]{2,1,0:T(8,128)}, f32[32,128]{1,0:T(8,128)S(1)}) custom-call(bf16[8,128,256]{2,1,0:T(8,128)(2,1)S(1)} %all_to_all.40.r_own, bf16[8,128,256]{2,1,0:T(8,128)(2,1)S(1)} %collective-permute-done.r_other, bf16[8,128,256]{2,1,0:T(8,128)(2,1)S(1)} %all-to-all-done.1.c_own, bf16[8,128,256]{2,1,0:T(8,128)(2,1)S(1)} %collective-permute-done.1.c_other), custom_call_target="tpu_custom_call" | custom-call | tf_op jit(solution)/shard_map/pallas_call | solution.py:294
  55.6 8.9 %all-to-all-start.2 = ((f32[16,24,128]{2,1,0:T(8,128)}), f32[16,24,128]{2,1,0:T(8,128)S(1)}, u32[]{:S(2)}, u32[]{:S(2)}) async-start(f32[16,24,128]{2,1,0:T(8,128)} %get-tuple-element.18), calls=%async_computation.2 | async-start | bytes 393216 | tf_op jit(solution)/shard_map/all_to_all | solution.py:304
  64.5 7.0 %all-to-all-done.2.got = f32[16,24,128]{2,1,0:T(8,128)S(1)} async-done(((f32[16,24,128]{2,1,0:T(8,128)}), f32[16,24,128]{2,1,0:T(8,128)S(1)}, u32[]{:S(2)}, u32[]{:S(2)}) %all-to-all-start.2) | async-done | bytes 196640 | tf_op jit(solution)/shard_map/all_to_all | solution.py:304
  71.5 2.1 %shard_map.50 = (f32[16,16,128]{2,1,0:T(8,128)S(1)}, f32[24,128]{1,0:T(8,128)S(1)}) custom-call(s32[4]{0:T(128)S(1)} %pad_add_fusion.place, bf16[8,128,256]{2,1,0:T(8,128)(2,1)S(1)} %all_to_all.40.r_own, bf16[8,128,256]{2,1,0:T(8,128)(2,1)S(1)} %collective-permute-done.r_other, bf16[8,128,256]{2,1,0:T(8,128)(2,1)S(1)} %all-to-all-done.1.c_own, ...), custom_call_target="tpu_custom_call" | custom-call | tf_op jit(solution)/shard_map/pallas_call | solution.py:294
  73.6 13.5 %all_to_all.41.got = f32[16,16,128]{2,1,0:T(8,128)S(1)} all-to-all(f32[16,16,128]{2,1,0:T(8,128)S(1)} %get-tuple-element.20), channel_id=1, replica_groups=mesh['xh'=2,'z'=8,'core'=2,'xl'=2,'y'=4] {'xh','z'}, dimensions={0} | all-to-all | bytes 262144 | tf_op jit(solution)/shard_map/all_to_all | solution.py:304
  87.1 2.9 %shard_map.51 = (f32[16,24,128]{2,1,0:T(8,128)S(1)}, f32[8,128]{1,0:T(8,128)S(1)}) custom-call(s32[4]{0:T(128)S(1)} %pad_add_fusion.place, bf16[8,128,256]{2,1,0:T(8,128)(2,1)S(1)} %all_to_all.40.r_own, bf16[8,128,256]{2,1,0:T(8,128)(2,1)S(1)} %collective-permute-done.r_other, bf16[8,128,256]{2,1,0:T(8,128)(2,1)S(1)} %all-to-all-done.1.c_own, ...), custom_call_target="tpu_custom_call" | custom-call | tf_op jit(solution)/shard_map/pallas_call | solution.py:294
  90.0 11.4 %all_to_all.42.got = f32[16,24,128]{2,1,0:T(8,128)S(1)} all-to-all(f32[16,24,128]{2,1,0:T(8,128)S(1)} %get-tuple-element.22), channel_id=1, replica_groups=mesh['xh'=2,'z'=8,'core'=2,'xl'=2,'y'=4] {'core','xl','y'}, dimensions={0} | all-to-all | bytes 393216 | tf_op jit(solution)/shard_map/all_to_all | solution.py:304
  101.4 1.5 shard_map.52
  102.9 11.9 %all_to_all.43.got = f32[16,16,128]{2,1,0:T(8,128)S(1)} all-to-all(f32[16,16,128]{2,1,0:T(8,128)S(1)} %get-tuple-element.24), channel_id=1, replica_groups=mesh['xh'=2,'z'=8,'core'=2,'xl'=2,'y'=4] {'xh','z'}, dimensions={0} | all-to-all | bytes 262144 | tf_op jit(solution)/shard_map/all_to_all | solution.py:304
  114.8 0.7 shard_map.53
  115.5 10.1 %all_to_all.44.got = f32[16,8,128]{2,1,0:T(8,128)S(1)} all-to-all(f32[16,8,128]{2,1,0:T(8,128)S(1)} %get-tuple-element.27), channel_id=1, replica_groups=mesh['xh'=2,'z'=8,'core'=2,'xl'=2,'y'=4] {'core','xl','y'}, dimensions={0} | all-to-all | bytes 131072 | tf_op jit(solution)/shard_map/all_to_all | solution.py:304
  125.6 5.3 %shard_map.54 = (f32[8,128,256]{2,1,0:T(8,128)S(1)}, f32[8,128,256]{2,1,0:T(8,128)S(1)}, f32[8,128]{1,0:T(8,128)S(1)}) custom-call(s32[4]{0:T(128)S(1)} %pad_add_fusion.place, bf16[8,128,256]{2,1,0:T(8,128)(2,1)S(1)} %all_to_all.40.r_own, bf16[8,128,256]{2,1,0:T(8,128)(2,1)S(1)} %collective-permute-done.r_other, ...), custom_call_target="tpu_custom_call" | custom-call | tf_op jit(solution)/shard_map/pallas_call | solution.py:294
  131.5 2.3 %collective-permute-done.2 = f32[8,128,256]{2,1,0:T(8,128)S(1)} collective-permute-done((f32[8,128,256]{2,1,0:T(8,128)S(1)}, f32[8,128,256]{2,1,0:T(8,128)S(1)}, u32[]{:S(2)}, u32[]{:S(2)}) %collective-permute-start.2) | collective-permute-done | bytes 1048608 | tf_op jit(solution)/shard_map/ppermute | solution.py:353
  133.7 1.1 add.7
  134.9 3.6 %all-to-all-start.7 = ((f32[8,128,256]{2,1,0:T(8,128)}), f32[8,128,256]{2,1,0:T(8,128)S(1)}, u32[]{:S(2)}, u32[]{:S(2)}) async-start(f32[8,128,256]{2,1,0:T(8,128)} %add.7), calls=%async_computation.7 | async-start | bytes 2097152 | tf_op jit(solution)/shard_map/all_to_all | solution.py:304
  138.9 14.4 %all-to-all-done.7 = f32[8,128,256]{2,1,0:T(8,128)S(1)} async-done(((f32[8,128,256]{2,1,0:T(8,128)}), f32[8,128,256]{2,1,0:T(8,128)S(1)}, u32[]{:S(2)}, u32[]{:S(2)}) %all-to-all-start.7) | async-done | bytes 1048608 | tf_op jit(solution)/shard_map/all_to_all | solution.py:304
  (6 shorter events, 1.8 us)
Async XLA Ops:
  16.8 22.9 %all-to-all-start.1 = ((bf16[8,128,256]{2,1,0:T(8,128)(2,1)}), bf16[8,128,256]{2,1,0:T(8,128)(2,1)S(1)}, u32[]{:S(2)}, u32[]{:S(2)}) async-start(bf16[8,128,256]{2,1,0:T(8,128)(2,1)} %broadcast_in_dim.2), calls=%async_computation.1 | async-start | bytes 1048576 | tf_op jit(solution)/shard_map/all_to_all | solution.py:304
  25.0 17.2 %collective-permute-start = (bf16[8,128,256]{2,1,0:T(8,128)(2,1)S(1)}, bf16[8,128,256]{2,1,0:T(8,128)(2,1)S(1)}, u32[]{:S(2)}, u32[]{:S(2)}) collective-permute-start(bf16[8,128,256]{2,1,0:T(8,128)(2,1)S(1)} %all_to_all.40.r_own), channel_id=1, source_target_pairs={{0,8},{8,0},{1,9},{9,1},{2,10},{10,2},{3,11},{11,3},{4,12},{12,4},... | collective-permute-start | bytes 1572872 | tf_op jit(solution)/shard_map/ppermute | solution.py:320
  39.7 11.2 %collective-permute-start.1 = (bf16[8,128,256]{2,1,0:T(8,128)(2,1)S(1)}, bf16[8,128,256]{2,1,0:T(8,128)(2,1)S(1)}, u32[]{:S(2)}, u32[]{:S(2)}) collective-permute-start(bf16[8,128,256]{2,1,0:T(8,128)(2,1)S(1)} %all-to-all-done.1.c_own), channel_id=1, source_target_pairs={{0,128},{128,0},{1,129},{129,1},{2,130},{130,2},{3,131},{131,3},{4... | collective-permute-start | bytes 1572872 | tf_op jit(solution)/shard_map/ppermute | solution.py:318
  55.6 15.9 %all-to-all-start.2 = ((f32[16,24,128]{2,1,0:T(8,128)}), f32[16,24,128]{2,1,0:T(8,128)S(1)}, u32[]{:S(2)}, u32[]{:S(2)}) async-start(f32[16,24,128]{2,1,0:T(8,128)} %get-tuple-element.18), calls=%async_computation.2 | async-start | bytes 393216 | tf_op jit(solution)/shard_map/all_to_all | solution.py:304
  131.0 2.8 %collective-permute-start.2 = (f32[8,128,256]{2,1,0:T(8,128)S(1)}, f32[8,128,256]{2,1,0:T(8,128)S(1)}, u32[]{:S(2)}, u32[]{:S(2)}) collective-permute-start(f32[8,128,256]{2,1,0:T(8,128)S(1)} %get-tuple-element.29), channel_id=1, source_target_pairs={{0,8},{8,0},{1,9},{9,1},{2,10},{10,2},{3,11},{11,3},{4,12},{12,4},... | collective-permute-start | bytes 3145736 | tf_op jit(solution)/shard_map/ppermute | solution.py:353
  134.9 18.5 %all-to-all-start.7 = ((f32[8,128,256]{2,1,0:T(8,128)}), f32[8,128,256]{2,1,0:T(8,128)S(1)}, u32[]{:S(2)}, u32[]{:S(2)}) async-start(f32[8,128,256]{2,1,0:T(8,128)} %add.7), calls=%async_computation.7 | async-start | bytes 2097152 | tf_op jit(solution)/shard_map/all_to_all | solution.py:304

commit v2 on v1

--- a/solution.py
+++ b/solution.py
@@ -20,7 +20,6 @@
 
 AXES = ("xh", "z", "core", "xl", "y")
 ROW_GROUP = ("core", "xl", "y")
-COL_GROUP = ("xh", "z")
 
 VMEM_LIMIT = 32 * 1024 * 1024
 
@@ -176,58 +175,58 @@
     message_ref[...] = jnp.broadcast_to(rows[None], message_ref.shape)
 
 
-def first_rows(r_own, r_other, c_own, c_other, message, norms):
+def first_rows(r_own, r_other, c_own, c_other, message):
+    y_col = block_rows(c_own, c_other, 1)
+    send_all(message, peak_pass(y_col, r_own, r_other, 0, -norms_sub(y_col)))
+
+
+def first_self(r_own, r_other, c_own, c_other, sums, norms):
+    x_row = block_rows(r_own, r_other, 0)
+    y_row = block_rows(r_own, r_other, 1)
+    x_norm_col = norms_lane(block_rows(c_own, c_other, 0))
+    y_norm_col = norms_lane(block_rows(c_own, c_other, 1))
+    self_p = sum_pass(x_row, c_own, c_other, 0, -norms_sub(x_row), -x_norm_col)
+    self_q = sum_pass(y_row, c_own, c_other, 1, -norms_sub(y_row), -y_norm_col)
+    sums[...] = jnp.concatenate([self_p, self_q], axis=0)
+    norms[...] = jnp.concatenate(
+        [lane_to_dense(v) for v in (norms_lane(x_row), norms_lane(y_row), x_norm_col, y_norm_col)],
+        axis=0,
+    )
+
+
+def first_cols(place, r_own, r_other, c_own, c_other, sums, got, message, state):
+    u = LOG_COUNT - join_logs(got, place[0], 0)
+    x_row = block_rows(r_own, r_other, 0)
+    cross = peak_pass(x_row, c_own, c_other, 1, dense_to_sub(u))
+    send_all(message, jnp.concatenate([cross, sums[...]], axis=0))
+    state[...] = u
+
+
+def second_rows(place, r_own, r_other, c_own, c_other, norms, state, got, message, h_out):
+    far, spot = place[2], place[3]
+    h = LOG_COUNT - join_logs(got, far, 0)
+    p = LOG_COUNT - log2(join_sums(got, far, 8))
+    q = LOG_COUNT - log2(join_sums(got, far, 16))
     x_col = block_rows(c_own, c_other, 0)
     y_col = block_rows(c_own, c_other, 1)
-    x_norm_sub = norms_sub(x_col)
-    y_norm_sub = norms_sub(y_col)
-    x_norm = norms_lane(block_rows(r_own, r_other, 0))
-    y_norm = norms_lane(block_rows(r_own, r_other, 1))
-    cross = peak_pass(y_col, r_own, r_other, 0, -y_norm_sub)
-    self_p = sum_pass(x_col, r_own, r_other, 0, -x_norm_sub, -x_norm)
-    self_q = sum_pass(y_col, r_own, r_other, 1, -y_norm_sub, -y_norm)
-    send_all(message, jnp.concatenate([cross, self_p, self_q], axis=0))
-    x_norm_col = norms_lane(x_col)
-    y_norm_col = norms_lane(y_col)
-    norms[...] = jnp.concatenate(
-        [lane_to_dense(v) for v in (x_norm, y_norm, x_norm_col, y_norm_col)], axis=0
-    )
-
-
-def first_cols(place, r_own, r_other, c_own, c_other, got, message, state):
-    core, spot = place[0], place[1]
-    u = LOG_COUNT - join_logs(got, core, 0)
-    p = LOG_COUNT - log2(join_sums(got, core, 8))
-    q = LOG_COUNT - log2(join_sums(got, core, 16))
-    x_row = block_rows(r_own, r_other, 0)
-    cross = peak_pass(x_row, c_own, c_other, 1, dense_to_sub(u))
-    carry = pair_row(own_piece(p, spot), own_piece(q, spot))
-    send_all(message, jnp.concatenate([cross, jnp.broadcast_to(carry, (8, 128))], axis=0))
-    state[...] = jnp.concatenate([u, p, q], axis=0)
-
-
-def second_rows(place, r_own, r_other, c_own, c_other, norms, state, got, message, h_out):
-    far = place[2]
-    h = LOG_COUNT - join_logs(got, far, 0)
-    p_col, q_col = unpair(*piggy_rows(got, far, 8))
-    x_col = block_rows(c_own, c_other, 0)
-    y_col = block_rows(c_own, c_other, 1)
-    cross = sum_pass(y_col, r_own, r_other, 0, dense_to_sub(h), dense_to_lane(state[0:8, :]))
+    cross = sum_pass(y_col, r_own, r_other, 0, dense_to_sub(h), dense_to_lane(state[...]))
     self_p = sum_pass(
-        x_col, r_own, r_other, 0, dense_to_sub(p_col - norms[16:24, :]), -dense_to_lane(norms[0:8, :])
+        x_col, r_own, r_other, 0, dense_to_sub(p - norms[16:24, :]), -dense_to_lane(norms[0:8, :])
     )
     self_q = sum_pass(
-        y_col, r_own, r_other, 1, dense_to_sub(q_col - norms[24:32, :]), -dense_to_lane(norms[8:16, :])
-    )
-    send_all(message, jnp.concatenate([cross, self_p, self_q], axis=0))
+        y_col, r_own, r_other, 1, dense_to_sub(q - norms[24:32, :]), -dense_to_lane(norms[8:16, :])
+    )
+    carry = jnp.broadcast_to(pair_row(own_piece(p, spot), own_piece(q, spot)), (8, 128))
+    send_all(message, jnp.concatenate([cross, self_p, self_q, carry], axis=0))
     h_out[...] = h
 
 
 def second_cols(place, r_own, r_other, c_own, c_other, norms, state, h_in, got, message, shifts):
     core, spot = place[0], place[1]
-    u = state[0:8, :] + (LOG_COUNT - log2(join_sums(got, core, 0)))
-    p = 0.5 * (state[8:16, :] + (LOG_COUNT - log2(join_sums(got, core, 8))))
-    q = 0.5 * (state[16:24, :] + (LOG_COUNT - log2(join_sums(got, core, 16))))
+    p_first, q_first = unpair(*piggy_rows(got, core, 24))
+    u = state[...] + (LOG_COUNT - log2(join_sums(got, core, 0)))
+    p = 0.5 * (p_first + (LOG_COUNT - log2(join_sums(got, core, 8))))
+    q = 0.5 * (q_first + (LOG_COUNT - log2(join_sums(got, core, 16))))
     pt = p - norms[0:8, :]
     qt = q - norms[8:16, :]
     x_row = block_rows(r_own, r_other, 0)
@@ -251,42 +250,46 @@
     total[...] = jnp.sum(got[:, 8:16, :], axis=0)
 
 
-def gradients(place, r_own, r_other, c_own, c_other, shifts, cols, total, got, kept, sent, divergence):
-    core = place[0]
-    h_row, unused = unpair(*piggy_rows(got, core, 0))
+def weights(rows, columns, sub, lane):
+    products = dot_nt(rows, columns)
+    values = jnp.exp2(products * BETA + widen(sub, BLOCK) + lane)
+    mass = jnp.sum(values, axis=1, keepdims=True)
+    mixed = jnp.dot(values.astype(jnp.bfloat16), columns, preferred_element_type=jnp.float32)
+    return mass, mixed
+
+
+def gradient_half(ref, which, part, cross, self_):
+    rows = half_rows(ref, which)
+    cross_mass, cross_mixed = weights(rows, cross[0], cross[1][part], cross[2])
+    self_mass, self_mixed = weights(rows, self_[0], self_[1][part], self_[2])
+    grad = rows.astype(jnp.float32) * (cross_mass - self_mass) - cross_mixed + self_mixed
+    return grad.reshape(8, OWN, WIDTH)
+
+
+def col_lane(cols, k):
+    return dense_to_lane(cols[8 * k : 8 * k + 8, :]) - LOG_COUNT
+
+
+def region_gradients(r_own, r_other, c_own, c_other, shifts, cols, kept, sent):
+    cross = (block_rows(c_own, c_other, 1), dense_to_sub(shifts[0:8, :]), col_lane(cols, 0))
+    self_ = (block_rows(c_own, c_other, 0), dense_to_sub(shifts[8:16, :]), col_lane(cols, 2))
+    sent[...] = gradient_half(r_other, 0, slice(HALF, BLOCK), cross, self_)
+    kept[...] = gradient_half(r_own, 0, slice(0, HALF), cross, self_)
+
+
+def phrase_gradients(
+    place, r_own, r_other, c_own, c_other, shifts, cols, total, got, kept, sent, divergence
+):
+    h_row, unused = unpair(*piggy_rows(got, place[0], 0))
     summed = total[...] + jnp.sum(got[...], axis=0)
     divergence[...] = summed * (1.0 / (POINTS * BETA))
-    u_sub = dense_to_sub(shifts[0:8, :])
-    p_sub = dense_to_sub(shifts[8:16, :])
-    q_sub = dense_to_sub(shifts[16:24, :])
-    h_sub = dense_to_sub(h_row)
-    h_lane, u_lane, p_lane, q_lane = [
-        dense_to_lane(cols[8 * k : 8 * k + 8, :]) - LOG_COUNT for k in range(4)
-    ]
-    x_col = block_rows(c_own, c_other, 0)
-    y_col = block_rows(c_own, c_other, 1)
-
-    def weights(rows, columns, sub, lane):
-        products = dot_nt(rows, columns)
-        values = jnp.exp2(products * BETA + widen(sub, BLOCK) + lane)
-        mass = jnp.sum(values, axis=1, keepdims=True)
-        mixed = jnp.dot(values.astype(jnp.bfloat16), columns, preferred_element_type=jnp.float32)
-        return mass, mixed
-
-    for ref, out, start in ((r_other, sent, HALF), (r_own, kept, 0)):
-        part = slice(start, start + HALF)
-        for which, cross_col, self_col, cross_sub, self_sub, cross_lane, self_lane in (
-            (0, y_col, x_col, u_sub, p_sub, h_lane, p_lane),
-            (1, x_col, y_col, h_sub, q_sub, u_lane, q_lane),
-        ):
-            rows = half_rows(ref, which)
-            cross_mass, cross_mixed = weights(rows, cross_col, cross_sub[part], cross_lane)
-            self_mass, self_mixed = weights(rows, self_col, self_sub[part], self_lane)
-            grad = rows.astype(jnp.float32) * (cross_mass - self_mass) - cross_mixed + self_mixed
-            out[:, which * OWN : (which + 1) * OWN, :] = grad.reshape(8, OWN, WIDTH).astype(out.dtype)
-
-
-def call(body, outs, smem, *args):
+    cross = (block_rows(c_own, c_other, 0), dense_to_sub(h_row), col_lane(cols, 1))
+    self_ = (block_rows(c_own, c_other, 1), dense_to_sub(shifts[16:24, :]), col_lane(cols, 3))
+    sent[...] = gradient_half(r_other, 1, slice(HALF, BLOCK), cross, self_)
+    kept[...] = gradient_half(r_own, 1, slice(0, HALF), cross, self_)
+
+
+def call(body, outs, smem, passes, *args):
     shapes = [jax.ShapeDtypeStruct(shape, dtype) for shape, dtype in outs]
     specs = [pl.BlockSpec(memory_space=pltpu.VMEM)] * len(args)
     if smem:
@@ -297,11 +300,27 @@
         in_specs=specs,
         out_specs=[pl.BlockSpec(memory_space=pltpu.VMEM)] * len(outs),
         compiler_params=pltpu.CompilerParams(vmem_limit_bytes=VMEM_LIMIT),
+        cost_estimate=pl.CostEstimate(
+            flops=passes * 2 * BLOCK * BLOCK * WIDTH,
+            bytes_accessed=4 * BLOCK * WIDTH * 2,
+            transcendentals=passes * BLOCK * BLOCK,
+        ),
     )(*args)
 
 
-def share(message, axes):
-    return lax.all_to_all(message, axes, 0, 0, tiled=True)
+def share(message, axes, groups=None):
+    return lax.all_to_all(message, axes, 0, 0, tiled=True, axis_index_groups=groups)
+
+
+def share_col(message):
+    groups = [
+        [far * 16 + z * 2 + (side ^ far) for far in range(2) for z in range(8)] for side in range(2)
+    ]
+    return share(message, ("xh", "z", "xl"), groups)
+
+
+def core_swap(values):
+    return lax.ppermute(values, "core", [(0, 1), (1, 0)])
 
 
 def on_device(regions, phrases):
@@ -315,34 +334,52 @@
     own = jnp.concatenate([regions, phrases], axis=0)
     copies = jnp.broadcast_to(own[None], (8, 2 * OWN, WIDTH))
     c_own = share(copies, ("z",))
-    c_other = lax.ppermute(c_own, "xh", [(0, 1), (1, 0)])
+    c_own, copies = lax.optimization_barrier((c_own, copies))
+    c_other = lax.ppermute(c_own, ("xh", "xl"), [(0, 3), (1, 2), (2, 1), (3, 0)])
     r_own = share(copies, ("xl", "y"))
-    r_other = lax.ppermute(r_own, "core", [(0, 1), (1, 0)])
+    r_other = core_swap(r_own)
     points = (r_own, r_other, c_own, c_other)
 
     def message(rows):
         return ((16, rows, 128), f32)
 
-    sent, norms = call(first_rows, [message(24), ((32, 128), f32)], False, *points)
+    (sent,) = call(first_rows, [message(8)], False, 1, *points)
+    later, sent = lax.optimization_barrier((points, sent))
     got = share(sent, ROW_GROUP)
-    sent, state = call(first_cols, [message(16), ((24, 128), f32)], True, place, *points, got)
-    got = share(sent, COL_GROUP)
+    sums, norms = call(first_self, [((16, 128), f32), ((32, 128), f32)], False, 2, *later)
+    sent, state = call(
+        first_cols, [message(24), ((8, 128), f32)], True, 1, place, *points, sums, got
+    )
+    got = share_col(sent)
     sent, h_first = call(
-        second_rows, [message(24), ((8, 128), f32)], True, place, *points, norms, state, got
+        second_rows, [message(32), ((8, 128), f32)], True, 3, place, *points, norms, state, got
     )
     got = share(sent, ROW_GROUP)
     sent, shifts = call(
-        second_cols, [message(16), ((24, 128), f32)], True, place, *points, norms, state, h_first, got
-    )
-    got = share(sent, COL_GROUP)
+        second_cols,
+        [message(16), ((24, 128), f32)],
+        True,
+        1,
+        place,
+        *points,
+        norms,
+        state,
+        h_first,
+        got,
+    )
+    got = share_col(sent)
     sent, cols, total = call(
-        last_cols, [message(8), ((32, 128), f32), ((8, 128), f32)], True, place, h_first, got
+        last_cols, [message(8), ((32, 128), f32), ((8, 128), f32)], True, 0, place, h_first, got
     )
     got = share(sent, ROW_GROUP)
-    kept, away, divergence = call(
-        gradients,
-        [((8, 2 * OWN, WIDTH), f32), ((8, 2 * OWN, WIDTH), f32), ((8, 128), f32)],
+    half = ((8, OWN, WIDTH), f32)
+    x_kept, x_away = call(region_gradients, [half, half], False, 4, *points, shifts, cols)
+    x_back = core_swap(x_away)
+    y_kept, y_away, divergence = call(
+        phrase_gradients,
+        [half, half, ((8, 128), f32)],
         True,
+        4,
         place,
         *points,
         shifts,
@@ -350,8 +387,10 @@
         total,
         got,
     )
-    joined = kept + lax.ppermute(away, "core", [(0, 1), (1, 0)])
-    summed = jnp.sum(share(joined, ("xl", "y")), axis=0)
+    y_back = core_swap(y_away)
+    joined = jnp.concatenate([x_kept + x_back, y_kept + y_back], axis=1).astype(jnp.bfloat16)
+    parts = share(joined, ("xl", "y")).astype(f32)
+    summed = jnp.sum(parts, axis=0)
     return (summed[0:OWN], summed[OWN : 2 * OWN], divergence[2, 0])
 
 

time: 155 us -> 138 us (0.89)
  waiting for transfers between devices: 44.4 us -> 20 us
  starting transfers between devices: 26.2 us -> 29 us
  blocking collectives: 61.5 us -> 63.4 us
  Pallas kernels: 17.2 us -> 18.8 us
    all_to_all x3 -> x4, waiting for transfers between devices: 33.4 us -> 18.1 us  [share(): lax.all_to_all(message, axes, 0, 0, tiled=True, axis_index_groups=groups)]
    ppermute x3 -> x4, waiting for transfers between devices: 11 us -> 1.88 us  [the longest x3 1.03 us: core_swap(): return lax.ppermute(values, 'core', [(0, 1), (1, 0)])]
    all_to_all x5 -> x4, blocking collectives: 61.5 us -> 63.4 us  [share(): lax.all_to_all(message, axes, 0, 0, tiled=True, axis_index_groups=groups)]
    ppermute x3 -> x4, starting transfers between devices: 5.61 us -> 7.35 us  [the longest x3 4.62 us: core_swap(): return lax.ppermute(values, 'core', [(0, 1), (1, 0)])]
    pallas_call x6 -> x8, Pallas kernels: 17.2 us -> 18.8 us  [call(): pl.pallas_call(body, out_shape=shapes, in_specs=specs, out_specs=[pl.Bloc...]
    all_to_all x3 -> x4, starting transfers between devices: 20.6 us -> 21.6 us  [share(): lax.all_to_all(message, axes, 0, 0, tiled=True, axis_index_groups=groups)]
  transfers between devices with their start and end apart: 6 -> 8, of which waited for: 5 -> 7; matrix products, arithmetic and copies ran while one was open for 0% -> 1% of each run, Pallas kernels for 0% -> 6%
where the time goes in v2:
time: 138 us; the launch traced here: 137 us
  blocking collectives  63.4 us (46%)
  starting transfers between devices  29 us (21%)
  waiting for transfers between devices  20 us (14%)
  Pallas kernels  18.8 us (14%)
  other arithmetic  2.95 us (2%)
  local copies, waits for them, and re-layouts  2 us (1%)
    all_to_all x4, blocking collectives, share(): lax.all_to_all(message, axes, 0, 0, tiled=True, axis_index_groups=groups)  63.4 us
    all_to_all x4, starting transfers between devices, share(): lax.all_to_all(message, axes, 0, 0, tiled=True, axis_index_groups=groups)  21.6 us
    pallas_call x8, Pallas kernels, call(): pl.pallas_call(body, out_shape=shapes, in_specs=specs, out_specs=[pl.Bloc...  18.8 us
    all_to_all x4, waiting for transfers between devices, share(): lax.all_to_all(message, axes, 0, 0, tiled=True, axis_index_groups=groups)  18.1 us
    ppermute x3, starting transfers between devices, core_swap(): return lax.ppermute(values, 'core', [(0, 1), (1, 0)])  4.62 us
  transfers between devices with their start and end apart: 8, of which 7 were waited for; matrix products, arithmetic and copies ran while one was open for 1% of the time, Pallas kernels for 6%

profile of v2, /device:TPU:1, one launch (start us, length us, event | category | flops | bytes accessed | tf_op | source)
XLA Modules:
  0.0 136.8 jit_solution(604034370522850195)
XLA Ops:
  2.2 25.0 %all_to_all.40.c_own = bf16[8,128,256]{2,1,0:T(8,128)(2,1)S(1)} all-to-all(bf16[8,128,256]{2,1,0:T(8,128)(2,1)} %broadcast_in_dim.2), channel_id=1, replica_groups=mesh['xh'=2,'z'=8,'core'=2,'xl'=2,'y'=4] {'z'}, dimensions={0} | all-to-all | bytes 1048576 | tf_op jit(solution)/shard_map/all_to_all | solution.py:312
  27.2 5.1 %all-to-all-start.1 = ((bf16[8,128,256]{2,1,0:T(8,128)(2,1)}), bf16[8,128,256]{2,1,0:T(8,128)(2,1)S(1)}, u32[]{:S(2)}, u32[]{:S(2)}) async-start(bf16[8,128,256]{2,1,0:T(8,128)(2,1)} %broadcast_in_dim.2), calls=%async_computation.1 | async-start | bytes 1048576 | tf_op jit(solution)/shard_map/all_to_all | solution.py:312
  32.4 2.7 %collective-permute-start.1 = (bf16[8,128,256]{2,1,0:T(8,128)(2,1)S(1)}, bf16[8,128,256]{2,1,0:T(8,128)(2,1)S(1)}, u32[]{:S(2)}, u32[]{:S(2)}) collective-permute-start(bf16[8,128,256]{2,1,0:T(8,128)(2,1)S(1)} %all_to_all.40.c_own), channel_id=1, source_target_pairs={{0,132},{4,128},{128,4},{132,0},{1,133},{5,129},{129,5},{133,1},{2... | collective-permute-start | bytes 1572872 | tf_op jit(solution)/shard_map/ppermute | solution.py:338
  35.1 4.4 %all-to-all-done.1.r_own = bf16[8,128,256]{2,1,0:T(8,128)(2,1)S(1)} async-done(((bf16[8,128,256]{2,1,0:T(8,128)(2,1)}), bf16[8,128,256]{2,1,0:T(8,128)(2,1)S(1)}, u32[]{:S(2)}, u32[]{:S(2)}) %all-to-all-start.1) | async-done | bytes 524320 | tf_op jit(solution)/shard_map/all_to_all | solution.py:312
  39.5 3.9 %collective-permute-start = (bf16[8,128,256]{2,1,0:T(8,128)(2,1)S(1)}, bf16[8,128,256]{2,1,0:T(8,128)(2,1)S(1)}, u32[]{:S(2)}, u32[]{:S(2)}) collective-permute-start(bf16[8,128,256]{2,1,0:T(8,128)(2,1)S(1)} %all-to-all-done.1.r_own), channel_id=1, source_target_pairs={{0,8},{8,0},{1,9},{9,1},{2,10},{10,2},{3,11},{11,3},{4,12},{12,4},... | collective-permute-start | bytes 1572872 | tf_op jit(solution)/shard_map/ppermute | solution.py:323
  43.5 0.9 collective-permute-done.1.c_other
  44.9 2.3 %shard_map.49 = f32[16,8,128]{2,1,0:T(8,128)} custom-call(bf16[8,128,256]{2,1,0:T(8,128)(2,1)S(1)} %all-to-all-done.1.r_own, bf16[8,128,256]{2,1,0:T(8,128)(2,1)S(1)} %collective-permute-done.r_other, bf16[8,128,256]{2,1,0:T(8,128)(2,1)S(1)} %all_to_all.40.c_own, bf16[8,128,256]{2,1,0:T(8,128)(2,1)S(1)} %collective-permute-done.1.c_other), custom_call_target="tpu_custom_call" | custom-call | flops 536870912 | bytes 2097152 | tf_op jit(solution)/shard_map/pallas_call | solution.py:297
  47.2 7.5 %all-to-all-start.2 = ((f32[16,8,128]{2,1,0:T(8,128)}), f32[16,8,128]{2,1,0:T(8,128)S(1)}, u32[]{:S(2)}, u32[]{:S(2)}) async-start(f32[16,8,128]{2,1,0:T(8,128)} %shard_map.49), calls=%async_computation.2 | async-start | bytes 131072 | tf_op jit(solution)/shard_map/all_to_all | solution.py:312
  54.8 3.1 %shard_map.50 = (f32[16,128]{1,0:T(8,128)S(1)}, f32[32,128]{1,0:T(8,128)S(1)}) custom-call(bf16[8,128,256]{2,1,0:T(8,128)(2,1)S(1)} %all-to-all-done.1.r_own, bf16[8,128,256]{2,1,0:T(8,128)(2,1)S(1)} %collective-permute-done.r_other, bf16[8,128,256]{2,1,0:T(8,128)(2,1)S(1)} %all_to_all.40.c_own, bf16[8,128,256]{2,1,0:T(8,128)(2,1)S(1)} %collective-permute-done.1.c_other), custom_call_target="tpu_custom_call" | custom-call | flops 1073741824 | bytes 2097152 | tf_op jit(solution)/shard_map/pallas_call | solution.py:297
  57.9 2.7 %all-to-all-done.2.got = f32[16,8,128]{2,1,0:T(8,128)S(1)} async-done(((f32[16,8,128]{2,1,0:T(8,128)}), f32[16,8,128]{2,1,0:T(8,128)S(1)}, u32[]{:S(2)}, u32[]{:S(2)}) %all-to-all-start.2) | async-done | bytes 65568 | tf_op jit(solution)/shard_map/all_to_all | solution.py:312
  60.6 2.0 %shard_map.51 = (f32[16,24,128]{2,1,0:T(8,128)S(1)}, f32[8,128]{1,0:T(8,128)S(1)}) custom-call(s32[4]{0:T(128)S(1)} %pad_add_fusion.place, bf16[8,128,256]{2,1,0:T(8,128)(2,1)S(1)} %all-to-all-done.1.r_own, bf16[8,128,256]{2,1,0:T(8,128)(2,1)S(1)} %collective-permute-done.r_other, bf16[8,128,256]{2,1,0:T(8,128)(2,1)S(1)} %all_to_all.40.c_own, ...), custom_call_target="tpu_custom_call" | custom-call | flops 536870912 | bytes 2097152 | tf_op jit(solution)/shard_map/pallas_call | solution.py:297
  62.6 13.4 %all_to_all.41.got = f32[16,24,128]{2,1,0:T(8,128)S(1)} all-to-all(f32[16,24,128]{2,1,0:T(8,128)S(1)} %get-tuple-element.36), channel_id=1, replica_groups={{0,16,32,48,64,80,96,112,132,148,164,180,196,212,228,244},{4,20,36,52,6..., dimensions={0} | all-to-all | bytes 393216 | tf_op jit(solution)/shard_map/all_to_all | solution.py:312
  76.1 2.9 %shard_map.52 = (f32[16,32,128]{2,1,0:T(8,128)S(1)}, f32[8,128]{1,0:T(8,128)S(1)}) custom-call(s32[4]{0:T(128)S(1)} %pad_add_fusion.place, bf16[8,128,256]{2,1,0:T(8,128)(2,1)S(1)} %all-to-all-done.1.r_own, bf16[8,128,256]{2,1,0:T(8,128)(2,1)S(1)} %collective-permute-done.r_other, bf16[8,128,256]{2,1,0:T(8,128)(2,1)S(1)} %all_to_all.40.c_own, ...), custom_call_target="tpu_custom_call" | custom-call | flops 1610612736 | bytes 2097152 | tf_op jit(solution)/shard_map/pallas_call | solution.py:297
  79.0 12.7 %all_to_all.42.got = f32[16,32,128]{2,1,0:T(8,128)S(1)} all-to-all(f32[16,32,128]{2,1,0:T(8,128)S(1)} %get-tuple-element.38), channel_id=1, replica_groups=mesh['xh'=2,'z'=8,'core'=2,'xl'=2,'y'=4] {'core','xl','y'}, dimensions={0} | all-to-all | bytes 524288 | tf_op jit(solution)/shard_map/all_to_all | solution.py:312
  91.7 1.5 %shard_map.53 = (f32[16,16,128]{2,1,0:T(8,128)S(1)}, f32[24,128]{1,0:T(8,128)S(1)}) custom-call(s32[4]{0:T(128)S(1)} %pad_add_fusion.place, bf16[8,128,256]{2,1,0:T(8,128)(2,1)S(1)} %all-to-all-done.1.r_own, bf16[8,128,256]{2,1,0:T(8,128)(2,1)S(1)} %collective-permute-done.r_other, bf16[8,128,256]{2,1,0:T(8,128)(2,1)S(1)} %all_to_all.40.c_own, ...), custom_call_target="tpu_custom_call" | custom-call | flops 536870912 | bytes 2097152 | tf_op jit(solution)/shard_map/pallas_call | solution.py:297
  93.2 12.3 %all_to_all.43.got = f32[16,16,128]{2,1,0:T(8,128)S(1)} all-to-all(f32[16,16,128]{2,1,0:T(8,128)S(1)} %get-tuple-element.40), channel_id=1, replica_groups={{0,16,32,48,64,80,96,112,132,148,164,180,196,212,228,244},{4,20,36,52,6..., dimensions={0} | all-to-all | bytes 262144 | tf_op jit(solution)/shard_map/all_to_all | solution.py:312
  105.5 1.3 shard_map.54
  106.8 5.5 %all-to-all-start.6 = ((f32[16,8,128]{2,1,0:T(8,128)}), f32[16,8,128]{2,1,0:T(8,128)S(1)}, u32[]{:S(2)}, u32[]{:S(2)}) async-start(f32[16,8,128]{2,1,0:T(8,128)} %get-tuple-element.45), calls=%async_computation.6 | async-start | bytes 131072 | tf_op jit(solution)/shard_map/all_to_all | solution.py:312
  112.3 2.5 %shard_map.55 = (f32[8,64,256]{2,1,0:T(8,128)S(1)}, f32[8,64,256]{2,1,0:T(8,128)S(1)}) custom-call(bf16[8,128,256]{2,1,0:T(8,128)(2,1)S(1)} %all-to-all-done.1.r_own, bf16[8,128,256]{2,1,0:T(8,128)(2,1)S(1)} %collective-permute-done.r_other, bf16[8,128,256]{2,1,0:T(8,128)(2,1)S(1)} %all_to_all.40.c_own, ...), custom_call_target="tpu_custom_call" | custom-call | flops 2147483648 | bytes 2097152 | tf_op jit(solution)/shard_map/pallas_call | solution.py:297
  115.1 3.1 %all-to-all-done.6.got = f32[16,8,128]{2,1,0:T(8,128)S(1)} async-done(((f32[16,8,128]{2,1,0:T(8,128)}), f32[16,8,128]{2,1,0:T(8,128)S(1)}, u32[]{:S(2)}, u32[]{:S(2)}) %all-to-all-start.6) | async-done | bytes 65568 | tf_op jit(solution)/shard_map/all_to_all | solution.py:312
  118.2 3.1 %shard_map.56 = (f32[8,64,256]{2,1,0:T(8,128)S(1)}, f32[8,64,256]{2,1,0:T(8,128)S(1)}, f32[8,128]{1,0:T(8,128)S(1)}) custom-call(s32[4]{0:T(128)S(1)} %pad_add_fusion.place, bf16[8,128,256]{2,1,0:T(8,128)(2,1)S(1)} %all-to-all-done.1.r_own, bf16[8,128,256]{2,1,0:T(8,128)(2,1)S(1)} %collective-permute-done.r_other, ...), custom_call_target="tpu_custom_call" | custom-call | flops 2147483648 | bytes 2097152 | tf_op jit(solution)/shard_map/pallas_call | solution.py:297
  121.7 1.1 add_convert_fusion.1
  124.2 3.5 %all-to-all-start.7 = ((bf16[8,128,256]{2,1,0:T(8,128)(2,1)}), bf16[8,128,256]{2,1,0:T(8,128)(2,1)S(1)}, u32[]{:S(2)}, u32[]{:S(2)}) async-start(bf16[8,128,256]{2,1,0:T(8,128)(2,1)} %pad_maximum_fusion), calls=%async_computation.7 | async-start | bytes 1048576 | tf_op jit(solution)/shard_map/all_to_all | solution.py:312
  128.2 7.9 %all-to-all-done.7 = bf16[8,128,256]{2,1,0:T(8,128)(2,1)S(1)} async-done(((bf16[8,128,256]{2,1,0:T(8,128)(2,1)}), bf16[8,128,256]{2,1,0:T(8,128)(2,1)S(1)}, u32[]{:S(2)}, u32[]{:S(2)}) %all-to-all-start.7) | async-done | bytes 524320 | tf_op jit(solution)/shard_map/all_to_all | solution.py:312
  (13 shorter events, 5.6 us)
Async XLA Ops:
  27.2 12.3 %all-to-all-start.1 = ((bf16[8,128,256]{2,1,0:T(8,128)(2,1)}), bf16[8,128,256]{2,1,0:T(8,128)(2,1)S(1)}, u32[]{:S(2)}, u32[]{:S(2)}) async-start(bf16[8,128,256]{2,1,0:T(8,128)(2,1)} %broadcast_in_dim.2), calls=%async_computation.1 | async-start | bytes 1048576 | tf_op jit(solution)/shard_map/all_to_all | solution.py:312
  32.4 11.9 %collective-permute-start.1 = (bf16[8,128,256]{2,1,0:T(8,128)(2,1)S(1)}, bf16[8,128,256]{2,1,0:T(8,128)(2,1)S(1)}, u32[]{:S(2)}, u32[]{:S(2)}) collective-permute-start(bf16[8,128,256]{2,1,0:T(8,128)(2,1)S(1)} %all_to_all.40.c_own), channel_id=1, source_target_pairs={{0,132},{4,128},{128,4},{132,0},{1,133},{5,129},{129,5},{133,1},{2... | collective-permute-start | bytes 1572872 | tf_op jit(solution)/shard_map/ppermute | solution.py:338
  39.5 5.4 %collective-permute-start = (bf16[8,128,256]{2,1,0:T(8,128)(2,1)S(1)}, bf16[8,128,256]{2,1,0:T(8,128)(2,1)S(1)}, u32[]{:S(2)}, u32[]{:S(2)}) collective-permute-start(bf16[8,128,256]{2,1,0:T(8,128)(2,1)S(1)} %all-to-all-done.1.r_own), channel_id=1, source_target_pairs={{0,8},{8,0},{1,9},{9,1},{2,10},{10,2},{3,11},{11,3},{4,12},{12,4},... | collective-permute-start | bytes 1572872 | tf_op jit(solution)/shard_map/ppermute | solution.py:323
  47.2 13.4 %all-to-all-start.2 = ((f32[16,8,128]{2,1,0:T(8,128)}), f32[16,8,128]{2,1,0:T(8,128)S(1)}, u32[]{:S(2)}, u32[]{:S(2)}) async-start(f32[16,8,128]{2,1,0:T(8,128)} %shard_map.49), calls=%async_computation.2 | async-start | bytes 131072 | tf_op jit(solution)/shard_map/all_to_all | solution.py:312
  106.8 11.3 %all-to-all-start.6 = ((f32[16,8,128]{2,1,0:T(8,128)}), f32[16,8,128]{2,1,0:T(8,128)S(1)}, u32[]{:S(2)}, u32[]{:S(2)}) async-start(f32[16,8,128]{2,1,0:T(8,128)} %get-tuple-element.45), calls=%async_computation.6 | async-start | bytes 131072 | tf_op jit(solution)/shard_map/all_to_all | solution.py:312
  114.9 6.9 %collective-permute-start.2 = (f32[8,64,256]{2,1,0:T(8,128)S(1)}, f32[8,64,256]{2,1,0:T(8,128)}, u32[]{:S(2)}, u32[]{:S(2)}) collective-permute-start(f32[8,64,256]{2,1,0:T(8,128)S(1)} %get-tuple-element.43), channel_id=1, source_target_pairs={{0,8},{8,0},{1,9},{9,1},{2,10},{10,2},{3,11},{11,3},{4,12},{12,4},... | collective-permute-start | bytes 1572872 | tf_op jit(solution)/shard_map/ppermute | solution.py:323
  121.3 2.0 %collective-permute-start.3 = (f32[8,64,256]{2,1,0:T(8,128)S(1)}, f32[8,64,256]{2,1,0:T(8,128)S(1)}, u32[]{:S(2)}, u32[]{:S(2)}) collective-permute-start(f32[8,64,256]{2,1,0:T(8,128)S(1)} %get-tuple-element.47), channel_id=1, source_target_pairs={{0,8},{8,0},{1,9},{9,1},{2,10},{10,2},{3,11},{11,3},{4,12},{12,4},... | collective-permute-start | bytes 1572872 | tf_op jit(solution)/shard_map/ppermute | solution.py:323
  124.2 11.9 %all-to-all-start.7 = ((bf16[8,128,256]{2,1,0:T(8,128)(2,1)}), bf16[8,128,256]{2,1,0:T(8,128)(2,1)S(1)}, u32[]{:S(2)}, u32[]{:S(2)}) async-start(bf16[8,128,256]{2,1,0:T(8,128)(2,1)} %pad_maximum_fusion), calls=%async_computation.7 | async-start | bytes 1048576 | tf_op jit(solution)/shard_map/all_to_all | solution.py:312

commit v3 on v2

--- a/solution.py
+++ b/solution.py
@@ -21,7 +21,7 @@
 AXES = ("xh", "z", "core", "xl", "y")
 ROW_GROUP = ("core", "xl", "y")
 
-VMEM_LIMIT = 32 * 1024 * 1024
+VMEM_LIMIT = 20 * 1024 * 1024
 
 
 def log2(values):
@@ -141,7 +141,7 @@
 
 def own_piece(dense, place):
     row = jnp.zeros((1, 128), jnp.float32)
-    for k in range(4):
+    for k in range(8):
         row = jnp.where(place // 2 == k, dense[k : k + 1, :], row)
     return jnp.where(place % 2 == 0, row, pltpu.roll(row, 64, 1))
 
@@ -150,7 +150,7 @@
     return jnp.where(lane_index() < 64, first, pltpu.roll(second, 64, 1))
 
 
-def piggy_rows(ref, place, row):
+def piggy_rows(ref, row, place):
     order = []
     for base in (place * 8, (1 - place) * 8):
         for k in range(8):
@@ -175,12 +175,29 @@
     message_ref[...] = jnp.broadcast_to(rows[None], message_ref.shape)
 
 
-def first_rows(r_own, r_other, c_own, c_other, message):
-    y_col = block_rows(c_own, c_other, 1)
-    send_all(message, peak_pass(y_col, r_own, r_other, 0, -norms_sub(y_col)))
-
-
-def first_self(r_own, r_other, c_own, c_other, sums, norms):
+def first_half(place, near, across, near_far, across_far, c_own, r_own, r_other, partial):
+    side, spot = place[1] // 4, place[1] % 4
+    for step in range(4):
+        source = lax.rem(spot + 4 - step, 4)
+        r_own[pl.ds(side * 4 + source, 1)] = near[step : step + 1]
+        r_other[pl.ds(side * 4 + source, 1)] = near_far[step : step + 1]
+        r_own[pl.ds((1 - side) * 4 + source, 1)] = across[step : step + 1]
+        r_other[pl.ds((1 - side) * 4 + source, 1)] = across_far[step : step + 1]
+    y_col = half_rows(c_own, 1)
+    partial[...] = peak_pass(y_col, r_own, r_other, 0, -norms_sub(y_col))
+
+
+def first_rows(r_own, r_other, c_phrases, partial, message):
+    y_col = c_phrases[...].reshape(HALF, WIDTH)
+    rest = peak_pass(y_col, r_own, r_other, 0, -norms_sub(y_col))
+    peak = jnp.maximum(rest, partial[...])
+    mass = jnp.exp2(rest - peak) + jnp.exp2(partial[...] - peak)
+    send_all(message, peak + log2(mass))
+
+
+def first_self(r_own, r_other, c_own, c_phrases, c_regions, sums, norms, c_other):
+    c_other[:, 0:OWN, :] = c_regions[...]
+    c_other[:, OWN : 2 * OWN, :] = c_phrases[...]
     x_row = block_rows(r_own, r_other, 0)
     y_row = block_rows(r_own, r_other, 1)
     x_norm_col = norms_lane(block_rows(c_own, c_other, 0))
@@ -203,10 +220,10 @@
 
 
 def second_rows(place, r_own, r_other, c_own, c_other, norms, state, got, message, h_out):
-    far, spot = place[2], place[3]
-    h = LOG_COUNT - join_logs(got, far, 0)
-    p = LOG_COUNT - log2(join_sums(got, far, 8))
-    q = LOG_COUNT - log2(join_sums(got, far, 16))
+    spot = place[2]
+    h = LOG_COUNT - join_logs(got, place[3], 0)
+    p = LOG_COUNT - log2(join_sums(got, place[3], 8))
+    q = LOG_COUNT - log2(join_sums(got, place[3], 16))
     x_col = block_rows(c_own, c_other, 0)
     y_col = block_rows(c_own, c_other, 1)
     cross = sum_pass(y_col, r_own, r_other, 0, dense_to_sub(h), dense_to_lane(state[...]))
@@ -223,7 +240,7 @@
 
 def second_cols(place, r_own, r_other, c_own, c_other, norms, state, h_in, got, message, shifts):
     core, spot = place[0], place[1]
-    p_first, q_first = unpair(*piggy_rows(got, core, 24))
+    p_first, q_first = unpair(*piggy_rows(got, 24, core))
     u = state[...] + (LOG_COUNT - log2(join_sums(got, core, 0)))
     p = 0.5 * (p_first + (LOG_COUNT - log2(join_sums(got, core, 8))))
     q = 0.5 * (q_first + (LOG_COUNT - log2(join_sums(got, core, 16))))
@@ -239,11 +256,10 @@
 
 
 def last_cols(place, h_in, got, message, cols, total):
-    far, spot = place[2], place[3]
-    h = h_in[...] + (LOG_COUNT - log2(join_sums(got, far, 0)))
-    u_col, p_col = unpair(*piggy_rows(got, far, 8))
-    q_col, unused = unpair(*piggy_rows(got, far, 9))
-    piece = own_piece(h, spot)
+    h = h_in[...] + (LOG_COUNT - log2(join_sums(got, place[3], 0)))
+    u_col, p_col = unpair(*piggy_rows(got, 8, place[3]))
+    q_col, unused = unpair(*piggy_rows(got, 9, place[3]))
+    piece = own_piece(h, place[2])
     part = jnp.broadcast_to(canonical_sum(h), (7, 128))
     send_all(message, jnp.concatenate([piece, part], axis=0))
     cols[...] = jnp.concatenate([h, u_col, p_col, q_col], axis=0)
@@ -258,35 +274,45 @@
     return mass, mixed
 
 
-def gradient_half(ref, which, part, cross, self_):
-    rows = half_rows(ref, which)
-    cross_mass, cross_mixed = weights(rows, cross[0], cross[1][part], cross[2])
-    self_mass, self_mixed = weights(rows, self_[0], self_[1][part], self_[2])
-    grad = rows.astype(jnp.float32) * (cross_mass - self_mass) - cross_mixed + self_mixed
-    return grad.reshape(8, OWN, WIDTH)
+def term(rows, part, columns, sub, lane):
+    mass, mixed = weights(rows, columns, sub[part], lane)
+    return (rows.astype(jnp.float32) * mass - mixed).reshape(8, OWN, WIDTH)
+
+
+SECOND = slice(HALF, BLOCK)
+FIRST = slice(0, HALF)
 
 
 def col_lane(cols, k):
     return dense_to_lane(cols[8 * k : 8 * k + 8, :]) - LOG_COUNT
+
+
+def gradient(rows, part, cross, self_):
+    return term(rows, part, *cross) - term(rows, part, *self_)
 
 
 def region_gradients(r_own, r_other, c_own, c_other, shifts, cols, kept, sent):
     cross = (block_rows(c_own, c_other, 1), dense_to_sub(shifts[0:8, :]), col_lane(cols, 0))
     self_ = (block_rows(c_own, c_other, 0), dense_to_sub(shifts[8:16, :]), col_lane(cols, 2))
-    sent[...] = gradient_half(r_other, 0, slice(HALF, BLOCK), cross, self_)
-    kept[...] = gradient_half(r_own, 0, slice(0, HALF), cross, self_)
+    sent[...] = gradient(half_rows(r_other, 0), SECOND, cross, self_)
+    kept[...] = gradient(half_rows(r_own, 0), FIRST, cross, self_)
 
 
 def phrase_gradients(
     place, r_own, r_other, c_own, c_other, shifts, cols, total, got, kept, sent, divergence
 ):
-    h_row, unused = unpair(*piggy_rows(got, place[0], 0))
+    h_row, unused = unpair(*piggy_rows(got, 0, place[0]))
     summed = total[...] + jnp.sum(got[...], axis=0)
     divergence[...] = summed * (1.0 / (POINTS * BETA))
     cross = (block_rows(c_own, c_other, 0), dense_to_sub(h_row), col_lane(cols, 1))
     self_ = (block_rows(c_own, c_other, 1), dense_to_sub(shifts[16:24, :]), col_lane(cols, 3))
-    sent[...] = gradient_half(r_other, 1, slice(HALF, BLOCK), cross, self_)
-    kept[...] = gradient_half(r_own, 1, slice(0, HALF), cross, self_)
+    sent[...] = gradient(half_rows(r_other, 1), SECOND, cross, self_)
+    kept[...] = gradient(half_rows(r_own, 1), FIRST, cross, self_)
+
+
+def join_gradients(x_kept, x_back, y_kept, y_back, out):
+    out[:, 0:OWN, :] = (x_kept[...] + x_back[...]).astype(out.dtype)
+    out[:, OWN : 2 * OWN, :] = (y_kept[...] + y_back[...]).astype(out.dtype)
 
 
 def call(body, outs, smem, passes, *args):
@@ -323,30 +349,55 @@
     return lax.ppermute(values, "core", [(0, 1), (1, 0)])
 
 
+def pair_swap(values):
+    return lax.ppermute(values, ("xh", "xl"), [(0, 3), (1, 2), (2, 1), (3, 0)])
+
+
+def y_step(values, shift):
+    return lax.ppermute(values, "y", [(y, (y + shift) % 4) for y in range(4)])
+
+
 def on_device(regions, phrases):
     f32 = jnp.float32
     core = lax.axis_index("core")
     spot_row = lax.axis_index("xl") * 4 + lax.axis_index("y")
-    far = lax.axis_index("xh")
-    spot_col = lax.axis_index("z")
-    place = jnp.stack([core, spot_row, far, spot_col]).astype(jnp.int32)
-
+    place = jnp.stack([core, spot_row, lax.axis_index("z"), lax.axis_index("xh")]).astype(jnp.int32)
+
+    block = ((8, 2 * OWN, WIDTH), jnp.bfloat16)
     own = jnp.concatenate([regions, phrases], axis=0)
     copies = jnp.broadcast_to(own[None], (8, 2 * OWN, WIDTH))
+    copies, own = lax.optimization_barrier((copies, own))
     c_own = share(copies, ("z",))
-    c_own, copies = lax.optimization_barrier((c_own, copies))
-    c_other = lax.ppermute(c_own, ("xh", "xl"), [(0, 3), (1, 2), (2, 1), (3, 0)])
-    r_own = share(copies, ("xl", "y"))
-    r_other = core_swap(r_own)
-    points = (r_own, r_other, c_own, c_other)
+    c_phrases = pair_swap(c_own[:, OWN : 2 * OWN, :])
+    near = jnp.stack([own] + [y_step(own, shift) for shift in (1, 2, 3)])
+    across = lax.ppermute(near, "xl", [(0, 1), (1, 0)])
+    near_far = core_swap(near)
+    across_far = core_swap(across)
 
     def message(rows):
         return ((16, rows, 128), f32)
 
-    (sent,) = call(first_rows, [message(8)], False, 1, *points)
-    later, sent = lax.optimization_barrier((points, sent))
+    r_own, r_other, partial = call(
+        first_half,
+        [block, block, ((8, 128), f32)],
+        True,
+        1,
+        place,
+        near,
+        across,
+        near_far,
+        across_far,
+        c_own,
+    )
+    partial, c_after = lax.optimization_barrier((partial, c_own))
+    c_regions = pair_swap(c_after[:, 0:OWN, :])
+    (sent,) = call(first_rows, [message(8)], False, 1, r_own, r_other, c_phrases, partial)
+    later, sent = lax.optimization_barrier(((r_own, r_other, c_own, c_phrases), sent))
     got = share(sent, ROW_GROUP)
-    sums, norms = call(first_self, [((16, 128), f32), ((32, 128), f32)], False, 2, *later)
+    sums, norms, c_other = call(
+        first_self, [((16, 128), f32), ((32, 128), f32), block], False, 2, *later, c_regions
+    )
+    points = (r_own, r_other, c_own, c_other)
     sent, state = call(
         first_cols, [message(24), ((8, 128), f32)], True, 1, place, *points, sums, got
     )
@@ -387,11 +438,11 @@
         total,
         got,
     )
-    y_back = core_swap(y_away)
-    joined = jnp.concatenate([x_kept + x_back, y_kept + y_back], axis=1).astype(jnp.bfloat16)
+    y_back, divergence = lax.optimization_barrier((core_swap(y_away), divergence[2, 0]))
+    (joined,) = call(join_gradients, [block], False, 0, x_kept, x_back, y_kept, y_back)
     parts = share(joined, ("xl", "y")).astype(f32)
     summed = jnp.sum(parts, axis=0)
-    return (summed[0:OWN], summed[OWN : 2 * OWN], divergence[2, 0])
+    return (summed[0:OWN], summed[OWN : 2 * OWN], divergence)
 
 
 def solution(mesh):

time: 138 us -> 131 us (0.949)
  waiting for transfers between devices: 20 us -> 14.4 us
  other arithmetic: 2.95 us -> 0.18 us
  starting transfers between devices: 29 us -> 31 us
    all_to_all x4 -> x2, waiting for transfers between devices: 18.1 us -> 4.12 us  [share(): lax.all_to_all(message, axes, 0, 0, tiled=True, axis_index_groups=groups)]
    ppermute x1 -> x6, waiting for transfers between devices: 0.85 us -> 9.03 us  [the longest x2 4.33 us: pair_swap(): return lax.ppermute(values, ('xh', 'xl'), [(0, 3), (1, 2), (2, 1), (3, 0)])]
    ppermute x1 -> x6, starting transfers between devices: 2.73 us -> 9.13 us  [the longest x3 4.99 us: y_step(): return lax.ppermute(values, 'y', [(y, (y + shift) % 4) for y in range(4)])]
    all_to_all x4 -> x2, starting transfers between devices: 21.6 us -> 15.8 us  [share(): lax.all_to_all(message, axes, 0, 0, tiled=True, axis_index_groups=groups)]
    concatenate x2 -> x0, other arithmetic: 1.61 us -> none  [the longest x1 0.83 us: on_device(): jnp.concatenate([x_kept + x_back, y_kept + y_back], axis=1)]
    ppermute x3 -> x4, starting transfers between devices: 4.62 us -> 6.09 us  [core_swap(): return lax.ppermute(values, 'core', [(0, 1), (1, 0)])]
    all_to_all x4 -> x5, blocking collectives: 63.4 us -> 62.1 us  [share(): lax.all_to_all(message, axes, 0, 0, tiled=True, axis_index_groups=groups)]
    pallas_call x8 -> x10, Pallas kernels: 18.8 us -> 19 us  [call(): pl.pallas_call(body, out_shape=shapes, in_specs=specs, out_specs=[pl.Bloc...]
  transfers between devices with their start and end apart: 8 -> 12, of which waited for: 7 -> 7; matrix products, arithmetic and copies ran while one was open for 1% -> 1% of each run, Pallas kernels for 6% -> 7%
where the time goes in v3:
time: 131 us; the launch traced here: 130 us
  blocking collectives  62.1 us (47%)
  starting transfers between devices  31 us (24%)
  Pallas kernels  19 us (15%)
  waiting for transfers between devices  14.4 us (11%)
  local copies, waits for them, and re-layouts  2.83 us (2%)
    all_to_all x5, blocking collectives, share(): lax.all_to_all(message, axes, 0, 0, tiled=True, axis_index_groups=groups)  62.1 us
    pallas_call x10, Pallas kernels, call(): pl.pallas_call(body, out_shape=shapes, in_specs=specs, out_specs=[pl.Bloc...  19 us
    all_to_all x2, starting transfers between devices, share(): lax.all_to_all(message, axes, 0, 0, tiled=True, axis_index_groups=groups)  15.8 us
    ppermute x4, starting transfers between devices, core_swap(): return lax.ppermute(values, 'core', [(0, 1), (1, 0)])  6.09 us
    ppermute x3, starting transfers between devices, y_step(): return lax.ppermute(values, 'y', [(y, (y + shift) % 4) for y in range(4)])  4.99 us
    ppermute x2, waiting for transfers between devices, pair_swap(): return lax.ppermute(values, ('xh', 'xl'), [(0, 3), (1, 2), (2, 1), (3, 0)])  4.33 us
    all_to_all x2, waiting for transfers between devices, share(): lax.all_to_all(message, axes, 0, 0, tiled=True, axis_index_groups=groups)  4.12 us
    ppermute x2, starting transfers between devices, pair_swap(): return lax.ppermute(values, ('xh', 'xl'), [(0, 3), (1, 2), (2, 1), (3, 0)])  2.85 us
  transfers between devices with their start and end apart: 12, of which 7 were waited for; matrix products, arithmetic and copies ran while one was open for 1% of the time, Pallas kernels for 7%

profile of v3, /device:TPU:1, one launch (start us, length us, event | category | flops | bytes accessed | tf_op | source)
XLA Modules:
  0.0 130.3 jit_solution(12667196211947571732)
XLA Ops:
  2.3 9.0 %all-to-all-start = ((bf16[8,128,256]{2,1,0:T(8,128)(2,1)}), bf16[8,128,256]{2,1,0:T(8,128)(2,1)S(1)}, u32[]{:S(2)}, u32[]{:S(2)}) async-start(bf16[8,128,256]{2,1,0:T(8,128)(2,1)} %broadcast_in_dim.2), calls=%async_computation | async-start | bytes 1048576 | tf_op jit(solution)/shard_map/all_to_all | solution.py:338
  12.6 2.6 %collective-permute-start.1 = (bf16[128,256]{1,0:T(8,128)(2,1)S(1)}, bf16[128,256]{1,0:T(8,128)(2,1)S(1)}, u32[]{:S(2)}, u32[]{:S(2)}) collective-permute-start(bf16[128,256]{1,0:T(8,128)(2,1)S(1)} %constant_dynamic-update-slice_fusion), channel_id=1, source_target_pairs={{0,2},{1,3},{2,0},{3,1},{4,6},{5,7},{6,4},{7,5},{8,10},{9,11},{10,... | collective-permute-start | bytes 196616 | tf_op jit(solution)/shard_map/ppermute | solution.py:357
  16.3 1.4 %collective-permute-done.1 = bf16[128,256]{1,0:T(8,128)(2,1)S(1)} collective-permute-done((bf16[128,256]{1,0:T(8,128)(2,1)S(1)}, bf16[128,256]{1,0:T(8,128)(2,1)S(1)}, u32[]{:S(2)}, u32[]{:S(2)}) %collective-permute-start.1) | collective-permute-done | bytes 65568 | tf_op jit(solution)/shard_map/ppermute | solution.py:357
  20.2 2.4 %collective-permute-start.4 = (bf16[4,128,256]{2,1,0:T(8,128)(2,1)S(1)}, bf16[4,128,256]{2,1,0:T(8,128)(2,1)S(1)}, u32[]{:S(2)}, u32[]{:S(2)}) collective-permute-start(bf16[4,128,256]{2,1,0:T(8,128)(2,1)S(1)} %pad_maximum_fusion.near), channel_id=1, source_target_pairs={{0,8},{8,0},{1,9},{9,1},{2,10},{10,2},{3,11},{11,3},{4,12},{12,4},... | collective-permute-start | bytes 786440 | tf_op jit(solution)/shard_map/ppermute | solution.py:349
  22.6 2.1 %collective-permute-done.3.across = bf16[4,128,256]{2,1,0:T(8,128)(2,1)S(1)} collective-permute-done((bf16[4,128,256]{2,1,0:T(8,128)(2,1)S(1)}, bf16[4,128,256]{2,1,0:T(8,128)(2,1)S(1)}, u32[]{:S(2)}, u32[]{:S(2)}) %collective-permute-start.3) | collective-permute-done | bytes 262176 | tf_op jit(solution)/shard_map/ppermute | solution.py:373
  24.7 3.0 %collective-permute-start.5 = (bf16[4,128,256]{2,1,0:T(8,128)(2,1)S(1)}, bf16[4,128,256]{2,1,0:T(8,128)(2,1)S(1)}, u32[]{:S(2)}, u32[]{:S(2)}) collective-permute-start(bf16[4,128,256]{2,1,0:T(8,128)(2,1)S(1)} %collective-permute-done.3.across), channel_id=1, source_target_pairs={{0,8},{8,0},{1,9},{9,1},{2,10},{10,2},{3,11},{11,3},{4,12},{12,4},... | collective-permute-start | bytes 786440 | tf_op jit(solution)/shard_map/ppermute | solution.py:349
  27.8 1.4 %all-to-all-done.c_own = bf16[8,128,256]{2,1,0:T(8,128)(2,1)S(1)} async-done(((bf16[8,128,256]{2,1,0:T(8,128)(2,1)}), bf16[8,128,256]{2,1,0:T(8,128)(2,1)S(1)}, u32[]{:S(2)}, u32[]{:S(2)}) %all-to-all-start) | async-done | bytes 524320 | tf_op jit(solution)/shard_map/all_to_all | solution.py:338
  29.2 2.6 %collective-permute-start.6 = (bf16[8,64,256]{2,1,0:T(8,128)(2,1)S(1)}, bf16[8,64,256]{2,1,0:T(8,128)(2,1)S(1)}, u32[]{:S(2)}, u32[]{:S(2)}) collective-permute-start(bf16[8,64,256]{2,1,0:T(8,128)(2,1)S(1)} %slice.20), channel_id=1, source_target_pairs={{0,132},{4,128},{128,4},{132,0},{1,133},{5,129},{129,5},{133,1},{2... | collective-permute-start | bytes 786440 | tf_op jit(solution)/shard_map/ppermute | solution.py:353
  31.8 1.5 %shard_map.49 = (bf16[8,128,256]{2,1,0:T(8,128)(2,1)S(1)}, bf16[8,128,256]{2,1,0:T(8,128)(2,1)S(1)}, f32[8,128]{1,0:T(8,128)S(1)}) custom-call(s32[4]{0:T(128)S(1)} %pad_add_fusion.place, bf16[4,128,256]{2,1,0:T(8,128)(2,1)S(1)} %pad_maximum_fusion.near, bf16[4,128,256]{2,1,0:T(8,128)(2,1)S(1)} %collective-permute-done.3.across, ...), custom_call_target="tpu_custom_call" | custom-call | flops 536870912 | bytes 2097152 | tf_op jit(solution)/shard_map/pallas_call | solution.py:323
  33.6 4.3 %collective-permute-done.6.c_phrases = bf16[8,64,256]{2,1,0:T(8,128)(2,1)S(1)} collective-permute-done((bf16[8,64,256]{2,1,0:T(8,128)(2,1)S(1)}, bf16[8,64,256]{2,1,0:T(8,128)(2,1)S(1)}, u32[]{:S(2)}, u32[]{:S(2)}) %collective-permute-start.6) | collective-permute-done | bytes 262176 | tf_op jit(solution)/shard_map/ppermute | solution.py:353
  37.9 1.6 %shard_map.50 = f32[16,8,128]{2,1,0:T(8,128)} custom-call(bf16[8,128,256]{2,1,0:T(8,128)(2,1)S(1)} %get-tuple-element.40.r_own, bf16[8,128,256]{2,1,0:T(8,128)(2,1)S(1)} %get-tuple-element.41.r_other, bf16[8,64,256]{2,1,0:T(8,128)(2,1)S(1)} %collective-permute-done.6.c_phrases, f32[8,128]{1,0:T(8,128)S(1)} %get-tuple-element.39.partial), custom_call_target="tpu_custom_call" | custom-call | flops 536870912 | bytes 2097152 | tf_op jit(solution)/shard_map/pallas_call | solution.py:323
  39.5 6.8 %all-to-all-start.1 = ((f32[16,8,128]{2,1,0:T(8,128)}), f32[16,8,128]{2,1,0:T(8,128)S(1)}, u32[]{:S(2)}, u32[]{:S(2)}) async-start(f32[16,8,128]{2,1,0:T(8,128)} %shard_map.50), calls=%async_computation.1 | async-start | bytes 131072 | tf_op jit(solution)/shard_map/all_to_all | solution.py:338
  46.3 3.2 %shard_map.51 = (f32[16,128]{1,0:T(8,128)S(1)}, f32[32,128]{1,0:T(8,128)S(1)}, bf16[8,128,256]{2,1,0:T(8,128)(2,1)S(1)}) custom-call(bf16[8,128,256]{2,1,0:T(8,128)(2,1)S(1)} %get-tuple-element.40.r_own, bf16[8,128,256]{2,1,0:T(8,128)(2,1)S(1)} %get-tuple-element.41.r_other, bf16[8,128,256]{2,1,0:T(8,128)(2,1)S(1)} %all-to-all-done.c_own, ...), custom_call_target="tpu_custom_call" | custom-call | flops 1073741824 | bytes 2097152 | tf_op jit(solution)/shard_map/pallas_call | solution.py:323
  49.4 2.7 %all-to-all-done.1.got = f32[16,8,128]{2,1,0:T(8,128)S(1)} async-done(((f32[16,8,128]{2,1,0:T(8,128)}), f32[16,8,128]{2,1,0:T(8,128)S(1)}, u32[]{:S(2)}, u32[]{:S(2)}) %all-to-all-start.1) | async-done | bytes 65568 | tf_op jit(solution)/shard_map/all_to_all | solution.py:338
  52.1 2.0 %shard_map.52 = (f32[16,24,128]{2,1,0:T(8,128)S(1)}, f32[8,128]{1,0:T(8,128)S(1)}) custom-call(s32[4]{0:T(128)S(1)} %pad_add_fusion.place, bf16[8,128,256]{2,1,0:T(8,128)(2,1)S(1)} %get-tuple-element.40.r_own, bf16[8,128,256]{2,1,0:T(8,128)(2,1)S(1)} %get-tuple-element.41.r_other, bf16[8,128,256]{2,1,0:T(8,128)(2,1)S(1)} %all-to-all-done.c_own, ...), custom_call_target="tpu_custom_call" | custom-call | flops 536870912 | bytes 2097152 | tf_op jit(solution)/shard_map/pallas_call | solution.py:323
  54.1 15.2 %all_to_all.35.got = f32[16,24,128]{2,1,0:T(8,128)S(1)} all-to-all(f32[16,24,128]{2,1,0:T(8,128)S(1)} %get-tuple-element.50), channel_id=1, replica_groups={{0,16,32,48,64,80,96,112,132,148,164,180,196,212,228,244},{4,20,36,52,6..., dimensions={0} | all-to-all | bytes 393216 | tf_op jit(solution)/shard_map/all_to_all | solution.py:338
  69.4 3.0 %shard_map.53 = (f32[16,32,128]{2,1,0:T(8,128)S(1)}, f32[8,128]{1,0:T(8,128)S(1)}) custom-call(s32[4]{0:T(128)S(1)} %pad_add_fusion.place, bf16[8,128,256]{2,1,0:T(8,128)(2,1)S(1)} %get-tuple-element.40.r_own, bf16[8,128,256]{2,1,0:T(8,128)(2,1)S(1)} %get-tuple-element.41.r_other, bf16[8,128,256]{2,1,0:T(8,128)(2,1)S(1)} %all-to-all-done.c_own, ...), custom_call_target="tpu_custom_call" | custom-call | flops 1610612736 | bytes 2097152 | tf_op jit(solution)/shard_map/pallas_call | solution.py:323
  72.3 12.7 %all_to_all.36.got = f32[16,32,128]{2,1,0:T(8,128)S(1)} all-to-all(f32[16,32,128]{2,1,0:T(8,128)S(1)} %get-tuple-element.52), channel_id=1, replica_groups=mesh['xh'=2,'z'=8,'core'=2,'xl'=2,'y'=4] {'core','xl','y'}, dimensions={0} | all-to-all | bytes 524288 | tf_op jit(solution)/shard_map/all_to_all | solution.py:338
  85.0 1.5 %shard_map.54 = (f32[16,16,128]{2,1,0:T(8,128)S(1)}, f32[24,128]{1,0:T(8,128)S(1)}) custom-call(s32[4]{0:T(128)S(1)} %pad_add_fusion.place, bf16[8,128,256]{2,1,0:T(8,128)(2,1)S(1)} %get-tuple-element.40.r_own, bf16[8,128,256]{2,1,0:T(8,128)(2,1)S(1)} %get-tuple-element.41.r_other, bf16[8,128,256]{2,1,0:T(8,128)(2,1)S(1)} %all-to-all-done.c_own, ...), custom_call_target="tpu_custom_call" | custom-call | flops 536870912 | bytes 2097152 | tf_op jit(solution)/shard_map/pallas_call | solution.py:323
  86.4 12.4 %all_to_all.37.got = f32[16,16,128]{2,1,0:T(8,128)S(1)} all-to-all(f32[16,16,128]{2,1,0:T(8,128)S(1)} %get-tuple-element.54), channel_id=1, replica_groups={{0,16,32,48,64,80,96,112,132,148,164,180,196,212,228,244},{4,20,36,52,6..., dimensions={0} | all-to-all | bytes 262144 | tf_op jit(solution)/shard_map/all_to_all | solution.py:338
  99.5 10.5 %all_to_all.38.got = f32[16,8,128]{2,1,0:T(8,128)S(1)} all-to-all(f32[16,8,128]{2,1,0:T(8,128)S(1)} %get-tuple-element.59), channel_id=1, replica_groups=mesh['xh'=2,'z'=8,'core'=2,'xl'=2,'y'=4] {'core','xl','y'}, dimensions={0} | all-to-all | bytes 131072 | tf_op jit(solution)/shard_map/all_to_all | solution.py:338
  110.0 3.1 %shard_map.57 = (f32[8,64,256]{2,1,0:T(8,128)S(1)}, f32[8,64,256]{2,1,0:T(8,128)S(1)}, f32[8,128]{1,0:T(8,128)S(1)}) custom-call(s32[4]{0:T(128)S(1)} %pad_add_fusion.place, bf16[8,128,256]{2,1,0:T(8,128)(2,1)S(1)} %get-tuple-element.40.r_own, bf16[8,128,256]{2,1,0:T(8,128)(2,1)S(1)} %get-tuple-element.41.r_other, ...), custom_call_target="tpu_custom_call" | custom-call | flops 2147483648 | bytes 2097152 | tf_op jit(solution)/shard_map/pallas_call | solution.py:323
  113.5 2.6 %shard_map.56 = (f32[8,64,256]{2,1,0:T(8,128)S(1)}, f32[8,64,256]{2,1,0:T(8,128)S(1)}) custom-call(bf16[8,128,256]{2,1,0:T(8,128)(2,1)S(1)} %get-tuple-element.40.r_own, bf16[8,128,256]{2,1,0:T(8,128)(2,1)S(1)} %get-tuple-element.41.r_other, bf16[8,128,256]{2,1,0:T(8,128)(2,1)S(1)} %all-to-all-done.c_own, ...), custom_call_target="tpu_custom_call" | custom-call | flops 2147483648 | bytes 2097152 | tf_op jit(solution)/shard_map/pallas_call | solution.py:323
  118.2 11.4 %all_to_all.39 = bf16[8,128,256]{2,1,0:T(8,128)(2,1)S(1)} all-to-all(bf16[8,128,256]{2,1,0:T(8,128)(2,1)S(1)} %shard_map.58), channel_id=1, replica_groups=mesh['xh'=2,'z'=8,'core'=2,'xl'=2,'y'=4] {'xl','y'}, dimensions={0} | all-to-all | bytes 1048576 | tf_op jit(solution)/shard_map/all_to_all | solution.py:338
  (27 shorter events, 10.9 us)
Async XLA Ops:
  0.6 0.8 copy-start
  2.3 27.0 %all-to-all-start = ((bf16[8,128,256]{2,1,0:T(8,128)(2,1)}), bf16[8,128,256]{2,1,0:T(8,128)(2,1)S(1)}, u32[]{:S(2)}, u32[]{:S(2)}) async-start(bf16[8,128,256]{2,1,0:T(8,128)(2,1)} %broadcast_in_dim.2), calls=%async_computation | async-start | bytes 1048576 | tf_op jit(solution)/shard_map/all_to_all | solution.py:338
  11.3 5.0 %collective-permute-start = (bf16[128,256]{1,0:T(8,128)(2,1)S(1)}, bf16[128,256]{1,0:T(8,128)(2,1)S(1)}, u32[]{:S(2)}, u32[]{:S(2)}) collective-permute-start(bf16[128,256]{1,0:T(8,128)(2,1)S(1)} %constant_dynamic-update-slice_fusion), channel_id=1, source_target_pairs={{0,1},{1,2},{2,3},{3,0},{4,5},{5,6},{6,7},{7,4},{8,9},{9,10},{10,1... | collective-permute-start | bytes 196616 | tf_op jit(solution)/shard_map/ppermute | solution.py:357
  12.6 5.1 %collective-permute-start.1 = (bf16[128,256]{1,0:T(8,128)(2,1)S(1)}, bf16[128,256]{1,0:T(8,128)(2,1)S(1)}, u32[]{:S(2)}, u32[]{:S(2)}) collective-permute-start(bf16[128,256]{1,0:T(8,128)(2,1)S(1)} %constant_dynamic-update-slice_fusion), channel_id=1, source_target_pairs={{0,2},{1,3},{2,0},{3,1},{4,6},{5,7},{6,4},{7,5},{8,10},{9,11},{10,... | collective-permute-start | bytes 196616 | tf_op jit(solution)/shard_map/ppermute | solution.py:357
  15.2 3.7 %collective-permute-start.2 = (bf16[128,256]{1,0:T(8,128)(2,1)S(1)}, bf16[128,256]{1,0:T(8,128)(2,1)S(1)}, u32[]{:S(2)}, u32[]{:S(2)}) collective-permute-start(bf16[128,256]{1,0:T(8,128)(2,1)S(1)} %constant_dynamic-update-slice_fusion), channel_id=1, source_target_pairs={{0,3},{1,0},{2,1},{3,2},{4,7},{5,4},{6,5},{7,6},{8,11},{9,8},{10,9... | collective-permute-start | bytes 196616 | tf_op jit(solution)/shard_map/ppermute | solution.py:357
  18.9 5.8 %collective-permute-start.3 = (bf16[4,128,256]{2,1,0:T(8,128)(2,1)S(1)}, bf16[4,128,256]{2,1,0:T(8,128)(2,1)S(1)}, u32[]{:S(2)}, u32[]{:S(2)}) collective-permute-start(bf16[4,128,256]{2,1,0:T(8,128)(2,1)S(1)} %pad_maximum_fusion.near), channel_id=1, source_target_pairs={{0,4},{4,0},{1,5},{5,1},{2,6},{6,2},{3,7},{7,3},{8,12},{12,8},{9,1... | collective-permute-start | bytes 786440 | tf_op jit(solution)/shard_map/ppermute | solution.py:373
  20.2 11.6 %collective-permute-start.4 = (bf16[4,128,256]{2,1,0:T(8,128)(2,1)S(1)}, bf16[4,128,256]{2,1,0:T(8,128)(2,1)S(1)}, u32[]{:S(2)}, u32[]{:S(2)}) collective-permute-start(bf16[4,128,256]{2,1,0:T(8,128)(2,1)S(1)} %pad_maximum_fusion.near), channel_id=1, source_target_pairs={{0,8},{8,0},{1,9},{9,1},{2,10},{10,2},{3,11},{11,3},{4,12},{12,4},... | collective-permute-start | bytes 786440 | tf_op jit(solution)/shard_map/ppermute | solution.py:349
  24.7 7.1 %collective-permute-start.5 = (bf16[4,128,256]{2,1,0:T(8,128)(2,1)S(1)}, bf16[4,128,256]{2,1,0:T(8,128)(2,1)S(1)}, u32[]{:S(2)}, u32[]{:S(2)}) collective-permute-start(bf16[4,128,256]{2,1,0:T(8,128)(2,1)S(1)} %collective-permute-done.3.across), channel_id=1, source_target_pairs={{0,8},{8,0},{1,9},{9,1},{2,10},{10,2},{3,11},{11,3},{4,12},{12,4},... | collective-permute-start | bytes 786440 | tf_op jit(solution)/shard_map/ppermute | solution.py:349
  29.2 8.7 %collective-permute-start.6 = (bf16[8,64,256]{2,1,0:T(8,128)(2,1)S(1)}, bf16[8,64,256]{2,1,0:T(8,128)(2,1)S(1)}, u32[]{:S(2)}, u32[]{:S(2)}) collective-permute-start(bf16[8,64,256]{2,1,0:T(8,128)(2,1)S(1)} %slice.20), channel_id=1, source_target_pairs={{0,132},{4,128},{128,4},{132,0},{1,133},{5,129},{129,5},{133,1},{2... | collective-permute-start | bytes 786440 | tf_op jit(solution)/shard_map/ppermute | solution.py:353
  33.3 12.9 %collective-permute-start.7 = (bf16[8,64,256]{2,1,0:T(8,128)(2,1)S(1)}, bf16[8,64,256]{2,1,0:T(8,128)(2,1)S(1)}, u32[]{:S(2)}, u32[]{:S(2)}) collective-permute-start(bf16[8,64,256]{2,1,0:T(8,128)(2,1)S(1)} %slice.16), channel_id=1, source_target_pairs={{0,132},{4,128},{128,4},{132,0},{1,133},{5,129},{129,5},{133,1},{2... | collective-permute-start | bytes 786440 | tf_op jit(solution)/shard_map/ppermute | solution.py:353
  39.5 12.6 %all-to-all-start.1 = ((f32[16,8,128]{2,1,0:T(8,128)}), f32[16,8,128]{2,1,0:T(8,128)S(1)}, u32[]{:S(2)}, u32[]{:S(2)}) async-start(f32[16,8,128]{2,1,0:T(8,128)} %shard_map.50), calls=%async_computation.1 | async-start | bytes 131072 | tf_op jit(solution)/shard_map/all_to_all | solution.py:338
  113.1 3.8 %collective-permute-start.9 = (f32[8,64,256]{2,1,0:T(8,128)S(1)}, f32[8,64,256]{2,1,0:T(8,128)S(1)}, u32[]{:S(2)}, u32[]{:S(2)}) collective-permute-start(f32[8,64,256]{2,1,0:T(8,128)S(1)} %get-tuple-element.61), channel_id=1, source_target_pairs={{0,8},{8,0},{1,9},{9,1},{2,10},{10,2},{3,11},{11,3},{4,12},{12,4},... | collective-permute-start | bytes 1572872 | tf_op jit(solution)/shard_map/ppermute | solution.py:349
  116.1 2.0 %collective-permute-start.8 = (f32[8,64,256]{2,1,0:T(8,128)S(1)}, f32[8,64,256]{2,1,0:T(8,128)S(1)}, u32[]{:S(2)}, u32[]{:S(2)}) collective-permute-start(f32[8,64,256]{2,1,0:T(8,128)S(1)} %get-tuple-element.57), channel_id=1, source_target_pairs={{0,8},{8,0},{1,9},{9,1},{2,10},{10,2},{3,11},{11,3},{4,12},{12,4},... | collective-permute-start | bytes 1572872 | tf_op jit(solution)/shard_map/ppermute | solution.py:349

commit v4 on v3

--- a/solution.py
+++ b/solution.py
@@ -175,8 +175,8 @@
     message_ref[...] = jnp.broadcast_to(rows[None], message_ref.shape)
 
 
-def first_half(place, near, across, near_far, across_far, c_own, r_own, r_other, partial):
-    side, spot = place[1] // 4, place[1] % 4
+def first_half(near, across, near_far, across_far, c_own, r_own, r_other, partial):
+    side, spot = lax.axis_index("xl"), lax.axis_index("y")
     for step in range(4):
         source = lax.rem(spot + 4 - step, 4)
         r_own[pl.ds(side * 4 + source, 1)] = near[step : step + 1]
@@ -211,19 +211,19 @@
     )
 
 
-def first_cols(place, r_own, r_other, c_own, c_other, sums, got, message, state):
-    u = LOG_COUNT - join_logs(got, place[0], 0)
+def first_cols(r_own, r_other, c_own, c_other, sums, got, message, state):
+    u = LOG_COUNT - join_logs(got, lax.axis_index("core"), 0)
     x_row = block_rows(r_own, r_other, 0)
     cross = peak_pass(x_row, c_own, c_other, 1, dense_to_sub(u))
     send_all(message, jnp.concatenate([cross, sums[...]], axis=0))
     state[...] = u
 
 
-def second_rows(place, r_own, r_other, c_own, c_other, norms, state, got, message, h_out):
-    spot = place[2]
-    h = LOG_COUNT - join_logs(got, place[3], 0)
-    p = LOG_COUNT - log2(join_sums(got, place[3], 8))
-    q = LOG_COUNT - log2(join_sums(got, place[3], 16))
+def second_rows(r_own, r_other, c_own, c_other, norms, state, got, message, h_out):
+    far, spot = lax.axis_index("xh"), lax.axis_index("z")
+    h = LOG_COUNT - join_logs(got, far, 0)
+    p = LOG_COUNT - log2(join_sums(got, far, 8))
+    q = LOG_COUNT - log2(join_sums(got, far, 16))
     x_col = block_rows(c_own, c_other, 0)
     y_col = block_rows(c_own, c_other, 1)
     cross = sum_pass(y_col, r_own, r_other, 0, dense_to_sub(h), dense_to_lane(state[...]))
@@ -233,14 +233,16 @@
     self_q = sum_pass(
         y_col, r_own, r_other, 1, dense_to_sub(q - norms[24:32, :]), -dense_to_lane(norms[8:16, :])
     )
-    carry = jnp.broadcast_to(pair_row(own_piece(p, spot), own_piece(q, spot)), (8, 128))
-    send_all(message, jnp.concatenate([cross, self_p, self_q, carry], axis=0))
+    carry = pair_row(own_piece(p, spot), own_piece(q, spot))
+    other = jnp.broadcast_to(own_piece(h, spot), (7, 128))
+    send_all(message, jnp.concatenate([cross, self_p, self_q, carry, other], axis=0))
     h_out[...] = h
 
 
-def second_cols(place, r_own, r_other, c_own, c_other, norms, state, h_in, got, message, shifts):
-    core, spot = place[0], place[1]
+def second_cols(r_own, r_other, c_own, c_other, norms, state, h_in, got, message, shifts):
+    core, spot = lax.axis_index("core"), lax.axis_index("xl") * 4 + lax.axis_index("y")
     p_first, q_first = unpair(*piggy_rows(got, 24, core))
+    h_row, unused = unpair(*piggy_rows(got, 25, core))
     u = state[...] + (LOG_COUNT - log2(join_sums(got, core, 0)))
     p = 0.5 * (p_first + (LOG_COUNT - log2(join_sums(got, core, 8))))
     q = 0.5 * (q_first + (LOG_COUNT - log2(join_sums(got, core, 16))))
@@ -252,18 +254,7 @@
     second = pair_row(own_piece(qt, spot), jnp.zeros((1, 128), jnp.float32))
     total = jnp.broadcast_to(canonical_sum(u - pt - qt), (6, 128))
     send_all(message, jnp.concatenate([cross, first, second, total], axis=0))
-    shifts[...] = jnp.concatenate([u, pt, qt], axis=0)
-
-
-def last_cols(place, h_in, got, message, cols, total):
-    h = h_in[...] + (LOG_COUNT - log2(join_sums(got, place[3], 0)))
-    u_col, p_col = unpair(*piggy_rows(got, 8, place[3]))
-    q_col, unused = unpair(*piggy_rows(got, 9, place[3]))
-    piece = own_piece(h, place[2])
-    part = jnp.broadcast_to(canonical_sum(h), (7, 128))
-    send_all(message, jnp.concatenate([piece, part], axis=0))
-    cols[...] = jnp.concatenate([h, u_col, p_col, q_col], axis=0)
-    total[...] = jnp.sum(got[:, 8:16, :], axis=0)
+    shifts[...] = jnp.concatenate([u, pt, qt, h_row], axis=0)
 
 
 def weights(rows, columns, sub, lane):
@@ -283,43 +274,83 @@
 FIRST = slice(0, HALF)
 
 
-def col_lane(cols, k):
-    return dense_to_lane(cols[8 * k : 8 * k + 8, :]) - LOG_COUNT
-
-
 def gradient(rows, part, cross, self_):
     return term(rows, part, *cross) - term(rows, part, *self_)
 
 
-def region_gradients(r_own, r_other, c_own, c_other, shifts, cols, kept, sent):
-    cross = (block_rows(c_own, c_other, 1), dense_to_sub(shifts[0:8, :]), col_lane(cols, 0))
-    self_ = (block_rows(c_own, c_other, 0), dense_to_sub(shifts[8:16, :]), col_lane(cols, 2))
+def region_gradients(
+    r_own, r_other, c_own, c_other, shifts, h_in, got, kept, sent, cols, scale, sums
+):
+    far = lax.axis_index("xh")
+    change = LOG_COUNT - log2(join_sums(got, far, 0))
+    h = h_in[...] + change
+    u_col, p_col = unpair(*piggy_rows(got, 8, far))
+    q_col, unused = unpair(*piggy_rows(got, 9, far))
+    cols[...] = jnp.concatenate([u_col, q_col], axis=0) - LOG_COUNT
+    own_change = jnp.broadcast_to(own_piece(change, lax.axis_index("z")), (128, 128)).T
+    scale[...] = widen(jnp.exp2(own_change[0:OWN, :]), WIDTH)
+    total = jnp.sum(got[:, 8:16, :], axis=0)
+    part = jnp.broadcast_to(canonical_sum(h), (8, 128))
+    sums[...] = jnp.concatenate([jnp.broadcast_to(total[2:3], (8, 128)), part], axis=0)
+    h_lane = dense_to_lane(h) - LOG_COUNT
+    cross = (block_rows(c_own, c_other, 1), dense_to_sub(shifts[0:8, :]), h_lane)
+    p_lane = dense_to_lane(p_col) - LOG_COUNT
+    self_ = (block_rows(c_own, c_other, 0), dense_to_sub(shifts[8:16, :]), p_lane)
     sent[...] = gradient(half_rows(r_other, 0), SECOND, cross, self_)
     kept[...] = gradient(half_rows(r_own, 0), FIRST, cross, self_)
 
 
 def phrase_gradients(
-    place, r_own, r_other, c_own, c_other, shifts, cols, total, got, kept, sent, divergence
+    r_own, r_other, c_own, c_other, shifts, cols, kept, sent, cross_kept, cross_sent
 ):
-    h_row, unused = unpair(*piggy_rows(got, 0, place[0]))
-    summed = total[...] + jnp.sum(got[...], axis=0)
-    divergence[...] = summed * (1.0 / (POINTS * BETA))
-    cross = (block_rows(c_own, c_other, 0), dense_to_sub(h_row), col_lane(cols, 1))
-    self_ = (block_rows(c_own, c_other, 1), dense_to_sub(shifts[16:24, :]), col_lane(cols, 3))
-    sent[...] = gradient(half_rows(r_other, 1), SECOND, cross, self_)
-    kept[...] = gradient(half_rows(r_own, 1), FIRST, cross, self_)
-
-
-def join_gradients(x_kept, x_back, y_kept, y_back, out):
-    out[:, 0:OWN, :] = (x_kept[...] + x_back[...]).astype(out.dtype)
-    out[:, OWN : 2 * OWN, :] = (y_kept[...] + y_back[...]).astype(out.dtype)
-
-
-def call(body, outs, smem, passes, *args):
+    cross = (
+        block_rows(c_own, c_other, 0),
+        dense_to_sub(shifts[24:32, :]),
+        dense_to_lane(cols[0:8, :]),
+    )
+    self_ = (
+        block_rows(c_own, c_other, 1),
+        dense_to_sub(shifts[16:24, :]),
+        dense_to_lane(cols[8:16, :]),
+    )
+    for ref, part, out, cross_out in (
+        (r_other, SECOND, sent, cross_sent),
+        (r_own, FIRST, kept, cross_kept),
+    ):
+        rows = half_rows(ref, 1)
+        cross_out[...] = term(rows, part, *cross)
+        out[...] = cross_out[...] - term(rows, part, *self_)
+
+
+def join_gradients(
+    x_kept, x_back, y_kept, y_back, cross_kept, cross_back, sums, sum_back, out
+):
+    kept_back = ((x_kept, x_back), (y_kept, y_back), (cross_kept, cross_back))
+    for k, (kept, back) in enumerate(kept_back):
+        out[:, k * OWN : (k + 1) * OWN, :] = (kept[...] + back[...]).astype(out.dtype)
+    part = jnp.broadcast_to(sums[8:9, :] + sum_back[8:9, :], (16, 128))
+    high = part.astype(jnp.bfloat16)
+    left = part - high.astype(jnp.float32)
+    middle = left.astype(jnp.bfloat16)
+    low = left - middle.astype(jnp.float32)
+    row = lax.broadcasted_iota(jnp.int32, (16, 128), 0)
+    rest = jnp.where(row < 8, left, low).astype(jnp.bfloat16)
+    tail = jnp.concatenate([high, rest], axis=1)
+    out[:, 3 * OWN :, :] = jnp.broadcast_to(tail[None], (8, 16, WIDTH))
+
+
+def finish(parts, scale, sums, grad_x, grad_y, divergence):
+    summed = jnp.sum(parts[...].astype(jnp.float32), axis=0)
+    grad_x[...] = summed[0:OWN]
+    grad_y[...] = summed[OWN : 2 * OWN] + (scale[...] - 1.0) * summed[2 * OWN : 3 * OWN]
+    high = summed[192:193, 0:128]
+    whole = high + (summed[192:193, 128:256] + summed[200:201, 128:256])
+    divergence[...] = (whole + sums[0:1, :])[0:1, 0:1] * (1.0 / (POINTS * BETA))
+
+
+def call(body, outs, passes, *args):
     shapes = [jax.ShapeDtypeStruct(shape, dtype) for shape, dtype in outs]
     specs = [pl.BlockSpec(memory_space=pltpu.VMEM)] * len(args)
-    if smem:
-        specs[0] = pl.BlockSpec(memory_space=pltpu.SMEM)
     return pl.pallas_call(
         body,
         out_shape=shapes,
@@ -359,14 +390,12 @@
 
 def on_device(regions, phrases):
     f32 = jnp.float32
-    core = lax.axis_index("core")
-    spot_row = lax.axis_index("xl") * 4 + lax.axis_index("y")
-    place = jnp.stack([core, spot_row, lax.axis_index("z"), lax.axis_index("xh")]).astype(jnp.int32)
-
     block = ((8, 2 * OWN, WIDTH), jnp.bfloat16)
+    spread = [jnp.broadcast_to(points[None], (8, OWN, WIDTH)) for points in (regions, phrases)]
+    copies, regions, phrases = lax.optimization_barrier(
+        (jnp.concatenate(spread, axis=1), regions, phrases)
+    )
     own = jnp.concatenate([regions, phrases], axis=0)
-    copies = jnp.broadcast_to(own[None], (8, 2 * OWN, WIDTH))
-    copies, own = lax.optimization_barrier((copies, own))
     c_own = share(copies, ("z",))
     c_phrases = pair_swap(c_own[:, OWN : 2 * OWN, :])
     near = jnp.stack([own] + [y_step(own, shift) for shift in (1, 2, 3)])
@@ -380,9 +409,7 @@
     r_own, r_other, partial = call(
         first_half,
         [block, block, ((8, 128), f32)],
-        True,
         1,
-        place,
         near,
         across,
         near_far,
@@ -391,27 +418,25 @@
     )
     partial, c_after = lax.optimization_barrier((partial, c_own))
     c_regions = pair_swap(c_after[:, 0:OWN, :])
-    (sent,) = call(first_rows, [message(8)], False, 1, r_own, r_other, c_phrases, partial)
+    (sent,) = call(first_rows, [message(8)], 1, r_own, r_other, c_phrases, partial)
     later, sent = lax.optimization_barrier(((r_own, r_other, c_own, c_phrases), sent))
     got = share(sent, ROW_GROUP)
     sums, norms, c_other = call(
-        first_self, [((16, 128), f32), ((32, 128), f32), block], False, 2, *later, c_regions
+        first_self, [((16, 128), f32), ((32, 128), f32), block], 2, *later, c_regions
     )
     points = (r_own, r_other, c_own, c_other)
     sent, state = call(
-        first_cols, [message(24), ((8, 128), f32)], True, 1, place, *points, sums, got
+        first_cols, [message(24), ((8, 128), f32)], 1, *points, sums, got
     )
     got = share_col(sent)
     sent, h_first = call(
-        second_rows, [message(32), ((8, 128), f32)], True, 3, place, *points, norms, state, got
+        second_rows, [message(32), ((8, 128), f32)], 3, *points, norms, state, got
     )
     got = share(sent, ROW_GROUP)
     sent, shifts = call(
         second_cols,
-        [message(16), ((24, 128), f32)],
-        True,
+        [message(16), ((32, 128), f32)],
         1,
-        place,
         *points,
         norms,
         state,
@@ -419,30 +444,43 @@
         got,
     )
     got = share_col(sent)
-    sent, cols, total = call(
-        last_cols, [message(8), ((32, 128), f32), ((8, 128), f32)], True, 0, place, h_first, got
-    )
-    got = share(sent, ROW_GROUP)
     half = ((8, OWN, WIDTH), f32)
-    x_kept, x_away = call(region_gradients, [half, half], False, 4, *points, shifts, cols)
-    x_back = core_swap(x_away)
-    y_kept, y_away, divergence = call(
-        phrase_gradients,
-        [half, half, ((8, 128), f32)],
-        True,
-        4,
-        place,
+    x_kept, x_away, cols, scale, sums = call(
+        region_gradients,
+        [half, half, ((16, 128), f32), ((OWN, WIDTH), f32), ((16, 128), f32)],
+        2,
         *points,
         shifts,
-        cols,
-        total,
+        h_first,
         got,
     )
-    y_back, divergence = lax.optimization_barrier((core_swap(y_away), divergence[2, 0]))
-    (joined,) = call(join_gradients, [block], False, 0, x_kept, x_back, y_kept, y_back)
-    parts = share(joined, ("xl", "y")).astype(f32)
-    summed = jnp.sum(parts, axis=0)
-    return (summed[0:OWN], summed[OWN : 2 * OWN], divergence)
+    x_back, sum_back = core_swap(x_away), core_swap(sums)
+    y_kept, y_away, cross_kept, cross_away = call(
+        phrase_gradients, [half] * 4, 2, *points, shifts, cols
+    )
+    y_back, cross_back = core_swap(y_away), core_swap(cross_away)
+    (joined,) = call(
+        join_gradients,
+        [((8, 3 * OWN + 16, WIDTH), jnp.bfloat16)],
+        0,
+        x_kept,
+        x_back,
+        y_kept,
+        y_back,
+        cross_kept,
+        cross_back,
+        sums,
+        sum_back,
+    )
+    grad_x, grad_y, divergence = call(
+        finish,
+        [((OWN, WIDTH), f32), ((OWN, WIDTH), f32), ((1, 1), f32)],
+        0,
+        share(joined, ("xl", "y")),
+        scale,
+        sums,
+    )
+    return (grad_x, grad_y, divergence[0, 0])
 
 
 def solution(mesh):

time: 131 us -> 124 us (0.947)
  blocking collectives: 62.1 us -> 55.1 us
  Pallas kernels: 19 us -> 16.5 us
  waiting for transfers between devices: 14.4 us -> 16.8 us
  local copies, waits for them, and re-layouts: 2.83 us -> 0.86 us
  starting transfers between devices: 31 us -> 32.4 us
    all_to_all x5 -> x4, blocking collectives: 62.1 us -> 55.1 us  [share(): lax.all_to_all(message, axes, 0, 0, tiled=True, axis_index_groups=groups)]
    pallas_call x10, Pallas kernels: 19 us -> 16.5 us  [call(): pl.pallas_call(body, out_shape=shapes, in_specs=specs, out_specs=[pl.Bloc...]
    ppermute x4 -> x6, starting transfers between devices: 6.09 us -> 8.34 us  [core_swap(): return lax.ppermute(values, 'core', [(0, 1), (1, 0)])]
    ppermute x3, waiting for transfers between devices: 2.61 us -> 4.57 us  [y_step(): return lax.ppermute(values, 'y', [(y, (y + shift) % 4) for y in range(4)])]
  transfers between devices with their start and end apart: 12 -> 14, of which waited for: 7 -> 8; matrix products, arithmetic and copies ran while one was open for 1% -> 0% of each run, Pallas kernels for 7% -> 7%
where the time goes in v4:
time: 124 us; the launch traced here: 123 us
  blocking collectives  55.1 us (44%)
  starting transfers between devices  32.4 us (26%)
  waiting for transfers between devices  16.8 us (14%)
  Pallas kernels  16.5 us (13%)
    all_to_all x4, blocking collectives, share(): lax.all_to_all(message, axes, 0, 0, tiled=True, axis_index_groups=groups)  55.1 us
    pallas_call x10, Pallas kernels, call(): pl.pallas_call(body, out_shape=shapes, in_specs=specs, out_specs=[pl.Bloc...  16.5 us
    all_to_all x2, starting transfers between devices, share(): lax.all_to_all(message, axes, 0, 0, tiled=True, axis_index_groups=groups)  15.9 us
    ppermute x6, starting transfers between devices, core_swap(): return lax.ppermute(values, 'core', [(0, 1), (1, 0)])  8.34 us
    ppermute x2, waiting for transfers between devices, pair_swap(): return lax.ppermute(values, ('xh', 'xl'), [(0, 3), (1, 2), (2, 1), (3, 0)])  4.67 us
    ppermute x3, waiting for transfers between devices, y_step(): return lax.ppermute(values, 'y', [(y, (y + shift) % 4) for y in range(4)])  4.57 us
    ppermute x3, starting transfers between devices, y_step(): return lax.ppermute(values, 'y', [(y, (y + shift) % 4) for y in range(4)])  3.85 us
    all_to_all x2, waiting for transfers between devices, share(): lax.all_to_all(message, axes, 0, 0, tiled=True, axis_index_groups=groups)  3.34 us
  transfers between devices with their start and end apart: 14, of which 8 were waited for; matrix products, arithmetic and copies ran while one was open for 0% of the time, Pallas kernels for 7%

profile of v4, /device:TPU:1, one launch (start us, length us, event | category | flops | bytes accessed | tf_op | source)
XLA Modules:
  0.0 123.4 jit_solution(4445313834965307119)
XLA Ops:
  2.3 9.1 %all-to-all-start = ((bf16[8,128,256]{2,1,0:T(8,128)(2,1)}), bf16[8,128,256]{2,1,0:T(8,128)(2,1)S(1)}, u32[]{:S(2)}, u32[]{:S(2)}) async-start(bf16[8,128,256]{2,1,0:T(8,128)(2,1)} %pad_maximum_fusion), calls=%async_computation | async-start | bytes 1048576 | tf_op jit(solution)/shard_map/all_to_all | solution.py:369
  11.5 2.8 %collective-permute-start.2 = (bf16[128,256]{1,0:T(8,128)(2,1)S(1)}, bf16[128,256]{1,0:T(8,128)(2,1)S(1)}, u32[]{:S(2)}, u32[]{:S(2)}) collective-permute-start(bf16[128,256]{1,0:T(8,128)(2,1)S(1)} %constant_dynamic-update-slice_fusion), channel_id=1, source_target_pairs={{0,3},{1,0},{2,1},{3,2},{4,7},{5,4},{6,5},{7,6},{8,11},{9,8},{10,9... | collective-permute-start | bytes 196616 | tf_op jit(solution)/shard_map/ppermute | solution.py:388
  15.6 3.6 %collective-permute-done.1 = bf16[128,256]{1,0:T(8,128)(2,1)S(1)} collective-permute-done((bf16[128,256]{1,0:T(8,128)(2,1)S(1)}, bf16[128,256]{1,0:T(8,128)(2,1)S(1)}, u32[]{:S(2)}, u32[]{:S(2)}) %collective-permute-start.1) | collective-permute-done | bytes 65568 | tf_op jit(solution)/shard_map/ppermute | solution.py:388
  19.9 1.3 %collective-permute-start.3 = (bf16[4,128,256]{2,1,0:T(8,128)(2,1)S(1)}, bf16[4,128,256]{2,1,0:T(8,128)(2,1)S(1)}, u32[]{:S(2)}, u32[]{:S(2)}) collective-permute-start(bf16[4,128,256]{2,1,0:T(8,128)(2,1)S(1)} %pad_maximum_fusion.1.near), channel_id=1, source_target_pairs={{0,4},{4,0},{1,5},{5,1},{2,6},{6,2},{3,7},{7,3},{8,12},{12,8},{9,1... | collective-permute-start | bytes 786440 | tf_op jit(solution)/shard_map/ppermute | solution.py:402
  21.2 2.4 %collective-permute-start.4 = (bf16[4,128,256]{2,1,0:T(8,128)(2,1)S(1)}, bf16[4,128,256]{2,1,0:T(8,128)(2,1)S(1)}, u32[]{:S(2)}, u32[]{:S(2)}) collective-permute-start(bf16[4,128,256]{2,1,0:T(8,128)(2,1)S(1)} %pad_maximum_fusion.1.near), channel_id=1, source_target_pairs={{0,8},{8,0},{1,9},{9,1},{2,10},{10,2},{3,11},{11,3},{4,12},{12,4},... | collective-permute-start | bytes 786440 | tf_op jit(solution)/shard_map/ppermute | solution.py:380
  23.6 2.1 %collective-permute-done.3.across = bf16[4,128,256]{2,1,0:T(8,128)(2,1)S(1)} collective-permute-done((bf16[4,128,256]{2,1,0:T(8,128)(2,1)S(1)}, bf16[4,128,256]{2,1,0:T(8,128)(2,1)S(1)}, u32[]{:S(2)}, u32[]{:S(2)}) %collective-permute-start.3) | collective-permute-done | bytes 262176 | tf_op jit(solution)/shard_map/ppermute | solution.py:402
  25.7 3.0 %collective-permute-start.5 = (bf16[4,128,256]{2,1,0:T(8,128)(2,1)S(1)}, bf16[4,128,256]{2,1,0:T(8,128)(2,1)S(1)}, u32[]{:S(2)}, u32[]{:S(2)}) collective-permute-start(bf16[4,128,256]{2,1,0:T(8,128)(2,1)S(1)} %collective-permute-done.3.across), channel_id=1, source_target_pairs={{0,8},{8,0},{1,9},{9,1},{2,10},{10,2},{3,11},{11,3},{4,12},{12,4},... | collective-permute-start | bytes 786440 | tf_op jit(solution)/shard_map/ppermute | solution.py:380
  29.4 2.6 %collective-permute-start.6 = (bf16[8,64,256]{2,1,0:T(8,128)(2,1)S(1)}, bf16[8,64,256]{2,1,0:T(8,128)(2,1)S(1)}, u32[]{:S(2)}, u32[]{:S(2)}) collective-permute-start(bf16[8,64,256]{2,1,0:T(8,128)(2,1)S(1)} %slice.8), channel_id=1, source_target_pairs={{0,132},{4,128},{128,4},{132,0},{1,133},{5,129},{129,5},{133,1},{2... | collective-permute-start | bytes 786440 | tf_op jit(solution)/shard_map/ppermute | solution.py:384
  33.4 4.7 %collective-permute-done.6.c_phrases = bf16[8,64,256]{2,1,0:T(8,128)(2,1)S(1)} collective-permute-done((bf16[8,64,256]{2,1,0:T(8,128)(2,1)S(1)}, bf16[8,64,256]{2,1,0:T(8,128)(2,1)S(1)}, u32[]{:S(2)}, u32[]{:S(2)}) %collective-permute-start.6) | collective-permute-done | bytes 262176 | tf_op jit(solution)/shard_map/ppermute | solution.py:384
  38.1 1.6 %shard_map.50 = f32[16,8,128]{2,1,0:T(8,128)} custom-call(bf16[8,128,256]{2,1,0:T(8,128)(2,1)S(1)} %get-tuple-element.44.r_own, bf16[8,128,256]{2,1,0:T(8,128)(2,1)S(1)} %get-tuple-element.45.r_other, bf16[8,64,256]{2,1,0:T(8,128)(2,1)S(1)} %collective-permute-done.6.c_phrases, f32[8,128]{1,0:T(8,128)S(1)} %get-tuple-element.43.partial), custom_call_target="tpu_custom_call" | custom-call | flops 536870912 | bytes 2097152 | tf_op jit(solution)/shard_map/pallas_call | solution.py:354
  39.7 6.8 %all-to-all-start.1 = ((f32[16,8,128]{2,1,0:T(8,128)}), f32[16,8,128]{2,1,0:T(8,128)S(1)}, u32[]{:S(2)}, u32[]{:S(2)}) async-start(f32[16,8,128]{2,1,0:T(8,128)} %shard_map.50), calls=%async_computation.1 | async-start | bytes 131072 | tf_op jit(solution)/shard_map/all_to_all | solution.py:369
  46.4 3.2 %shard_map.51 = (f32[16,128]{1,0:T(8,128)S(1)}, f32[32,128]{1,0:T(8,128)S(1)}, bf16[8,128,256]{2,1,0:T(8,128)(2,1)S(1)}) custom-call(bf16[8,128,256]{2,1,0:T(8,128)(2,1)S(1)} %get-tuple-element.44.r_own, bf16[8,128,256]{2,1,0:T(8,128)(2,1)S(1)} %get-tuple-element.45.r_other, bf16[8,128,256]{2,1,0:T(8,128)(2,1)S(1)} %all-to-all-done.c_own, ...), custom_call_target="tpu_custom_call" | custom-call | flops 1073741824 | bytes 2097152 | tf_op jit(solution)/shard_map/pallas_call | solution.py:354
  49.6 2.7 %all-to-all-done.1.got = f32[16,8,128]{2,1,0:T(8,128)S(1)} async-done(((f32[16,8,128]{2,1,0:T(8,128)}), f32[16,8,128]{2,1,0:T(8,128)S(1)}, u32[]{:S(2)}, u32[]{:S(2)}) %all-to-all-start.1) | async-done | bytes 65568 | tf_op jit(solution)/shard_map/all_to_all | solution.py:369
  52.3 1.5 %shard_map.52 = (f32[16,24,128]{2,1,0:T(8,128)S(1)}, f32[8,128]{1,0:T(8,128)S(1)}) custom-call(bf16[8,128,256]{2,1,0:T(8,128)(2,1)S(1)} %get-tuple-element.44.r_own, bf16[8,128,256]{2,1,0:T(8,128)(2,1)S(1)} %get-tuple-element.45.r_other, bf16[8,128,256]{2,1,0:T(8,128)(2,1)S(1)} %all-to-all-done.c_own, bf16[8,128,256]{2,1,0:T(8,128)(2,1)S(1)} %get-tuple-element.49.c_other, ...), custom_call_target="tpu_custom_call" | custom-call | flops 536870912 | bytes 2097152 | tf_op jit(solution)/shard_map/pallas_call | solution.py:354
  53.7 14.4 %all_to_all.30.got = f32[16,24,128]{2,1,0:T(8,128)S(1)} all-to-all(f32[16,24,128]{2,1,0:T(8,128)S(1)} %get-tuple-element.54), channel_id=1, replica_groups={{0,16,32,48,64,80,96,112,132,148,164,180,196,212,228,244},{4,20,36,52,6..., dimensions={0} | all-to-all | bytes 393216 | tf_op jit(solution)/shard_map/all_to_all | solution.py:369
  68.2 2.4 %shard_map.53 = (f32[16,32,128]{2,1,0:T(8,128)S(1)}, f32[8,128]{1,0:T(8,128)S(1)}) custom-call(bf16[8,128,256]{2,1,0:T(8,128)(2,1)S(1)} %get-tuple-element.44.r_own, bf16[8,128,256]{2,1,0:T(8,128)(2,1)S(1)} %get-tuple-element.45.r_other, bf16[8,128,256]{2,1,0:T(8,128)(2,1)S(1)} %all-to-all-done.c_own, bf16[8,128,256]{2,1,0:T(8,128)(2,1)S(1)} %get-tuple-element.49.c_other, ...), custom_call_target="tpu_custom_call" | custom-call | flops 1610612736 | bytes 2097152 | tf_op jit(solution)/shard_map/pallas_call | solution.py:354
  70.6 12.7 %all_to_all.31.got = f32[16,32,128]{2,1,0:T(8,128)S(1)} all-to-all(f32[16,32,128]{2,1,0:T(8,128)S(1)} %get-tuple-element.56), channel_id=1, replica_groups=mesh['xh'=2,'z'=8,'core'=2,'xl'=2,'y'=4] {'core','xl','y'}, dimensions={0} | all-to-all | bytes 524288 | tf_op jit(solution)/shard_map/all_to_all | solution.py:369
  83.3 0.9 shard_map.54
  84.2 12.3 %all_to_all.32.got = f32[16,16,128]{2,1,0:T(8,128)S(1)} all-to-all(f32[16,16,128]{2,1,0:T(8,128)S(1)} %get-tuple-element.58), channel_id=1, replica_groups={{0,16,32,48,64,80,96,112,132,148,164,180,196,212,228,244},{4,20,36,52,6..., dimensions={0} | all-to-all | bytes 262144 | tf_op jit(solution)/shard_map/all_to_all | solution.py:369
  96.6 2.6 %shard_map.55 = (f32[8,64,256]{2,1,0:T(8,128)S(1)}, f32[8,64,256]{2,1,0:T(8,128)S(1)}, f32[16,128]{1,0:T(8,128)S(1)}, f32[64,256]{1,0:T(8,128)S(1)}, f32[16,128]{1,0:T(8,128)S(1)}) custom-call(bf16[8,128,256]{2,1,0:T(8,128)(2,1)S(1)} %get-tuple-element.44.r_own, bf16[8,128,256]{2,1,0:T(8,128)(2,1)S(1)} %get-tuple-element.45.r_other, ...), custom_call_target="tpu_custom_call" | custom-call | flops 1073741824 | bytes 2097152 | tf_op jit(solution)/shard_map/pallas_call | solution.py:354
  99.1 2.3 %collective-permute-start.8 = (f32[8,64,256]{2,1,0:T(8,128)S(1)}, f32[8,64,256]{2,1,0:T(8,128)S(1)}, u32[]{:S(2)}, u32[]{:S(2)}) collective-permute-start(f32[8,64,256]{2,1,0:T(8,128)S(1)} %get-tuple-element.60), channel_id=1, source_target_pairs={{0,8},{8,0},{1,9},{9,1},{2,10},{10,2},{3,11},{11,3},{4,12},{12,4},... | collective-permute-start | bytes 1572872 | tf_op jit(solution)/shard_map/ppermute | solution.py:380
  101.4 2.6 %shard_map.56 = (f32[8,64,256]{2,1,0:T(8,128)S(1)}, f32[8,64,256]{2,1,0:T(8,128)S(1)}, f32[8,64,256]{2,1,0:T(8,128)S(1)}, f32[8,64,256]{2,1,0:T(8,128)S(1)}) custom-call(bf16[8,128,256]{2,1,0:T(8,128)(2,1)S(1)} %get-tuple-element.44.r_own, bf16[8,128,256]{2,1,0:T(8,128)(2,1)S(1)} %get-tuple-element.45.r_other, bf16[8,128,256]{2,1,0:T(8,128)(2,1)S(1)} %all-to-all-done.c_own, ...), custom_call_target="tpu_custom_call" | custom-call | flops 1073741824 | bytes 2097152 | tf_op jit(solution)/shard_map/pallas_call | solution.py:354
  104.6 2.1 %collective-permute-done.11.sum_back = f32[16,128]{1,0:T(8,128)S(1)} collective-permute-done((f32[16,128]{1,0:T(8,128)S(1)}, f32[16,128]{1,0:T(8,128)S(1)}, u32[]{:S(2)}, u32[]{:S(2)}) %collective-permute-start.11) | collective-permute-done | bytes 8224 | tf_op jit(solution)/shard_map/ppermute | solution.py:380
  106.9 15.7 %all_to_all.33.parts = bf16[8,208,256]{2,1,0:T(8,128)(2,1)S(1)} all-to-all(bf16[8,208,256]{2,1,0:T(8,128)(2,1)S(1)} %shard_map.57), channel_id=1, replica_groups=mesh['xh'=2,'z'=8,'core'=2,'xl'=2,'y'=4] {'xl','y'}, dimensions={0} | all-to-all | bytes 1703936 | tf_op jit(solution)/shard_map/all_to_all | solution.py:369
  (30 shorter events, 7.5 us)
Async XLA Ops:
  0.6 0.8 copy-start.1
  2.3 9.2 %copy-start = (bf16[64,256]{1,0:T(8,128)(2,1)S(1)}, bf16[64,256]{1,0:T(8,128)(2,1)}, u32[]{:S(2)}) copy-start(bf16[64,256]{1,0:T(8,128)(2,1)} %param.2) | copy-start | bytes 98308
  2.3 27.1 %all-to-all-start = ((bf16[8,128,256]{2,1,0:T(8,128)(2,1)}), bf16[8,128,256]{2,1,0:T(8,128)(2,1)S(1)}, u32[]{:S(2)}, u32[]{:S(2)}) async-start(bf16[8,128,256]{2,1,0:T(8,128)(2,1)} %pad_maximum_fusion), calls=%async_computation | async-start | bytes 1048576 | tf_op jit(solution)/shard_map/all_to_all | solution.py:369
  11.5 4.1 %collective-permute-start.2 = (bf16[128,256]{1,0:T(8,128)(2,1)S(1)}, bf16[128,256]{1,0:T(8,128)(2,1)S(1)}, u32[]{:S(2)}, u32[]{:S(2)}) collective-permute-start(bf16[128,256]{1,0:T(8,128)(2,1)S(1)} %constant_dynamic-update-slice_fusion), channel_id=1, source_target_pairs={{0,3},{1,0},{2,1},{3,2},{4,7},{5,4},{6,5},{7,6},{8,11},{9,8},{10,9... | collective-permute-start | bytes 196616 | tf_op jit(solution)/shard_map/ppermute | solution.py:388
  14.3 4.9 %collective-permute-start.1 = (bf16[128,256]{1,0:T(8,128)(2,1)S(1)}, bf16[128,256]{1,0:T(8,128)(2,1)S(1)}, u32[]{:S(2)}, u32[]{:S(2)}) collective-permute-start(bf16[128,256]{1,0:T(8,128)(2,1)S(1)} %constant_dynamic-update-slice_fusion), channel_id=1, source_target_pairs={{0,2},{1,3},{2,0},{3,1},{4,6},{5,7},{6,4},{7,5},{8,10},{9,11},{10,... | collective-permute-start | bytes 196616 | tf_op jit(solution)/shard_map/ppermute | solution.py:388
  14.6 5.3 %collective-permute-start = (bf16[128,256]{1,0:T(8,128)(2,1)S(1)}, bf16[128,256]{1,0:T(8,128)(2,1)S(1)}, u32[]{:S(2)}, u32[]{:S(2)}) collective-permute-start(bf16[128,256]{1,0:T(8,128)(2,1)S(1)} %constant_dynamic-update-slice_fusion), channel_id=1, source_target_pairs={{0,1},{1,2},{2,3},{3,0},{4,5},{5,6},{6,7},{7,4},{8,9},{9,10},{10,1... | collective-permute-start | bytes 196616 | tf_op jit(solution)/shard_map/ppermute | solution.py:388
  19.9 5.8 %collective-permute-start.3 = (bf16[4,128,256]{2,1,0:T(8,128)(2,1)S(1)}, bf16[4,128,256]{2,1,0:T(8,128)(2,1)S(1)}, u32[]{:S(2)}, u32[]{:S(2)}) collective-permute-start(bf16[4,128,256]{2,1,0:T(8,128)(2,1)S(1)} %pad_maximum_fusion.1.near), channel_id=1, source_target_pairs={{0,4},{4,0},{1,5},{5,1},{2,6},{6,2},{3,7},{7,3},{8,12},{12,8},{9,1... | collective-permute-start | bytes 786440 | tf_op jit(solution)/shard_map/ppermute | solution.py:402
  21.2 10.7 %collective-permute-start.4 = (bf16[4,128,256]{2,1,0:T(8,128)(2,1)S(1)}, bf16[4,128,256]{2,1,0:T(8,128)(2,1)S(1)}, u32[]{:S(2)}, u32[]{:S(2)}) collective-permute-start(bf16[4,128,256]{2,1,0:T(8,128)(2,1)S(1)} %pad_maximum_fusion.1.near), channel_id=1, source_target_pairs={{0,8},{8,0},{1,9},{9,1},{2,10},{10,2},{3,11},{11,3},{4,12},{12,4},... | collective-permute-start | bytes 786440 | tf_op jit(solution)/shard_map/ppermute | solution.py:380
  25.7 6.3 %collective-permute-start.5 = (bf16[4,128,256]{2,1,0:T(8,128)(2,1)S(1)}, bf16[4,128,256]{2,1,0:T(8,128)(2,1)S(1)}, u32[]{:S(2)}, u32[]{:S(2)}) collective-permute-start(bf16[4,128,256]{2,1,0:T(8,128)(2,1)S(1)} %collective-permute-done.3.across), channel_id=1, source_target_pairs={{0,8},{8,0},{1,9},{9,1},{2,10},{10,2},{3,11},{11,3},{4,12},{12,4},... | collective-permute-start | bytes 786440 | tf_op jit(solution)/shard_map/ppermute | solution.py:380
  29.4 8.7 %collective-permute-start.6 = (bf16[8,64,256]{2,1,0:T(8,128)(2,1)S(1)}, bf16[8,64,256]{2,1,0:T(8,128)(2,1)S(1)}, u32[]{:S(2)}, u32[]{:S(2)}) collective-permute-start(bf16[8,64,256]{2,1,0:T(8,128)(2,1)S(1)} %slice.8), channel_id=1, source_target_pairs={{0,132},{4,128},{128,4},{132,0},{1,133},{5,129},{129,5},{133,1},{2... | collective-permute-start | bytes 786440 | tf_op jit(solution)/shard_map/ppermute | solution.py:384
  33.0 13.5 %collective-permute-start.7 = (bf16[8,64,256]{2,1,0:T(8,128)(2,1)S(1)}, bf16[8,64,256]{2,1,0:T(8,128)(2,1)S(1)}, u32[]{:S(2)}, u32[]{:S(2)}) collective-permute-start(bf16[8,64,256]{2,1,0:T(8,128)(2,1)S(1)} %slice.7), channel_id=1, source_target_pairs={{0,132},{4,128},{128,4},{132,0},{1,133},{5,129},{129,5},{133,1},{2... | collective-permute-start | bytes 786440 | tf_op jit(solution)/shard_map/ppermute | solution.py:384
  39.7 12.6 %all-to-all-start.1 = ((f32[16,8,128]{2,1,0:T(8,128)}), f32[16,8,128]{2,1,0:T(8,128)S(1)}, u32[]{:S(2)}, u32[]{:S(2)}) async-start(f32[16,8,128]{2,1,0:T(8,128)} %shard_map.50), calls=%async_computation.1 | async-start | bytes 131072 | tf_op jit(solution)/shard_map/all_to_all | solution.py:369
  99.1 7.6 %collective-permute-start.8 = (f32[8,64,256]{2,1,0:T(8,128)S(1)}, f32[8,64,256]{2,1,0:T(8,128)S(1)}, u32[]{:S(2)}, u32[]{:S(2)}) collective-permute-start(f32[8,64,256]{2,1,0:T(8,128)S(1)} %get-tuple-element.60), channel_id=1, source_target_pairs={{0,8},{8,0},{1,9},{9,1},{2,10},{10,2},{3,11},{11,3},{4,12},{12,4},... | collective-permute-start | bytes 1572872 | tf_op jit(solution)/shard_map/ppermute | solution.py:380
  103.9 2.8 %collective-permute-start.9 = (f32[8,64,256]{2,1,0:T(8,128)S(1)}, f32[8,64,256]{2,1,0:T(8,128)S(1)}, u32[]{:S(2)}, u32[]{:S(2)}) collective-permute-start(f32[8,64,256]{2,1,0:T(8,128)S(1)} %get-tuple-element.63), channel_id=1, source_target_pairs={{0,8},{8,0},{1,9},{9,1},{2,10},{10,2},{3,11},{11,3},{4,12},{12,4},... | collective-permute-start | bytes 1572872 | tf_op jit(solution)/shard_map/ppermute | solution.py:380
  104.1 2.7 %collective-permute-start.10 = (f32[8,64,256]{2,1,0:T(8,128)S(1)}, f32[8,64,256]{2,1,0:T(8,128)S(1)}, u32[]{:S(2)}, u32[]{:S(2)}) collective-permute-start(f32[8,64,256]{2,1,0:T(8,128)S(1)} %get-tuple-element.65), channel_id=1, source_target_pairs={{0,8},{8,0},{1,9},{9,1},{2,10},{10,2},{3,11},{11,3},{4,12},{12,4},... | collective-permute-start | bytes 1572872 | tf_op jit(solution)/shard_map/ppermute | solution.py:380
  104.5 2.2 %collective-permute-start.11 = (f32[16,128]{1,0:T(8,128)S(1)}, f32[16,128]{1,0:T(8,128)S(1)}, u32[]{:S(2)}, u32[]{:S(2)}) collective-permute-start(f32[16,128]{1,0:T(8,128)S(1)} %get-tuple-element.66.sums), channel_id=1, source_target_pairs={{0,8},{8,0},{1,9},{9,1},{2,10},{10,2},{3,11},{11,3},{4,12},{12,4},... | collective-permute-start | bytes 24584 | tf_op jit(solution)/shard_map/ppermute | solution.py:380

commit v5 on v4

--- a/solution.py
+++ b/solution.py
@@ -175,7 +175,12 @@
     message_ref[...] = jnp.broadcast_to(rows[None], message_ref.shape)
 
 
-def first_half(near, across, near_far, across_far, c_own, r_own, r_other, partial):
+def spread(own, paired, copies):
+    copies[:, 0 : 2 * OWN, :] = jnp.broadcast_to(own[...][None], (8, 2 * OWN, WIDTH))
+    copies[:, 2 * OWN :, :] = jnp.broadcast_to(paired[...][None], (8, OWN, WIDTH))
+
+
+def first_rows(near, across, near_far, across_far, c_own, message, r_own, r_other):
     side, spot = lax.axis_index("xl"), lax.axis_index("y")
     for step in range(4):
         source = lax.rem(spot + 4 - step, 4)
@@ -183,21 +188,13 @@
         r_other[pl.ds(side * 4 + source, 1)] = near_far[step : step + 1]
         r_own[pl.ds((1 - side) * 4 + source, 1)] = across[step : step + 1]
         r_other[pl.ds((1 - side) * 4 + source, 1)] = across_far[step : step + 1]
-    y_col = half_rows(c_own, 1)
-    partial[...] = peak_pass(y_col, r_own, r_other, 0, -norms_sub(y_col))
-
-
-def first_rows(r_own, r_other, c_phrases, partial, message):
-    y_col = c_phrases[...].reshape(HALF, WIDTH)
-    rest = peak_pass(y_col, r_own, r_other, 0, -norms_sub(y_col))
-    peak = jnp.maximum(rest, partial[...])
-    mass = jnp.exp2(rest - peak) + jnp.exp2(partial[...] - peak)
-    send_all(message, peak + log2(mass))
-
-
-def first_self(r_own, r_other, c_own, c_phrases, c_regions, sums, norms, c_other):
+    y_col = jnp.concatenate([half_rows(c_own, 1), half_rows(c_own, 2)], axis=0)
+    send_all(message, peak_pass(y_col, r_own, r_other, 0, -norms_sub(y_col)))
+
+
+def first_self(r_own, r_other, c_own, c_regions, sums, norms, c_other):
     c_other[:, 0:OWN, :] = c_regions[...]
-    c_other[:, OWN : 2 * OWN, :] = c_phrases[...]
+    c_other[:, OWN : 2 * OWN, :] = c_own[:, 2 * OWN : 3 * OWN, :]
     x_row = block_rows(r_own, r_other, 0)
     y_row = block_rows(r_own, r_other, 1)
     x_norm_col = norms_lane(block_rows(c_own, c_other, 0))
@@ -278,56 +275,44 @@
     return term(rows, part, *cross) - term(rows, part, *self_)
 
 
-def region_gradients(
-    r_own, r_other, c_own, c_other, shifts, h_in, got, kept, sent, cols, scale, sums
-):
+def half_gradients(ref, part, c_own, c_other, shifts, cols, out):
+    x_col = block_rows(c_own, c_other, 0)
+    y_col = block_rows(c_own, c_other, 1)
+    u_sub, p_sub, q_sub, h_sub = [
+        dense_to_sub(shifts[8 * k : 8 * k + 8, :]) for k in range(4)
+    ]
+    h_lane, u_lane, p_lane, q_lane = [
+        dense_to_lane(cols[8 * k : 8 * k + 8, :]) - LOG_COUNT for k in range(4)
+    ]
+    rows = half_rows(ref, 0)
+    out[:, 0:OWN, :] = gradient(rows, part, (y_col, u_sub, h_lane), (x_col, p_sub, p_lane))
+    rows = half_rows(ref, 1)
+    cross = term(rows, part, x_col, h_sub, u_lane)
+    out[:, 2 * OWN : 3 * OWN, :] = cross
+    out[:, OWN : 2 * OWN, :] = cross - term(rows, part, y_col, q_sub, q_lane)
+
+
+def other_gradients(r_other, c_own, c_other, shifts, h_in, got, sent, cols, scale, sums):
     far = lax.axis_index("xh")
     change = LOG_COUNT - log2(join_sums(got, far, 0))
     h = h_in[...] + change
     u_col, p_col = unpair(*piggy_rows(got, 8, far))
     q_col, unused = unpair(*piggy_rows(got, 9, far))
-    cols[...] = jnp.concatenate([u_col, q_col], axis=0) - LOG_COUNT
+    cols[...] = jnp.concatenate([h, u_col, p_col, q_col], axis=0)
     own_change = jnp.broadcast_to(own_piece(change, lax.axis_index("z")), (128, 128)).T
     scale[...] = widen(jnp.exp2(own_change[0:OWN, :]), WIDTH)
     total = jnp.sum(got[:, 8:16, :], axis=0)
     part = jnp.broadcast_to(canonical_sum(h), (8, 128))
     sums[...] = jnp.concatenate([jnp.broadcast_to(total[2:3], (8, 128)), part], axis=0)
-    h_lane = dense_to_lane(h) - LOG_COUNT
-    cross = (block_rows(c_own, c_other, 1), dense_to_sub(shifts[0:8, :]), h_lane)
-    p_lane = dense_to_lane(p_col) - LOG_COUNT
-    self_ = (block_rows(c_own, c_other, 0), dense_to_sub(shifts[8:16, :]), p_lane)
-    sent[...] = gradient(half_rows(r_other, 0), SECOND, cross, self_)
-    kept[...] = gradient(half_rows(r_own, 0), FIRST, cross, self_)
-
-
-def phrase_gradients(
-    r_own, r_other, c_own, c_other, shifts, cols, kept, sent, cross_kept, cross_sent
-):
-    cross = (
-        block_rows(c_own, c_other, 0),
-        dense_to_sub(shifts[24:32, :]),
-        dense_to_lane(cols[0:8, :]),
-    )
-    self_ = (
-        block_rows(c_own, c_other, 1),
-        dense_to_sub(shifts[16:24, :]),
-        dense_to_lane(cols[8:16, :]),
-    )
-    for ref, part, out, cross_out in (
-        (r_other, SECOND, sent, cross_sent),
-        (r_own, FIRST, kept, cross_kept),
-    ):
-        rows = half_rows(ref, 1)
-        cross_out[...] = term(rows, part, *cross)
-        out[...] = cross_out[...] - term(rows, part, *self_)
-
-
-def join_gradients(
-    x_kept, x_back, y_kept, y_back, cross_kept, cross_back, sums, sum_back, out
-):
-    kept_back = ((x_kept, x_back), (y_kept, y_back), (cross_kept, cross_back))
-    for k, (kept, back) in enumerate(kept_back):
-        out[:, k * OWN : (k + 1) * OWN, :] = (kept[...] + back[...]).astype(out.dtype)
+    half_gradients(r_other, SECOND, c_own, c_other, shifts, cols, sent)
+
+
+def own_gradients(r_own, c_own, c_other, shifts, cols, kept):
+    half_gradients(r_own, FIRST, c_own, c_other, shifts, cols, kept)
+
+
+def join_gradients(kept, back, sums, sum_back, out):
+    out[:, 0 : 3 * OWN, :] = (kept[...] + back[...]).astype(out.dtype)
     part = jnp.broadcast_to(sums[8:9, :] + sum_back[8:9, :], (16, 128))
     high = part.astype(jnp.bfloat16)
     left = part - high.astype(jnp.float32)
@@ -391,13 +376,11 @@
 def on_device(regions, phrases):
     f32 = jnp.float32
     block = ((8, 2 * OWN, WIDTH), jnp.bfloat16)
-    spread = [jnp.broadcast_to(points[None], (8, OWN, WIDTH)) for points in (regions, phrases)]
-    copies, regions, phrases = lax.optimization_barrier(
-        (jnp.concatenate(spread, axis=1), regions, phrases)
-    )
     own = jnp.concatenate([regions, phrases], axis=0)
+    (copies,) = call(
+        spread, [((8, 3 * OWN, WIDTH), jnp.bfloat16)], 0, own, pair_swap(phrases)
+    )
     c_own = share(copies, ("z",))
-    c_phrases = pair_swap(c_own[:, OWN : 2 * OWN, :])
     near = jnp.stack([own] + [y_step(own, shift) for shift in (1, 2, 3)])
     across = lax.ppermute(near, "xl", [(0, 1), (1, 0)])
     near_far = core_swap(near)
@@ -406,20 +389,11 @@
     def message(rows):
         return ((16, rows, 128), f32)
 
-    r_own, r_other, partial = call(
-        first_half,
-        [block, block, ((8, 128), f32)],
-        1,
-        near,
-        across,
-        near_far,
-        across_far,
-        c_own,
-    )
-    partial, c_after = lax.optimization_barrier((partial, c_own))
-    c_regions = pair_swap(c_after[:, 0:OWN, :])
-    (sent,) = call(first_rows, [message(8)], 1, r_own, r_other, c_phrases, partial)
-    later, sent = lax.optimization_barrier(((r_own, r_other, c_own, c_phrases), sent))
+    sent, r_own, r_other = call(
+        first_rows, [message(8), block, block], 1, near, across, near_far, across_far, c_own
+    )
+    c_regions = pair_swap(c_own[:, 0:OWN, :])
+    later, sent = lax.optimization_barrier(((r_own, r_other, c_own), sent))
     got = share(sent, ROW_GROUP)
     sums, norms, c_other = call(
         first_self, [((16, 128), f32), ((32, 128), f32), block], 2, *later, c_regions
@@ -444,31 +418,24 @@
         got,
     )
     got = share_col(sent)
-    half = ((8, OWN, WIDTH), f32)
-    x_kept, x_away, cols, scale, sums = call(
-        region_gradients,
-        [half, half, ((16, 128), f32), ((OWN, WIDTH), f32), ((16, 128), f32)],
+    half = ((8, 3 * OWN, WIDTH), f32)
+    away, cols, scale, sums = call(
+        other_gradients,
+        [half, ((32, 128), f32), ((OWN, WIDTH), f32), ((16, 128), f32)],
         2,
-        *points,
+        *points[1:],
         shifts,
         h_first,
         got,
     )
-    x_back, sum_back = core_swap(x_away), core_swap(sums)
-    y_kept, y_away, cross_kept, cross_away = call(
-        phrase_gradients, [half] * 4, 2, *points, shifts, cols
-    )
-    y_back, cross_back = core_swap(y_away), core_swap(cross_away)
+    back, sum_back = core_swap(away), core_swap(sums)
+    (kept,) = call(own_gradients, [half], 2, r_own, c_own, c_other, shifts, cols)
     (joined,) = call(
         join_gradients,
         [((8, 3 * OWN + 16, WIDTH), jnp.bfloat16)],
         0,
-        x_kept,
-        x_back,
-        y_kept,
-        y_back,
-        cross_kept,
-        cross_back,
+        kept,
+        back,
         sums,
         sum_back,
     )

time: 124 us -> 120 us (0.968)
  waiting for transfers between devices: 16.8 us -> 12.8 us
  blocking collectives: 55.1 us -> 51.8 us
  starting transfers between devices: 32.4 us -> 35.7 us
    ppermute x2, waiting for transfers between devices: 4.67 us -> 0.01 us  [pair_swap(): return lax.ppermute(values, ('xh', 'xl'), [(0, 3), (1, 2), (2, 1), (3, 0)])]
    all_to_all x4, blocking collectives: 55.1 us -> 51.8 us  [share(): lax.all_to_all(message, axes, 0, 0, tiled=True, axis_index_groups=groups)]
    all_to_all x2, waiting for transfers between devices: 3.34 us -> 6.44 us  [share(): lax.all_to_all(message, axes, 0, 0, tiled=True, axis_index_groups=groups)]
    ppermute x2, starting transfers between devices: 3.05 us -> 5.96 us  [pair_swap(): return lax.ppermute(values, ('xh', 'xl'), [(0, 3), (1, 2), (2, 1), (3, 0)])]
    ppermute x6 -> x4, starting transfers between devices: 8.34 us -> 10.5 us  [core_swap(): return lax.ppermute(values, 'core', [(0, 1), (1, 0)])]
    ppermute x6 -> x4, waiting for transfers between devices: 2.07 us -> 0.4 us  [core_swap(): return lax.ppermute(values, 'core', [(0, 1), (1, 0)])]
  transfers between devices with their start and end apart: 14 -> 12, of which waited for: 8 -> 7; matrix products, arithmetic and copies ran while one was open for 0% -> 1% of each run, Pallas kernels for 7% -> 7%
where the time goes in v5:
time: 120 us
  blocking collectives  51.8 us (43%)
  starting transfers between devices  35.7 us (30%)
  Pallas kernels  17.4 us (14%)
  waiting for transfers between devices  12.8 us (11%)
  local copies, waits for them, and re-layouts  1.54 us (1%)
    all_to_all x4, blocking collectives, share(): lax.all_to_all(message, axes, 0, 0, tiled=True, axis_index_groups=groups)  51.8 us
    pallas_call x10, Pallas kernels, call(): pl.pallas_call(body, out_shape=shapes, in_specs=specs, out_specs=[pl.Bloc...  17.4 us
    all_to_all x2, starting transfers between devices, share(): lax.all_to_all(message, axes, 0, 0, tiled=True, axis_index_groups=groups)  15.4 us
    ppermute x4, starting transfers between devices, core_swap(): return lax.ppermute(values, 'core', [(0, 1), (1, 0)])  10.5 us
    all_to_all x2, waiting for transfers between devices, share(): lax.all_to_all(message, axes, 0, 0, tiled=True, axis_index_groups=groups)  6.44 us
    ppermute x2, starting transfers between devices, pair_swap(): return lax.ppermute(values, ('xh', 'xl'), [(0, 3), (1, 2), (2, 1), (3, 0)])  5.96 us
    ppermute x3, waiting for transfers between devices, y_step(): return lax.ppermute(values, 'y', [(y, (y + shift) % 4) for y in range(4)])  4.28 us
    ppermute x3, starting transfers between devices, y_step(): return lax.ppermute(values, 'y', [(y, (y + shift) % 4) for y in range(4)])  3.77 us
  transfers between devices with their start and end apart: 12, of which 7 were waited for; matrix products, arithmetic and copies ran while one was open for 1% of the time, Pallas kernels for 7%

profile of v5, /device:TPU:1, one launch (start us, length us, event | category | flops | bytes accessed | tf_op | source)
XLA Modules:
  0.0 119.9 jit_solution(5889359671887092378)
XLA Ops:
  0.6 3.4 %collective-permute-start.6 = (bf16[64,256]{1,0:T(8,128)(2,1)}, bf16[64,256]{1,0:T(8,128)(2,1)S(1)}, u32[]{:S(2)}, u32[]{:S(2)}) collective-permute-start(bf16[64,256]{1,0:T(8,128)(2,1)} %param.3), channel_id=1, source_target_pairs={{0,132},{4,128},{128,4},{132,0},{1,133},{5,129},{129,5},{133,1},{2... | collective-permute-start | bytes 98312 | tf_op jit(solution)/shard_map/ppermute | solution.py:369
  5.5 0.9 shard_map.49
  6.5 8.4 %all-to-all-start = ((bf16[8,192,256]{2,1,0:T(8,128)(2,1)}), bf16[8,192,256]{2,1,0:T(8,128)(2,1)S(1)}, u32[]{:S(2)}, u32[]{:S(2)}) async-start(bf16[8,192,256]{2,1,0:T(8,128)(2,1)} %shard_map.49), calls=%async_computation | async-start | bytes 1572864 | tf_op jit(solution)/shard_map/all_to_all | solution.py:354
  14.9 2.7 %collective-permute-start.2 = (bf16[128,256]{1,0:T(8,128)(2,1)S(1)}, bf16[128,256]{1,0:T(8,128)(2,1)S(1)}, u32[]{:S(2)}, u32[]{:S(2)}) collective-permute-start(bf16[128,256]{1,0:T(8,128)(2,1)S(1)} %constant_dynamic-update-slice_fusion.own), channel_id=1, source_target_pairs={{0,3},{1,0},{2,1},{3,2},{4,7},{5,4},{6,5},{7,6},{8,11},{9,8},{10,9... | collective-permute-start | bytes 196616 | tf_op jit(solution)/shard_map/ppermute | solution.py:373
  18.9 3.4 %collective-permute-done.1 = bf16[128,256]{1,0:T(8,128)(2,1)S(1)} collective-permute-done((bf16[128,256]{1,0:T(8,128)(2,1)S(1)}, bf16[128,256]{1,0:T(8,128)(2,1)S(1)}, u32[]{:S(2)}, u32[]{:S(2)}) %collective-permute-start.1) | collective-permute-done | bytes 65568 | tf_op jit(solution)/shard_map/ppermute | solution.py:373
  23.1 3.8 %collective-permute-start.4 = (bf16[4,128,256]{2,1,0:T(8,128)(2,1)S(1)}, bf16[4,128,256]{2,1,0:T(8,128)(2,1)S(1)}, u32[]{:S(2)}, u32[]{:S(2)}) collective-permute-start(bf16[4,128,256]{2,1,0:T(8,128)(2,1)S(1)} %pad_maximum_fusion.near), channel_id=1, source_target_pairs={{0,8},{8,0},{1,9},{9,1},{2,10},{10,2},{3,11},{11,3},{4,12},{12,4},... | collective-permute-start | bytes 786440 | tf_op jit(solution)/shard_map/ppermute | solution.py:365
  26.9 1.7 %collective-permute-done.3.across = bf16[4,128,256]{2,1,0:T(8,128)(2,1)S(1)} collective-permute-done((bf16[4,128,256]{2,1,0:T(8,128)(2,1)S(1)}, bf16[4,128,256]{2,1,0:T(8,128)(2,1)S(1)}, u32[]{:S(2)}, u32[]{:S(2)}) %collective-permute-start.3) | collective-permute-done | bytes 262176 | tf_op jit(solution)/shard_map/ppermute | solution.py:385
  28.6 4.4 %collective-permute-start.5 = (bf16[4,128,256]{2,1,0:T(8,128)(2,1)S(1)}, bf16[4,128,256]{2,1,0:T(8,128)(2,1)S(1)}, u32[]{:S(2)}, u32[]{:S(2)}) collective-permute-start(bf16[4,128,256]{2,1,0:T(8,128)(2,1)S(1)} %collective-permute-done.3.across), channel_id=1, source_target_pairs={{0,8},{8,0},{1,9},{9,1},{2,10},{10,2},{3,11},{11,3},{4,12},{12,4},... | collective-permute-start | bytes 786440 | tf_op jit(solution)/shard_map/ppermute | solution.py:365
  32.9 3.7 %all-to-all-done.c_own = bf16[8,192,256]{2,1,0:T(8,128)(2,1)S(1)} async-done(((bf16[8,192,256]{2,1,0:T(8,128)(2,1)}), bf16[8,192,256]{2,1,0:T(8,128)(2,1)S(1)}, u32[]{:S(2)}, u32[]{:S(2)}) %all-to-all-start) | async-done | bytes 786464 | tf_op jit(solution)/shard_map/all_to_all | solution.py:354
  36.7 2.6 %collective-permute-start.7 = (bf16[8,64,256]{2,1,0:T(8,128)(2,1)S(1)}, bf16[8,64,256]{2,1,0:T(8,128)(2,1)S(1)}, u32[]{:S(2)}, u32[]{:S(2)}) collective-permute-start(bf16[8,64,256]{2,1,0:T(8,128)(2,1)S(1)} %slice.4), channel_id=1, source_target_pairs={{0,132},{4,128},{128,4},{132,0},{1,133},{5,129},{129,5},{133,1},{2... | collective-permute-start | bytes 786440 | tf_op jit(solution)/shard_map/ppermute | solution.py:369
  39.3 2.3 %shard_map.50 = (f32[16,8,128]{2,1,0:T(8,128)}, bf16[8,128,256]{2,1,0:T(8,128)(2,1)S(1)}, bf16[8,128,256]{2,1,0:T(8,128)(2,1)S(1)}) custom-call(bf16[4,128,256]{2,1,0:T(8,128)(2,1)S(1)} %pad_maximum_fusion.near, bf16[4,128,256]{2,1,0:T(8,128)(2,1)S(1)} %collective-permute-done.3.across, bf16[4,128,256]{2,1,0:T(8,128)(2,1)S(1)} %collective-permute-done.4.near_far, ...), custom_call_target="tpu_custom_call" | custom-call | flops 536870912 | bytes 2097152 | tf_op jit(solution)/shard_map/pallas_call | solution.py:339
  41.6 7.0 %all-to-all-start.1 = ((f32[16,8,128]{2,1,0:T(8,128)}), f32[16,8,128]{2,1,0:T(8,128)S(1)}, u32[]{:S(2)}, u32[]{:S(2)}) async-start(f32[16,8,128]{2,1,0:T(8,128)} %get-tuple-element.35), calls=%async_computation.1 | async-start | bytes 131072 | tf_op jit(solution)/shard_map/all_to_all | solution.py:354
  48.6 3.2 %shard_map.51 = (f32[16,128]{1,0:T(8,128)S(1)}, f32[32,128]{1,0:T(8,128)S(1)}, bf16[8,128,256]{2,1,0:T(8,128)(2,1)S(1)}) custom-call(bf16[8,128,256]{2,1,0:T(8,128)(2,1)S(1)} %get-tuple-element.29.r_own, bf16[8,128,256]{2,1,0:T(8,128)(2,1)S(1)} %get-tuple-element.30.r_other, bf16[8,192,256]{2,1,0:T(8,128)(2,1)S(1)} %all-to-all-done.c_own, ...), custom_call_target="tpu_custom_call" | custom-call | flops 1073741824 | bytes 2097152 | tf_op jit(solution)/shard_map/pallas_call | solution.py:339
  51.8 2.7 %all-to-all-done.1.got = f32[16,8,128]{2,1,0:T(8,128)S(1)} async-done(((f32[16,8,128]{2,1,0:T(8,128)}), f32[16,8,128]{2,1,0:T(8,128)S(1)}, u32[]{:S(2)}, u32[]{:S(2)}) %all-to-all-start.1) | async-done | bytes 65568 | tf_op jit(solution)/shard_map/all_to_all | solution.py:354
  54.5 1.5 %shard_map.52 = (f32[16,24,128]{2,1,0:T(8,128)S(1)}, f32[8,128]{1,0:T(8,128)S(1)}) custom-call(bf16[8,128,256]{2,1,0:T(8,128)(2,1)S(1)} %get-tuple-element.29.r_own, bf16[8,128,256]{2,1,0:T(8,128)(2,1)S(1)} %get-tuple-element.30.r_other, bf16[8,192,256]{2,1,0:T(8,128)(2,1)S(1)} %all-to-all-done.c_own, bf16[8,128,256]{2,1,0:T(8,128)(2,1)S(1)} %get-tuple-element.32.c_other, ...), custom_call_target="tpu_custom_call" | custom-call | flops 536870912 | bytes 2097152 | tf_op jit(solution)/shard_map/pallas_call | solution.py:339
  55.9 11.5 %all_to_all.30.got = f32[16,24,128]{2,1,0:T(8,128)S(1)} all-to-all(f32[16,24,128]{2,1,0:T(8,128)S(1)} %get-tuple-element.37), channel_id=1, replica_groups={{0,16,32,48,64,80,96,112,132,148,164,180,196,212,228,244},{4,20,36,52,6..., dimensions={0} | all-to-all | bytes 393216 | tf_op jit(solution)/shard_map/all_to_all | solution.py:354
  67.4 2.4 %shard_map.53 = (f32[16,32,128]{2,1,0:T(8,128)S(1)}, f32[8,128]{1,0:T(8,128)S(1)}) custom-call(bf16[8,128,256]{2,1,0:T(8,128)(2,1)S(1)} %get-tuple-element.29.r_own, bf16[8,128,256]{2,1,0:T(8,128)(2,1)S(1)} %get-tuple-element.30.r_other, bf16[8,192,256]{2,1,0:T(8,128)(2,1)S(1)} %all-to-all-done.c_own, bf16[8,128,256]{2,1,0:T(8,128)(2,1)S(1)} %get-tuple-element.32.c_other, ...), custom_call_target="tpu_custom_call" | custom-call | flops 1610612736 | bytes 2097152 | tf_op jit(solution)/shard_map/pallas_call | solution.py:339
  69.9 12.1 %all_to_all.31.got = f32[16,32,128]{2,1,0:T(8,128)S(1)} all-to-all(f32[16,32,128]{2,1,0:T(8,128)S(1)} %get-tuple-element.39), channel_id=1, replica_groups=mesh['xh'=2,'z'=8,'core'=2,'xl'=2,'y'=4] {'core','xl','y'}, dimensions={0} | all-to-all | bytes 524288 | tf_op jit(solution)/shard_map/all_to_all | solution.py:354
  82.0 0.9 shard_map.54
  83.0 12.6 %all_to_all.32.got = f32[16,16,128]{2,1,0:T(8,128)S(1)} all-to-all(f32[16,16,128]{2,1,0:T(8,128)S(1)} %get-tuple-element.41), channel_id=1, replica_groups={{0,16,32,48,64,80,96,112,132,148,164,180,196,212,228,244},{4,20,36,52,6..., dimensions={0} | all-to-all | bytes 262144 | tf_op jit(solution)/shard_map/all_to_all | solution.py:354
  95.5 2.6 %shard_map.55 = (f32[8,192,256]{2,1,0:T(8,128)S(1)}, f32[32,128]{1,0:T(8,128)S(1)}, f32[64,256]{1,0:T(8,128)S(1)}, f32[16,128]{1,0:T(8,128)S(1)}) custom-call(bf16[8,128,256]{2,1,0:T(8,128)(2,1)S(1)} %get-tuple-element.30.r_other, bf16[8,192,256]{2,1,0:T(8,128)(2,1)S(1)} %all-to-all-done.c_own, bf16[8,128,256]{2,1,0:T(8,128)(2,1)S(1)} %get-tuple-element.32.c_other, ...), custom_call_target="tpu_custom_call" | custom-call | flops 1073741824 | bytes 2097152 | tf_op jit(solution)/shard_map/pallas_call | solution.py:339
  98.1 2.2 %collective-permute-start.8 = (f32[8,192,256]{2,1,0:T(8,128)S(1)}, f32[8,192,256]{2,1,0:T(8,128)S(1)}, u32[]{:S(2)}, u32[]{:S(2)}) collective-permute-start(f32[8,192,256]{2,1,0:T(8,128)S(1)} %get-tuple-element.43), channel_id=1, source_target_pairs={{0,8},{8,0},{1,9},{9,1},{2,10},{10,2},{3,11},{11,3},{4,12},{12,4},... | collective-permute-start | bytes 4718600 | tf_op jit(solution)/shard_map/ppermute | solution.py:365
  100.4 2.5 %shard_map.56.kept = f32[8,192,256]{2,1,0:T(8,128)S(1)} custom-call(bf16[8,128,256]{2,1,0:T(8,128)(2,1)S(1)} %get-tuple-element.29.r_own, bf16[8,192,256]{2,1,0:T(8,128)(2,1)S(1)} %all-to-all-done.c_own, bf16[8,128,256]{2,1,0:T(8,128)(2,1)S(1)} %get-tuple-element.32.c_other, f32[32,128]{1,0:T(8,128)S(1)} %get-tuple-element.40.shifts, ...), custom_call_target="tpu_custom_call" | custom-call | flops 1073741824 | bytes 2097152 | tf_op jit(solution)/shard_map/pallas_call | solution.py:339
  103.6 15.6 %all_to_all.33.parts = bf16[8,208,256]{2,1,0:T(8,128)(2,1)S(1)} all-to-all(bf16[8,208,256]{2,1,0:T(8,128)(2,1)S(1)} %shard_map.57), channel_id=1, replica_groups=mesh['xh'=2,'z'=8,'core'=2,'xl'=2,'y'=4] {'xl','y'}, dimensions={0} | all-to-all | bytes 1703936 | tf_op jit(solution)/shard_map/all_to_all | solution.py:354
  (18 shorter events, 5.2 us)
Async XLA Ops:
  0.6 4.9 %collective-permute-start.6 = (bf16[64,256]{1,0:T(8,128)(2,1)}, bf16[64,256]{1,0:T(8,128)(2,1)S(1)}, u32[]{:S(2)}, u32[]{:S(2)}) collective-permute-start(bf16[64,256]{1,0:T(8,128)(2,1)} %param.3), channel_id=1, source_target_pairs={{0,132},{4,128},{128,4},{132,0},{1,133},{5,129},{129,5},{133,1},{2... | collective-permute-start | bytes 98312 | tf_op jit(solution)/shard_map/ppermute | solution.py:369
  6.5 30.2 %all-to-all-start = ((bf16[8,192,256]{2,1,0:T(8,128)(2,1)}), bf16[8,192,256]{2,1,0:T(8,128)(2,1)S(1)}, u32[]{:S(2)}, u32[]{:S(2)}) async-start(bf16[8,192,256]{2,1,0:T(8,128)(2,1)} %shard_map.49), calls=%async_computation | async-start | bytes 1572864 | tf_op jit(solution)/shard_map/all_to_all | solution.py:354
  14.9 4.1 %collective-permute-start.2 = (bf16[128,256]{1,0:T(8,128)(2,1)S(1)}, bf16[128,256]{1,0:T(8,128)(2,1)S(1)}, u32[]{:S(2)}, u32[]{:S(2)}) collective-permute-start(bf16[128,256]{1,0:T(8,128)(2,1)S(1)} %constant_dynamic-update-slice_fusion.own), channel_id=1, source_target_pairs={{0,3},{1,0},{2,1},{3,2},{4,7},{5,4},{6,5},{7,6},{8,11},{9,8},{10,9... | collective-permute-start | bytes 196616 | tf_op jit(solution)/shard_map/ppermute | solution.py:373
  17.6 4.7 %collective-permute-start.1 = (bf16[128,256]{1,0:T(8,128)(2,1)S(1)}, bf16[128,256]{1,0:T(8,128)(2,1)S(1)}, u32[]{:S(2)}, u32[]{:S(2)}) collective-permute-start(bf16[128,256]{1,0:T(8,128)(2,1)S(1)} %constant_dynamic-update-slice_fusion.own), channel_id=1, source_target_pairs={{0,2},{1,3},{2,0},{3,1},{4,6},{5,7},{6,4},{7,5},{8,10},{9,11},{10,... | collective-permute-start | bytes 196616 | tf_op jit(solution)/shard_map/ppermute | solution.py:373
  17.9 5.0 %collective-permute-start = (bf16[128,256]{1,0:T(8,128)(2,1)S(1)}, bf16[128,256]{1,0:T(8,128)(2,1)S(1)}, u32[]{:S(2)}, u32[]{:S(2)}) collective-permute-start(bf16[128,256]{1,0:T(8,128)(2,1)S(1)} %constant_dynamic-update-slice_fusion.own), channel_id=1, source_target_pairs={{0,1},{1,2},{2,3},{3,0},{4,5},{5,6},{6,7},{7,4},{8,9},{9,10},{10,1... | collective-permute-start | bytes 196616 | tf_op jit(solution)/shard_map/ppermute | solution.py:373
  22.9 5.6 %collective-permute-start.3 = (bf16[4,128,256]{2,1,0:T(8,128)(2,1)S(1)}, bf16[4,128,256]{2,1,0:T(8,128)(2,1)S(1)}, u32[]{:S(2)}, u32[]{:S(2)}) collective-permute-start(bf16[4,128,256]{2,1,0:T(8,128)(2,1)S(1)} %pad_maximum_fusion.near), channel_id=1, source_target_pairs={{0,4},{4,0},{1,5},{5,1},{2,6},{6,2},{3,7},{7,3},{8,12},{12,8},{9,1... | collective-permute-start | bytes 786440 | tf_op jit(solution)/shard_map/ppermute | solution.py:385
  23.1 16.2 %collective-permute-start.4 = (bf16[4,128,256]{2,1,0:T(8,128)(2,1)S(1)}, bf16[4,128,256]{2,1,0:T(8,128)(2,1)S(1)}, u32[]{:S(2)}, u32[]{:S(2)}) collective-permute-start(bf16[4,128,256]{2,1,0:T(8,128)(2,1)S(1)} %pad_maximum_fusion.near), channel_id=1, source_target_pairs={{0,8},{8,0},{1,9},{9,1},{2,10},{10,2},{3,11},{11,3},{4,12},{12,4},... | collective-permute-start | bytes 786440 | tf_op jit(solution)/shard_map/ppermute | solution.py:365
  28.6 10.7 %collective-permute-start.5 = (bf16[4,128,256]{2,1,0:T(8,128)(2,1)S(1)}, bf16[4,128,256]{2,1,0:T(8,128)(2,1)S(1)}, u32[]{:S(2)}, u32[]{:S(2)}) collective-permute-start(bf16[4,128,256]{2,1,0:T(8,128)(2,1)S(1)} %collective-permute-done.3.across), channel_id=1, source_target_pairs={{0,8},{8,0},{1,9},{9,1},{2,10},{10,2},{3,11},{11,3},{4,12},{12,4},... | collective-permute-start | bytes 786440 | tf_op jit(solution)/shard_map/ppermute | solution.py:365
  36.7 11.9 %collective-permute-start.7 = (bf16[8,64,256]{2,1,0:T(8,128)(2,1)S(1)}, bf16[8,64,256]{2,1,0:T(8,128)(2,1)S(1)}, u32[]{:S(2)}, u32[]{:S(2)}) collective-permute-start(bf16[8,64,256]{2,1,0:T(8,128)(2,1)S(1)} %slice.4), channel_id=1, source_target_pairs={{0,132},{4,128},{128,4},{132,0},{1,133},{5,129},{129,5},{133,1},{2... | collective-permute-start | bytes 786440 | tf_op jit(solution)/shard_map/ppermute | solution.py:369
  41.6 12.9 %all-to-all-start.1 = ((f32[16,8,128]{2,1,0:T(8,128)}), f32[16,8,128]{2,1,0:T(8,128)S(1)}, u32[]{:S(2)}, u32[]{:S(2)}) async-start(f32[16,8,128]{2,1,0:T(8,128)} %get-tuple-element.35), calls=%async_computation.1 | async-start | bytes 131072 | tf_op jit(solution)/shard_map/all_to_all | solution.py:354
  98.1 5.2 %collective-permute-start.8 = (f32[8,192,256]{2,1,0:T(8,128)S(1)}, f32[8,192,256]{2,1,0:T(8,128)S(1)}, u32[]{:S(2)}, u32[]{:S(2)}) collective-permute-start(f32[8,192,256]{2,1,0:T(8,128)S(1)} %get-tuple-element.43), channel_id=1, source_target_pairs={{0,8},{8,0},{1,9},{9,1},{2,10},{10,2},{3,11},{11,3},{4,12},{12,4},... | collective-permute-start | bytes 4718600 | tf_op jit(solution)/shard_map/ppermute | solution.py:365
  100.3 3.0 %collective-permute-start.9 = (f32[16,128]{1,0:T(8,128)S(1)}, f32[16,128]{1,0:T(8,128)S(1)}, u32[]{:S(2)}, u32[]{:S(2)}) collective-permute-start(f32[16,128]{1,0:T(8,128)S(1)} %get-tuple-element.44.sums), channel_id=1, source_target_pairs={{0,8},{8,0},{1,9},{9,1},{2,10},{10,2},{3,11},{11,3},{4,12},{12,4},... | collective-permute-start | bytes 24584 | tf_op jit(solution)/shard_map/ppermute | solution.py:365

commit v6 on v5

--- a/solution.py
+++ b/solution.py
@@ -312,7 +312,10 @@
 
 
 def join_gradients(kept, back, sums, sum_back, out):
-    out[:, 0 : 3 * OWN, :] = (kept[...] + back[...]).astype(out.dtype)
+    for spot in range(8):
+        side, y = spot // 4, spot % 4
+        total = kept[spot : spot + 1] + back[spot : spot + 1]
+        out[2 * y + side : 2 * y + side + 1, 0 : 3 * OWN, :] = total.astype(out.dtype)
     part = jnp.broadcast_to(sums[8:9, :] + sum_back[8:9, :], (16, 128))
     high = part.astype(jnp.bfloat16)
     left = part - high.astype(jnp.float32)
@@ -443,7 +446,7 @@
         finish,
         [((OWN, WIDTH), f32), ((OWN, WIDTH), f32), ((1, 1), f32)],
         0,
-        share(joined, ("xl", "y")),
+        share(joined, ("y", "xl")),
         scale,
         sums,
     )

time: 120 us -> 120 us (level)
  no operation moved by 1% of the time
where the time goes in v6:
time: 120 us
  blocking collectives  51.7 us (43%)
  starting transfers between devices  35.7 us (30%)
  Pallas kernels  17.4 us (14%)
  waiting for transfers between devices  12.8 us (11%)
  local copies, waits for them, and re-layouts  1.54 us (1%)
    all_to_all x4, blocking collectives, share(): lax.all_to_all(message, axes, 0, 0, tiled=True, axis_index_groups=groups)  51.7 us
    pallas_call x10, Pallas kernels, call(): pl.pallas_call(body, out_shape=shapes, in_specs=specs, out_specs=[pl.Bloc...  17.4 us
    all_to_all x2, starting transfers between devices, share(): lax.all_to_all(message, axes, 0, 0, tiled=True, axis_index_groups=groups)  15.4 us
    ppermute x4, starting transfers between devices, core_swap(): return lax.ppermute(values, 'core', [(0, 1), (1, 0)])  10.5 us
    all_to_all x2, waiting for transfers between devices, share(): lax.all_to_all(message, axes, 0, 0, tiled=True, axis_index_groups=groups)  6.44 us
    ppermute x2, starting transfers between devices, pair_swap(): return lax.ppermute(values, ('xh', 'xl'), [(0, 3), (1, 2), (2, 1), (3, 0)])  5.96 us
    ppermute x3, waiting for transfers between devices, y_step(): return lax.ppermute(values, 'y', [(y, (y + shift) % 4) for y in range(4)])  4.28 us
    ppermute x3, starting transfers between devices, y_step(): return lax.ppermute(values, 'y', [(y, (y + shift) % 4) for y in range(4)])  3.77 us
  transfers between devices with their start and end apart: 12, of which 7 were waited for; matrix products, arithmetic and copies ran while one was open for 1% of the time, Pallas kernels for 7%

profile of v6, /device:TPU:1, one launch (start us, length us, event | category | flops | bytes accessed | tf_op | source)
XLA Modules:
  0.0 119.9 jit_solution(14863726093679612352)
XLA Ops:
  0.6 3.4 %collective-permute-start.6 = (bf16[64,256]{1,0:T(8,128)(2,1)}, bf16[64,256]{1,0:T(8,128)(2,1)S(1)}, u32[]{:S(2)}, u32[]{:S(2)}) collective-permute-start(bf16[64,256]{1,0:T(8,128)(2,1)} %param.3), channel_id=1, source_target_pairs={{0,132},{4,128},{128,4},{132,0},{1,133},{5,129},{129,5},{133,1},{2... | collective-permute-start | bytes 98312 | tf_op jit(solution)/shard_map/ppermute | solution.py:372
  5.5 0.9 shard_map.49
  6.5 8.4 %all-to-all-start = ((bf16[8,192,256]{2,1,0:T(8,128)(2,1)}), bf16[8,192,256]{2,1,0:T(8,128)(2,1)S(1)}, u32[]{:S(2)}, u32[]{:S(2)}) async-start(bf16[8,192,256]{2,1,0:T(8,128)(2,1)} %shard_map.49), calls=%async_computation | async-start | bytes 1572864 | tf_op jit(solution)/shard_map/all_to_all | solution.py:357
  14.9 2.7 %collective-permute-start.2 = (bf16[128,256]{1,0:T(8,128)(2,1)S(1)}, bf16[128,256]{1,0:T(8,128)(2,1)S(1)}, u32[]{:S(2)}, u32[]{:S(2)}) collective-permute-start(bf16[128,256]{1,0:T(8,128)(2,1)S(1)} %constant_dynamic-update-slice_fusion.own), channel_id=1, source_target_pairs={{0,3},{1,0},{2,1},{3,2},{4,7},{5,4},{6,5},{7,6},{8,11},{9,8},{10,9... | collective-permute-start | bytes 196616 | tf_op jit(solution)/shard_map/ppermute | solution.py:376
  18.9 3.4 %collective-permute-done.1 = bf16[128,256]{1,0:T(8,128)(2,1)S(1)} collective-permute-done((bf16[128,256]{1,0:T(8,128)(2,1)S(1)}, bf16[128,256]{1,0:T(8,128)(2,1)S(1)}, u32[]{:S(2)}, u32[]{:S(2)}) %collective-permute-start.1) | collective-permute-done | bytes 65568 | tf_op jit(solution)/shard_map/ppermute | solution.py:376
  23.1 3.8 %collective-permute-start.4 = (bf16[4,128,256]{2,1,0:T(8,128)(2,1)S(1)}, bf16[4,128,256]{2,1,0:T(8,128)(2,1)S(1)}, u32[]{:S(2)}, u32[]{:S(2)}) collective-permute-start(bf16[4,128,256]{2,1,0:T(8,128)(2,1)S(1)} %pad_maximum_fusion.near), channel_id=1, source_target_pairs={{0,8},{8,0},{1,9},{9,1},{2,10},{10,2},{3,11},{11,3},{4,12},{12,4},... | collective-permute-start | bytes 786440 | tf_op jit(solution)/shard_map/ppermute | solution.py:368
  26.9 1.7 %collective-permute-done.3.across = bf16[4,128,256]{2,1,0:T(8,128)(2,1)S(1)} collective-permute-done((bf16[4,128,256]{2,1,0:T(8,128)(2,1)S(1)}, bf16[4,128,256]{2,1,0:T(8,128)(2,1)S(1)}, u32[]{:S(2)}, u32[]{:S(2)}) %collective-permute-start.3) | collective-permute-done | bytes 262176 | tf_op jit(solution)/shard_map/ppermute | solution.py:388
  28.6 4.4 %collective-permute-start.5 = (bf16[4,128,256]{2,1,0:T(8,128)(2,1)S(1)}, bf16[4,128,256]{2,1,0:T(8,128)(2,1)S(1)}, u32[]{:S(2)}, u32[]{:S(2)}) collective-permute-start(bf16[4,128,256]{2,1,0:T(8,128)(2,1)S(1)} %collective-permute-done.3.across), channel_id=1, source_target_pairs={{0,8},{8,0},{1,9},{9,1},{2,10},{10,2},{3,11},{11,3},{4,12},{12,4},... | collective-permute-start | bytes 786440 | tf_op jit(solution)/shard_map/ppermute | solution.py:368
  32.9 3.7 %all-to-all-done.c_own = bf16[8,192,256]{2,1,0:T(8,128)(2,1)S(1)} async-done(((bf16[8,192,256]{2,1,0:T(8,128)(2,1)}), bf16[8,192,256]{2,1,0:T(8,128)(2,1)S(1)}, u32[]{:S(2)}, u32[]{:S(2)}) %all-to-all-start) | async-done | bytes 786464 | tf_op jit(solution)/shard_map/all_to_all | solution.py:357
  36.7 2.6 %collective-permute-start.7 = (bf16[8,64,256]{2,1,0:T(8,128)(2,1)S(1)}, bf16[8,64,256]{2,1,0:T(8,128)(2,1)S(1)}, u32[]{:S(2)}, u32[]{:S(2)}) collective-permute-start(bf16[8,64,256]{2,1,0:T(8,128)(2,1)S(1)} %slice.4), channel_id=1, source_target_pairs={{0,132},{4,128},{128,4},{132,0},{1,133},{5,129},{129,5},{133,1},{2... | collective-permute-start | bytes 786440 | tf_op jit(solution)/shard_map/ppermute | solution.py:372
  39.3 2.3 %shard_map.50 = (f32[16,8,128]{2,1,0:T(8,128)}, bf16[8,128,256]{2,1,0:T(8,128)(2,1)S(1)}, bf16[8,128,256]{2,1,0:T(8,128)(2,1)S(1)}) custom-call(bf16[4,128,256]{2,1,0:T(8,128)(2,1)S(1)} %pad_maximum_fusion.near, bf16[4,128,256]{2,1,0:T(8,128)(2,1)S(1)} %collective-permute-done.3.across, bf16[4,128,256]{2,1,0:T(8,128)(2,1)S(1)} %collective-permute-done.4.near_far, ...), custom_call_target="tpu_custom_call" | custom-call | flops 536870912 | bytes 2097152 | tf_op jit(solution)/shard_map/pallas_call | solution.py:342
  41.6 7.0 %all-to-all-start.1 = ((f32[16,8,128]{2,1,0:T(8,128)}), f32[16,8,128]{2,1,0:T(8,128)S(1)}, u32[]{:S(2)}, u32[]{:S(2)}) async-start(f32[16,8,128]{2,1,0:T(8,128)} %get-tuple-element.35), calls=%async_computation.1 | async-start | bytes 131072 | tf_op jit(solution)/shard_map/all_to_all | solution.py:357
  48.6 3.2 %shard_map.51 = (f32[16,128]{1,0:T(8,128)S(1)}, f32[32,128]{1,0:T(8,128)S(1)}, bf16[8,128,256]{2,1,0:T(8,128)(2,1)S(1)}) custom-call(bf16[8,128,256]{2,1,0:T(8,128)(2,1)S(1)} %get-tuple-element.29.r_own, bf16[8,128,256]{2,1,0:T(8,128)(2,1)S(1)} %get-tuple-element.30.r_other, bf16[8,192,256]{2,1,0:T(8,128)(2,1)S(1)} %all-to-all-done.c_own, ...), custom_call_target="tpu_custom_call" | custom-call | flops 1073741824 | bytes 2097152 | tf_op jit(solution)/shard_map/pallas_call | solution.py:342
  51.8 2.7 %all-to-all-done.1.got = f32[16,8,128]{2,1,0:T(8,128)S(1)} async-done(((f32[16,8,128]{2,1,0:T(8,128)}), f32[16,8,128]{2,1,0:T(8,128)S(1)}, u32[]{:S(2)}, u32[]{:S(2)}) %all-to-all-start.1) | async-done | bytes 65568 | tf_op jit(solution)/shard_map/all_to_all | solution.py:357
  54.5 1.5 %shard_map.52 = (f32[16,24,128]{2,1,0:T(8,128)S(1)}, f32[8,128]{1,0:T(8,128)S(1)}) custom-call(bf16[8,128,256]{2,1,0:T(8,128)(2,1)S(1)} %get-tuple-element.29.r_own, bf16[8,128,256]{2,1,0:T(8,128)(2,1)S(1)} %get-tuple-element.30.r_other, bf16[8,192,256]{2,1,0:T(8,128)(2,1)S(1)} %all-to-all-done.c_own, bf16[8,128,256]{2,1,0:T(8,128)(2,1)S(1)} %get-tuple-element.32.c_other, ...), custom_call_target="tpu_custom_call" | custom-call | flops 536870912 | bytes 2097152 | tf_op jit(solution)/shard_map/pallas_call | solution.py:342
  55.9 11.5 %all_to_all.30.got = f32[16,24,128]{2,1,0:T(8,128)S(1)} all-to-all(f32[16,24,128]{2,1,0:T(8,128)S(1)} %get-tuple-element.37), channel_id=1, replica_groups={{0,16,32,48,64,80,96,112,132,148,164,180,196,212,228,244},{4,20,36,52,6..., dimensions={0} | all-to-all | bytes 393216 | tf_op jit(solution)/shard_map/all_to_all | solution.py:357
  67.4 2.4 %shard_map.53 = (f32[16,32,128]{2,1,0:T(8,128)S(1)}, f32[8,128]{1,0:T(8,128)S(1)}) custom-call(bf16[8,128,256]{2,1,0:T(8,128)(2,1)S(1)} %get-tuple-element.29.r_own, bf16[8,128,256]{2,1,0:T(8,128)(2,1)S(1)} %get-tuple-element.30.r_other, bf16[8,192,256]{2,1,0:T(8,128)(2,1)S(1)} %all-to-all-done.c_own, bf16[8,128,256]{2,1,0:T(8,128)(2,1)S(1)} %get-tuple-element.32.c_other, ...), custom_call_target="tpu_custom_call" | custom-call | flops 1610612736 | bytes 2097152 | tf_op jit(solution)/shard_map/pallas_call | solution.py:342
  69.9 12.1 %all_to_all.31.got = f32[16,32,128]{2,1,0:T(8,128)S(1)} all-to-all(f32[16,32,128]{2,1,0:T(8,128)S(1)} %get-tuple-element.39), channel_id=1, replica_groups=mesh['xh'=2,'z'=8,'core'=2,'xl'=2,'y'=4] {'core','xl','y'}, dimensions={0} | all-to-all | bytes 524288 | tf_op jit(solution)/shard_map/all_to_all | solution.py:357
  82.0 0.9 shard_map.54
  83.0 12.6 %all_to_all.32.got = f32[16,16,128]{2,1,0:T(8,128)S(1)} all-to-all(f32[16,16,128]{2,1,0:T(8,128)S(1)} %get-tuple-element.41), channel_id=1, replica_groups={{0,16,32,48,64,80,96,112,132,148,164,180,196,212,228,244},{4,20,36,52,6..., dimensions={0} | all-to-all | bytes 262144 | tf_op jit(solution)/shard_map/all_to_all | solution.py:357
  95.5 2.6 %shard_map.55 = (f32[8,192,256]{2,1,0:T(8,128)S(1)}, f32[32,128]{1,0:T(8,128)S(1)}, f32[64,256]{1,0:T(8,128)S(1)}, f32[16,128]{1,0:T(8,128)S(1)}) custom-call(bf16[8,128,256]{2,1,0:T(8,128)(2,1)S(1)} %get-tuple-element.30.r_other, bf16[8,192,256]{2,1,0:T(8,128)(2,1)S(1)} %all-to-all-done.c_own, bf16[8,128,256]{2,1,0:T(8,128)(2,1)S(1)} %get-tuple-element.32.c_other, ...), custom_call_target="tpu_custom_call" | custom-call | flops 1073741824 | bytes 2097152 | tf_op jit(solution)/shard_map/pallas_call | solution.py:342
  98.1 2.2 %collective-permute-start.8 = (f32[8,192,256]{2,1,0:T(8,128)S(1)}, f32[8,192,256]{2,1,0:T(8,128)S(1)}, u32[]{:S(2)}, u32[]{:S(2)}) collective-permute-start(f32[8,192,256]{2,1,0:T(8,128)S(1)} %get-tuple-element.43), channel_id=1, source_target_pairs={{0,8},{8,0},{1,9},{9,1},{2,10},{10,2},{3,11},{11,3},{4,12},{12,4},... | collective-permute-start | bytes 4718600 | tf_op jit(solution)/shard_map/ppermute | solution.py:368
  100.4 2.5 %shard_map.56.kept = f32[8,192,256]{2,1,0:T(8,128)S(1)} custom-call(bf16[8,128,256]{2,1,0:T(8,128)(2,1)S(1)} %get-tuple-element.29.r_own, bf16[8,192,256]{2,1,0:T(8,128)(2,1)S(1)} %all-to-all-done.c_own, bf16[8,128,256]{2,1,0:T(8,128)(2,1)S(1)} %get-tuple-element.32.c_other, f32[32,128]{1,0:T(8,128)S(1)} %get-tuple-element.40.shifts, ...), custom_call_target="tpu_custom_call" | custom-call | flops 1073741824 | bytes 2097152 | tf_op jit(solution)/shard_map/pallas_call | solution.py:342
  103.6 15.5 %all_to_all.33.parts = bf16[8,208,256]{2,1,0:T(8,128)(2,1)S(1)} all-to-all(bf16[8,208,256]{2,1,0:T(8,128)(2,1)S(1)} %shard_map.57), channel_id=1, replica_groups=mesh['xh'=2,'z'=8,'core'=2,'xl'=2,'y'=4] {'y','xl'}, dimensions={0} | all-to-all | bytes 1703936 | tf_op jit(solution)/shard_map/all_to_all | solution.py:357
  (18 shorter events, 5.2 us)
Async XLA Ops:
  0.6 4.9 %collective-permute-start.6 = (bf16[64,256]{1,0:T(8,128)(2,1)}, bf16[64,256]{1,0:T(8,128)(2,1)S(1)}, u32[]{:S(2)}, u32[]{:S(2)}) collective-permute-start(bf16[64,256]{1,0:T(8,128)(2,1)} %param.3), channel_id=1, source_target_pairs={{0,132},{4,128},{128,4},{132,0},{1,133},{5,129},{129,5},{133,1},{2... | collective-permute-start | bytes 98312 | tf_op jit(solution)/shard_map/ppermute | solution.py:372
  6.5 30.2 %all-to-all-start = ((bf16[8,192,256]{2,1,0:T(8,128)(2,1)}), bf16[8,192,256]{2,1,0:T(8,128)(2,1)S(1)}, u32[]{:S(2)}, u32[]{:S(2)}) async-start(bf16[8,192,256]{2,1,0:T(8,128)(2,1)} %shard_map.49), calls=%async_computation | async-start | bytes 1572864 | tf_op jit(solution)/shard_map/all_to_all | solution.py:357
  14.9 4.1 %collective-permute-start.2 = (bf16[128,256]{1,0:T(8,128)(2,1)S(1)}, bf16[128,256]{1,0:T(8,128)(2,1)S(1)}, u32[]{:S(2)}, u32[]{:S(2)}) collective-permute-start(bf16[128,256]{1,0:T(8,128)(2,1)S(1)} %constant_dynamic-update-slice_fusion.own), channel_id=1, source_target_pairs={{0,3},{1,0},{2,1},{3,2},{4,7},{5,4},{6,5},{7,6},{8,11},{9,8},{10,9... | collective-permute-start | bytes 196616 | tf_op jit(solution)/shard_map/ppermute | solution.py:376
  17.6 4.7 %collective-permute-start.1 = (bf16[128,256]{1,0:T(8,128)(2,1)S(1)}, bf16[128,256]{1,0:T(8,128)(2,1)S(1)}, u32[]{:S(2)}, u32[]{:S(2)}) collective-permute-start(bf16[128,256]{1,0:T(8,128)(2,1)S(1)} %constant_dynamic-update-slice_fusion.own), channel_id=1, source_target_pairs={{0,2},{1,3},{2,0},{3,1},{4,6},{5,7},{6,4},{7,5},{8,10},{9,11},{10,... | collective-permute-start | bytes 196616 | tf_op jit(solution)/shard_map/ppermute | solution.py:376
  17.9 5.0 %collective-permute-start = (bf16[128,256]{1,0:T(8,128)(2,1)S(1)}, bf16[128,256]{1,0:T(8,128)(2,1)S(1)}, u32[]{:S(2)}, u32[]{:S(2)}) collective-permute-start(bf16[128,256]{1,0:T(8,128)(2,1)S(1)} %constant_dynamic-update-slice_fusion.own), channel_id=1, source_target_pairs={{0,1},{1,2},{2,3},{3,0},{4,5},{5,6},{6,7},{7,4},{8,9},{9,10},{10,1... | collective-permute-start | bytes 196616 | tf_op jit(solution)/shard_map/ppermute | solution.py:376
  22.9 5.6 %collective-permute-start.3 = (bf16[4,128,256]{2,1,0:T(8,128)(2,1)S(1)}, bf16[4,128,256]{2,1,0:T(8,128)(2,1)S(1)}, u32[]{:S(2)}, u32[]{:S(2)}) collective-permute-start(bf16[4,128,256]{2,1,0:T(8,128)(2,1)S(1)} %pad_maximum_fusion.near), channel_id=1, source_target_pairs={{0,4},{4,0},{1,5},{5,1},{2,6},{6,2},{3,7},{7,3},{8,12},{12,8},{9,1... | collective-permute-start | bytes 786440 | tf_op jit(solution)/shard_map/ppermute | solution.py:388
  23.1 16.2 %collective-permute-start.4 = (bf16[4,128,256]{2,1,0:T(8,128)(2,1)S(1)}, bf16[4,128,256]{2,1,0:T(8,128)(2,1)S(1)}, u32[]{:S(2)}, u32[]{:S(2)}) collective-permute-start(bf16[4,128,256]{2,1,0:T(8,128)(2,1)S(1)} %pad_maximum_fusion.near), channel_id=1, source_target_pairs={{0,8},{8,0},{1,9},{9,1},{2,10},{10,2},{3,11},{11,3},{4,12},{12,4},... | collective-permute-start | bytes 786440 | tf_op jit(solution)/shard_map/ppermute | solution.py:368
  28.6 10.7 %collective-permute-start.5 = (bf16[4,128,256]{2,1,0:T(8,128)(2,1)S(1)}, bf16[4,128,256]{2,1,0:T(8,128)(2,1)S(1)}, u32[]{:S(2)}, u32[]{:S(2)}) collective-permute-start(bf16[4,128,256]{2,1,0:T(8,128)(2,1)S(1)} %collective-permute-done.3.across), channel_id=1, source_target_pairs={{0,8},{8,0},{1,9},{9,1},{2,10},{10,2},{3,11},{11,3},{4,12},{12,4},... | collective-permute-start | bytes 786440 | tf_op jit(solution)/shard_map/ppermute | solution.py:368
  36.7 11.9 %collective-permute-start.7 = (bf16[8,64,256]{2,1,0:T(8,128)(2,1)S(1)}, bf16[8,64,256]{2,1,0:T(8,128)(2,1)S(1)}, u32[]{:S(2)}, u32[]{:S(2)}) collective-permute-start(bf16[8,64,256]{2,1,0:T(8,128)(2,1)S(1)} %slice.4), channel_id=1, source_target_pairs={{0,132},{4,128},{128,4},{132,0},{1,133},{5,129},{129,5},{133,1},{2... | collective-permute-start | bytes 786440 | tf_op jit(solution)/shard_map/ppermute | solution.py:372
  41.6 12.9 %all-to-all-start.1 = ((f32[16,8,128]{2,1,0:T(8,128)}), f32[16,8,128]{2,1,0:T(8,128)S(1)}, u32[]{:S(2)}, u32[]{:S(2)}) async-start(f32[16,8,128]{2,1,0:T(8,128)} %get-tuple-element.35), calls=%async_computation.1 | async-start | bytes 131072 | tf_op jit(solution)/shard_map/all_to_all | solution.py:357
  98.1 5.2 %collective-permute-start.8 = (f32[8,192,256]{2,1,0:T(8,128)S(1)}, f32[8,192,256]{2,1,0:T(8,128)S(1)}, u32[]{:S(2)}, u32[]{:S(2)}) collective-permute-start(f32[8,192,256]{2,1,0:T(8,128)S(1)} %get-tuple-element.43), channel_id=1, source_target_pairs={{0,8},{8,0},{1,9},{9,1},{2,10},{10,2},{3,11},{11,3},{4,12},{12,4},... | collective-permute-start | bytes 4718600 | tf_op jit(solution)/shard_map/ppermute | solution.py:368
  100.3 3.0 %collective-permute-start.9 = (f32[16,128]{1,0:T(8,128)S(1)}, f32[16,128]{1,0:T(8,128)S(1)}, u32[]{:S(2)}, u32[]{:S(2)}) collective-permute-start(f32[16,128]{1,0:T(8,128)S(1)} %get-tuple-element.44.sums), channel_id=1, source_target_pairs={{0,8},{8,0},{1,9},{9,1},{2,10},{10,2},{3,11},{11,3},{4,12},{12,4},... | collective-permute-start | bytes 24584 | tf_op jit(solution)/shard_map/ppermute | solution.py:368
